TPU v7x, 32 devices: a whole 2x2x4 slice. The times are simulated.
32 devices in a mesh: segment: 4 (over y, x), dev: 8 (over z, core).
Axes of the slice: x: 2, y: 2, z: 4, core: 2. Of those that a mesh axis runs over, the one named last changes fastest.
Arguments:
- hidden: bfloat16 [4, 64, 8192], P('segment', 'dev'), may hold values from -6 to 6
- gain: float32 [4, 8192], P('segment'), may hold values from 0.5 to 1.5
- w_query: bfloat16 [4, 8192, 4096], P('segment', None, 'dev'), may hold values from -0.0625 to 0.0625
- w_key: bfloat16 [4, 8192, 512], P('segment', None, 'dev'), may hold values from -0.25 to 0.25
- w_value: bfloat16 [4, 8192, 512], P('segment', None, 'dev'), may hold values from -0.0625 to 0.0625
- w_out: bfloat16 [4, 4096, 8192], P('segment', None, 'dev'), may hold values from -0.09375 to 0.09375
- cache: bfloat16 [4, 32, 128, 1024], P('segment', 'dev'), may hold values from -128 to 128
- block_slot: int32 [32], replicated, may hold values from 0 to 31, as said below
- retrieved: int32 [4, 8, 6], P('segment', 'dev'), may hold values from 0 to 31, as said below
- counts: int32 [4, 8], P('segment', 'dev'), may hold values from 1 to 6, 36 in all within a row
Outputs:
- next_hidden: bfloat16 [4, 64, 8192], P('segment', 'dev')
Inputs may be any that keep to these rules, and one draw needn't show every extreme that they name: A permutation: block b lies in row block_slot[b] % 4 of the cache rows held by device block_slot[b] // 4 of dev. `retrieved`: passage block ids; the 6 entries of one request lie on 6 different devices of dev.
All inputs are finite; a program needn't handle non-finite values. No bound on the sum of `counts` on one device may be relied on, other than what follows from the above.
Results may differ from a plain program's by a relative error of at most 0.007.
The roundings to bfloat16 on the way count: a program that leaves them out, or rounds other values in their place, can miss the bound.
Values may be sent and summed in bfloat16 or wider, within the bound.
No kernel may reach another device: no remote copies, remote signals or barrier semaphores. Data moves between devices by JAX's collectives and lax.ppermute only.
A program may use at most 128 MiB of HBM per device.

v0:
```python
import jax
import jax.numpy as jnp
from jax import lax
from jax.sharding import PartitionSpec as P

HEADS = 32
KV_HEADS = 4
HEAD_DIM = 128


far_below = -1e30
norm_eps = 1e-05


def passed_along(shard, axis, by):
    size = lax.axis_size(axis)
    return lax.ppermute(shard, axis, [(i, (i + by) % size) for i in range(size)])


def lookup_slots(block_ids, block_slot):
    table_width = block_slot.shape[0]
    matches = block_ids[..., None] == jnp.arange(table_width, dtype=jnp.int32)
    return jnp.sum(jnp.where(matches, block_slot, 0), axis=-1)


def block_stats(scores, valid):
    block_top = jnp.max(scores, axis=-1)
    weights = jnp.exp(scores - block_top[..., None])
    block_total = jnp.sum(weights, axis=-1)
    live_mask = valid[:, None, None, None]
    block_top = jnp.where(live_mask, block_top, far_below)
    block_total = jnp.where(live_mask, block_total, 0.0)
    return (block_top, block_total, weights.astype(jnp.bfloat16))


def self_stats(queries, key_rows, value_rows, score_scale):
    scores = (
        jnp.einsum("qhgd,khd->qhgk", queries, key_rows, preferred_element_type=jnp.float32)
        * score_scale
    )
    row_count = queries.shape[0]
    causal = (jnp.arange(row_count)[None, :] <= jnp.arange(row_count)[:, None])[:, None, None, :]
    own_top = jnp.max(jnp.where(causal, scores, far_below), axis=-1)
    weights = jnp.where(causal, jnp.exp(scores - own_top[..., None]), 0.0)
    own_total = jnp.sum(weights, axis=-1)
    own_acc = jnp.einsum(
        "qhgk,khd->qhgd",
        weights.astype(jnp.bfloat16),
        value_rows,
        preferred_element_type=jnp.float32,
    )
    return (own_top, own_total, own_acc)


def combine_terms(block_top, block_total, block_acc, own_top, own_total, own_acc):
    row_peak = jnp.maximum(own_top, jnp.max(block_top, axis=0))
    block_scale = jnp.exp(block_top - row_peak)
    own_scale = jnp.exp(own_top - row_peak)
    numerator = own_acc * own_scale[..., None] + jnp.sum(block_acc * block_scale[..., None], axis=0)
    denominator = own_total * own_scale + jnp.sum(block_total * block_scale, axis=0)
    return (numerator / denominator[..., None]).astype(jnp.bfloat16)


def body(hidden, gain, w_query, w_key, w_value, w_out, cache, block_slot, retrieved, counts):
    devices = lax.axis_size("dev")
    owner_index = lax.axis_index("dev")
    group_size = HEADS // KV_HEADS
    score_scale = HEAD_DIM ** (-0.5)
    pair_width = KV_HEADS * HEAD_DIM
    query_width = HEADS * HEAD_DIM
    state = hidden[0].astype(jnp.float32)
    inverse = lax.rsqrt(jnp.mean(state * state, axis=-1, keepdims=True) + norm_eps)
    normed = (state * inverse * gain[0]).astype(jnp.bfloat16)
    stacked = jnp.concatenate([w_query[0], w_key[0], w_value[0]], axis=1)
    query_cols = w_query.shape[2]
    key_cols = w_key.shape[2]
    projected = jnp.dot(
        lax.all_gather(normed, "dev", axis=0, tiled=True),
        stacked,
        preferred_element_type=jnp.float32,
    ).astype(jnp.bfloat16)
    query_part = projected[:, :query_cols]
    key_part = projected[:, query_cols : query_cols + key_cols]
    value_part = projected[:, query_cols + key_cols :]
    query_flat, key_flat, value_flat = (
        lax.all_to_all(query_part, "dev", split_axis=0, concat_axis=1, tiled=True),
        lax.all_to_all(key_part, "dev", split_axis=0, concat_axis=1, tiled=True),
        lax.all_to_all(value_part, "dev", split_axis=0, concat_axis=1, tiled=True),
    )
    question = query_flat.shape[0]
    queries = query_flat.reshape(question, KV_HEADS, group_size, HEAD_DIM)
    own_keys = key_flat.reshape(question, KV_HEADS, HEAD_DIM)
    own_values = value_flat.reshape(question, KV_HEADS, HEAD_DIM)
    all_ids, all_counts = (
        lax.all_gather(retrieved[0], "dev", axis=0, tiled=True),
        lax.all_gather(counts[0], "dev", axis=0, tiled=True),
    )
    table_rows = cache.shape[1]
    slot_ids = lookup_slots(all_ids, block_slot)
    listed = jnp.arange(all_ids.shape[1], dtype=jnp.int32)[None, :] < all_counts[:, None]
    mine = listed & (slot_ids // table_rows == owner_index)
    local_row = slot_ids % table_rows
    picked = jnp.sum(
        (
            mine[:, :, None] & (local_row[:, :, None] == jnp.arange(table_rows, dtype=jnp.int32))
        ).astype(jnp.bfloat16),
        axis=1,
    )
    selected = jnp.einsum(
        "rb,btc->rtc", picked, cache[0], preferred_element_type=jnp.float32
    ).astype(jnp.bfloat16)
    own_top, own_total, own_acc = self_stats(queries, own_keys, own_values, score_scale)
    my_slots = lookup_slots(retrieved[0][0], block_slot)
    my_listed = jnp.arange(retrieved.shape[2], dtype=jnp.int32) < counts[0][0]
    owner_ids = jnp.arange(devices, dtype=jnp.int32)
    holders = jnp.any(
        my_listed[None, :] & (my_slots[None, :] // table_rows == owner_ids[:, None]), axis=1
    )
    arrived = lax.all_to_all(selected, "dev", split_axis=0, concat_axis=0, tiled=True)
    arrived_keys = arrived[:, :, :pair_width].reshape(devices, -1, KV_HEADS, HEAD_DIM)
    arrived_values = arrived[:, :, pair_width:].reshape(devices, -1, KV_HEADS, HEAD_DIM)
    scores = (
        jnp.einsum("qhgd,tbhd->tqhgb", queries, arrived_keys, preferred_element_type=jnp.float32)
        * score_scale
    )
    block_top, block_total, weights = block_stats(scores, holders)
    block_acc = jnp.einsum(
        "tqhgb,tbhd->tqhgd", weights, arrived_values, preferred_element_type=jnp.float32
    )
    block_acc = jnp.where(holders[:, None, None, None, None], block_acc, 0.0)
    context = combine_terms(block_top, block_total, block_acc, own_top, own_total, own_acc).reshape(
        question, query_width
    )
    branch_cols = jnp.dot(
        lax.all_gather(context, "dev", axis=0, tiled=True),
        w_out[0],
        preferred_element_type=jnp.float32,
    )
    branch = lax.all_to_all(branch_cols, "dev", split_axis=0, concat_axis=1, tiled=True)
    updated = (state + branch).astype(jnp.bfloat16)
    return passed_along(updated[None], "segment", 1)


def solution(mesh):
    return jax.shard_map(
        body,
        mesh=mesh,
        in_specs=(
            P("segment", "dev", None),
            P("segment", None),
            P("segment", None, "dev"),
            P("segment", None, "dev"),
            P("segment", None, "dev"),
            P("segment", None, "dev"),
            P("segment", "dev", None, None),
            P(),
            P("segment", "dev", None),
            P("segment", "dev"),
        ),
        out_specs=P("segment", "dev", None),
        check_vma=False,
    )
```

profile of v0, /device:TPU:0, one launch (start us, length us, event | category | flops | bytes accessed | tf_op | source)
XLA Modules:
  0.0 177.9 jit_solution(5471632724269096338)
XLA Ops:
  6.5 1.2 fusion.28
  7.7 1.7 fusion.30
  10.1 1.3 dynamic-slice
  11.4 0.7 bitcast_dynamic-update-slice_fusion
  12.1 10.7 %all-reduce = s32[8]{0:T(128)S(1)} all-reduce(s32[8]{0:T(128)S(1)} %bitcast_dynamic-update-slice_fusion), channel_id=2, replica_groups=mesh['segment'=4,'dev'=8] {'dev'}, use_global_device_ids=true, to_apply=%add | all-reduce | flops 8 | bytes 64
  22.9 9.2 %all-gather.1 = s32[8,1,6]{2,1,0:T(1,128)S(1)} all-gather(s32[1,1,6]{2,1,0:T(1,128)} %param.18), channel_id=3, replica_groups=mesh['segment'=4,'dev'=8] {'dev'}, dimensions={0}, use_global_device_ids=true | all-gather | bytes 216 | tf_op jit(solution)/shard_map/all_gather | solution.py:95
  32.2 2.0 %copy.72 = bf16[8192,64]{1,0:T(8,128)(2,1)S(1)} copy(bf16[8192,64]{0,1:T(8,128)(2,1)} %bitcast.91) | data formatting | bytes 2097152 | tf_op jit(solution)/shard_map/squeeze | solution.py:74
  34.2 2.8 %copy.71 = bf16[8192,64]{1,0:T(8,128)(2,1)} copy(bf16[8192,64]{0,1:T(8,128)(2,1)} %bitcast.92) | data formatting | bytes 2097152 | tf_op jit(solution)/shard_map/squeeze | solution.py:74
  37.0 0.9 select_reduce_fusion.2
  38.0 6.7 %fusion.16 = bf16[64,640]{1,0:T(8,128)(2,1)S(1)} fusion(bf16[64,8192]{1,0:T(8,128)(2,1)} %all-gather.4.cloned.1.call-done, bf16[8192,64]{1,0:T(8,128)(2,1)S(1)} %copy.72, bf16[8192,64]{1,0:T(8,128)(2,1)} %copy.71, bf16[8192,512]{1,0:T(8,128)(2,1)} %bitcast.105), kind=kOutput, calls=%fused_computation.21 | convolution fusion | flops 702586880 | bytes 11616256 | tf_op jit(solution)/shard_map/dot_general | solution.py:77
  44.7 0.7 reshape.203
  45.4 3.3 %all-to-all-start.1 = ((bf16[8,2,256]{2,1,0:T(2,128)(2,1)}), bf16[8,2,256]{2,1,0:T(2,128)(2,1)S(1)}, u32[]{:S(2)}, u32[]{:S(2)}) async-start(bf16[8,2,256]{2,1,0:T(2,128)(2,1)} %reshape.203), calls=%async_computation.1 | async-start | bytes 16384 | tf_op jit(solution)/shard_map/all_to_all | solution.py:87
  48.8 0.7 reshape.205
  49.5 4.8 %all-to-all-done.1 = bf16[8,2,256]{2,1,0:T(2,128)(2,1)S(1)} async-done(((bf16[8,2,256]{2,1,0:T(2,128)(2,1)}), bf16[8,2,256]{2,1,0:T(2,128)(2,1)S(1)}, u32[]{:S(2)}, u32[]{:S(2)}) %all-to-all-start.1) | async-done | bytes 8224 | tf_op jit(solution)/shard_map/all_to_all | solution.py:87
  54.3 3.3 %all-to-all-start = ((bf16[8,2,256]{2,1,0:T(2,128)(2,1)}), bf16[8,2,256]{2,1,0:T(2,128)(2,1)S(1)}, u32[]{:S(2)}, u32[]{:S(2)}) async-start(bf16[8,2,256]{2,1,0:T(2,128)(2,1)} %reshape.205), calls=%async_computation | async-start | bytes 16384 | tf_op jit(solution)/shard_map/all_to_all | solution.py:88
  58.3 4.9 %all-to-all-done = bf16[8,2,256]{2,1,0:T(2,128)(2,1)S(1)} async-done(((bf16[8,2,256]{2,1,0:T(2,128)(2,1)}), bf16[8,2,256]{2,1,0:T(2,128)(2,1)S(1)}, u32[]{:S(2)}, u32[]{:S(2)}) %all-to-all-start) | async-done | bytes 8224 | tf_op jit(solution)/shard_map/all_to_all | solution.py:88
  63.2 3.4 %all-to-all-start.2 = ((bf16[8,8,512]{2,1,0:T(8,128)(2,1)}), bf16[8,8,512]{2,1,0:T(8,128)(2,1)S(1)}, u32[]{:S(2)}, u32[]{:S(2)}) async-start(bf16[8,8,512]{2,1,0:T(8,128)(2,1)} %slice_bitcast_fusion), calls=%async_computation.2 | async-start | bytes 131072 | tf_op jit(solution)/shard_map/all_to_all | solution.py:86
  66.6 1.1 convolution_convert_fusion
  67.6 2.5 %copy.82 = bf16[8,128,1024]{2,1,0:T(8,128)(2,1)} copy(bf16[8,128,1024]{2,0,1:T(8,128)(2,1)S(1)} %convolution_convert_fusion) | data formatting | bytes 4194304 | tf_op jit(solution)/shard_map/convert_element_type | solution.py:111
  70.1 2.3 %all-to-all-done.2 = bf16[8,8,512]{2,1,0:T(8,128)(2,1)S(1)} async-done(((bf16[8,8,512]{2,1,0:T(8,128)(2,1)}), bf16[8,8,512]{2,1,0:T(8,128)(2,1)S(1)}, u32[]{:S(2)}, u32[]{:S(2)}) %all-to-all-start.2) | async-done | bytes 65568 | tf_op jit(solution)/shard_map/all_to_all | solution.py:86
  72.4 3.6 %all-to-all-start.3 = ((bf16[8,128,1024]{2,1,0:T(8,128)(2,1)}), bf16[8,128,1024]{2,1,0:T(8,128)(2,1)S(1)}, u32[]{:S(2)}, u32[]{:S(2)}) async-start(bf16[8,128,1024]{2,1,0:T(8,128)(2,1)} %copy.82), calls=%async_computation.3 | async-start | bytes 4194304 | tf_op jit(solution)/shard_map/all_to_all | solution.py:119
  77.4 47.6 %all-to-all-done.3 = bf16[8,128,1024]{2,1,0:T(8,128)(2,1)S(1)} async-done(((bf16[8,128,1024]{2,1,0:T(8,128)(2,1)}), bf16[8,128,1024]{2,1,0:T(8,128)(2,1)S(1)}, u32[]{:S(2)}, u32[]{:S(2)}) %all-to-all-start.3) | async-done | bytes 2097184 | tf_op jit(solution)/shard_map/all_to_all | solution.py:119
  125.0 1.6 fusion.54
  126.6 1.6 copy.108
  128.2 1.6 copy.107
  131.2 0.8 fusion.11
  132.4 14.9 %all_gather.15 = bf16[64,4096]{1,0:T(8,128)(2,1)S(1)} all-gather(bf16[8,4096]{1,0:T(8,128)(2,1)S(1)} %bitcast.95), channel_id=1, replica_groups=mesh['segment'=4,'dev'=8] {'dev'}, dimensions={0}, use_global_device_ids=true | all-gather | bytes 589824 | tf_op jit(solution)/shard_map/all_gather | solution.py:135
  147.4 4.9 %fusion.6 = f32[8,8,1024]{2,1,0:T(8,128)S(1)} fusion(bf16[1,4096,1024]{2,1,0:T(8,128)(2,1)} %param.15, bf16[64,4096]{1,0:T(8,128)(2,1)S(1)} %all_gather.15), kind=kOutput, calls=%fused_computation.6 | convolution fusion | flops 536870912 | bytes 9175040 | tf_op jit(solution)/shard_map/dot_general | solution.py:134
  152.3 12.1 %all_to_all.69 = f32[8,8,1024]{2,1,0:T(8,128)S(1)} all-to-all(f32[8,8,1024]{2,1,0:T(8,128)S(1)} %fusion.6), channel_id=1, replica_groups=mesh['segment'=4,'dev'=8] {'dev'}, dimensions={0} | all-to-all | bytes 524288 | tf_op jit(solution)/shard_map/all_to_all | solution.py:139
  164.5 1.6 collective-permute-start
  166.1 4.4 %collective-permute-done = bf16[1,8,8192]{2,1,0:T(8,128)(2,1)S(1)} collective-permute-done((bf16[1,8,8192]{2,1,0:T(8,128)(2,1)S(1)}, bf16[1,8,8192]{2,1,0:T(8,128)(2,1)S(1)}, u32[]{:S(2)}, u32[]{:S(2)}) %collective-permute-start) | collective-permute-done | bytes 131104 | tf_op jit(solution)/shard_map/ppermute | solution.py:17
  170.4 0.7 copy.141
  (44 shorter events, 3.9 us)
Async XLA Ops:
  6.5 60.0 %copy-start = (bf16[1,4,128,1024]{3,2,1,0:T(8,128)(2,1)S(1)}, bf16[1,4,128,1024]{3,2,1,0:T(8,128)(2,1)}, u32[]{:S(2)}) copy-start(bf16[1,4,128,1024]{3,2,1,0:T(8,128)(2,1)} %param.16) | copy-start | bytes 3145732
  6.5 31.4 %all-gather.4.cloned.1.call-start = ((), (), s32[]{:S(2)}) async-start(), calls=%async_computation.5 | async-start | bytes 1179648 | tf_op jit(solution)/shard_map/all_gather | solution.py:78
  44.6 31.4 %copy-start.2 = (s32[32]{0:T(128)S(1)}, s32[32]{0:T(128)}, u32[]{:S(2)}) copy-start(s32[32]{0:T(128)} %param.17) | copy-start | bytes 388
  44.7 31.4 %copy-start.3 = (s32[1,1,6]{2,1,0:T(1,128)S(1)}, s32[1,1,6]{2,1,0:T(1,128)}, u32[]{:S(2)}) copy-start(s32[1,1,6]{2,1,0:T(1,128)} %param.18) | copy-start | bytes 76
  45.4 8.9 %all-to-all-start.1 = ((bf16[8,2,256]{2,1,0:T(2,128)(2,1)}), bf16[8,2,256]{2,1,0:T(2,128)(2,1)S(1)}, u32[]{:S(2)}, u32[]{:S(2)}) async-start(bf16[8,2,256]{2,1,0:T(2,128)(2,1)} %reshape.203), calls=%async_computation.1 | async-start | bytes 16384 | tf_op jit(solution)/shard_map/all_to_all | solution.py:87
  54.3 8.9 %all-to-all-start = ((bf16[8,2,256]{2,1,0:T(2,128)(2,1)}), bf16[8,2,256]{2,1,0:T(2,128)(2,1)S(1)}, u32[]{:S(2)}, u32[]{:S(2)}) async-start(bf16[8,2,256]{2,1,0:T(2,128)(2,1)} %reshape.205), calls=%async_computation | async-start | bytes 16384 | tf_op jit(solution)/shard_map/all_to_all | solution.py:88
  63.2 9.2 %all-to-all-start.2 = ((bf16[8,8,512]{2,1,0:T(8,128)(2,1)}), bf16[8,8,512]{2,1,0:T(8,128)(2,1)S(1)}, u32[]{:S(2)}, u32[]{:S(2)}) async-start(bf16[8,8,512]{2,1,0:T(8,128)(2,1)} %slice_bitcast_fusion), calls=%async_computation.2 | async-start | bytes 131072 | tf_op jit(solution)/shard_map/all_to_all | solution.py:86
  72.4 52.6 %all-to-all-start.3 = ((bf16[8,128,1024]{2,1,0:T(8,128)(2,1)}), bf16[8,128,1024]{2,1,0:T(8,128)(2,1)S(1)}, u32[]{:S(2)}, u32[]{:S(2)}) async-start(bf16[8,128,1024]{2,1,0:T(8,128)(2,1)} %copy.82), calls=%async_computation.3 | async-start | bytes 4194304 | tf_op jit(solution)/shard_map/all_to_all | solution.py:119
  131.2 33.2 %copy-start.1 = (bf16[1,8,8192]{2,1,0:T(8,128)(2,1)S(1)}, bf16[1,8,8192]{2,1,0:T(8,128)(2,1)}, u32[]{:S(2)}) copy-start(bf16[1,8,8192]{2,1,0:T(8,128)(2,1)} %param.10) | copy-start | bytes 393220
  164.5 5.9 %collective-permute-start = (bf16[1,8,8192]{2,1,0:T(8,128)(2,1)S(1)}, bf16[1,8,8192]{2,1,0:T(8,128)(2,1)S(1)}, u32[]{:S(2)}, u32[]{:S(2)}) collective-permute-start(bf16[1,8,8192]{2,1,0:T(8,128)(2,1)S(1)} %fusion.31), channel_id=1, source_target_pairs={{0,8},{8,16},{16,24},{24,0},{1,9},{9,17},{17,25},{25,1},{2,10},{10... | collective-permute-start | bytes 393224 | tf_op jit(solution)/shard_map/ppermute | solution.py:17
Sparse Core Ops, SparseCore 0:
  9.5 24.7 all-gather.3
where the time goes:
time: 179 us; the launch traced here: 178 us
  waiting for transfers between devices  64 us (36%)
  blocking collectives  47.1 us (26%)
  local copies, waits for them, and re-layouts  17.5 us (10%)
  starting transfers between devices  15.2 us (8%)
  matrix products  14.7 us (8%)
  between operations  14.3 us (8%)
  other arithmetic  5.13 us (3%)
    all_to_all x1, waiting for transfers between devices, body(): lax.all_to_all(selected, 'dev', split_axis=0, concat_axis=0, tiled=True)  47.6 us
    all_gather x1, blocking collectives, body(): lax.all_gather(context, 'dev', axis=0, tiled=True)  14.9 us
    all_to_all x1, blocking collectives, body(): lax.all_to_all(branch_cols, 'dev', split_axis=0, concat_axis=1, tiled=True)  12.1 us
    unnamed x1, blocking collectives  10.7 us
    all_gather x1, blocking collectives, body(): lax.all_gather(retrieved[0], 'dev', axis=0, tiled=True)  9.25 us
    unnamed x19, local copies, waits for them, and re-layouts  7.52 us
    dot_general x1, matrix products, body(): jnp.dot(lax.all_gather(normed, 'dev', axis=0, tiled=True), stacked, prefe...  6.66 us
    dot_general x1, matrix products, body(): jnp.dot(lax.all_gather(context, 'dev', axis=0, tiled=True), w_out[0], pre...  4.95 us
  transfers between devices with their start and end apart: 6, of which 5 were waited for; matrix products, arithmetic and copies ran while one was open for 8% of the time, Pallas kernels for 0%

commit v1 on v0

--- a/solution.py
+++ b/solution.py
@@ -1,6 +1,10 @@
+import functools
+
 import jax
 import jax.numpy as jnp
 from jax import lax
+from jax.experimental import pallas as pl
+from jax.experimental.pallas import tpu as pltpu
 from jax.sharding import PartitionSpec as P
 
 HEADS = 32
@@ -61,7 +65,7 @@
     return (numerator / denominator[..., None]).astype(jnp.bfloat16)
 
 
-def body(hidden, gain, w_query, w_key, w_value, w_out, cache, block_slot, retrieved, counts):
+def general_body(hidden, gain, w_query, w_key, w_value, w_out, cache, block_slot, retrieved, counts):
     devices = lax.axis_size("dev")
     owner_index = lax.axis_index("dev")
     group_size = HEADS // KV_HEADS
@@ -141,9 +145,345 @@
     return passed_along(updated[None], "segment", 1)
 
 
+CORES = 2
+VMEM = pl.BlockSpec(memory_space=pltpu.VMEM)
+SMEM = pl.BlockSpec(memory_space=pltpu.SMEM)
+ANYWHERE = pl.BlockSpec(memory_space=pl.ANY)
+MIB = 1 << 20
+
+
+def to_pair(x, k):
+    size = lax.axis_size("dev")
+    return lax.ppermute(x, "dev", [(d, (d + CORES * k) % size) for d in range(size)])
+
+
+def to_partner(x):
+    return lax.ppermute(x, "dev", [(d, d ^ 1) for d in range(lax.axis_size("dev"))])
+
+
+def after(x, *others):
+    return lax.optimization_barrier((x, *others))[0]
+
+
+def matmul(a, b, dims=((1,), (0,))):
+    return lax.dot_general(a, b, (dims, ((), ())), preferred_element_type=jnp.float32)
+
+
+def pack_kernel(place, cache, *rest):
+    outs, sems = rest[:-1], rest[-1]
+    pairs = len(outs)
+    width = cache.shape[3] // 2
+    copies = []
+    for k in list(range(1, pairs)) + [0]:
+        head = lax.rem(place[0] + k, pairs)
+        for part in range(2):
+            columns = pl.ds(pl.multiple_of(part * width + head * HEAD_DIM, HEAD_DIM), HEAD_DIM)
+            copy = pltpu.make_async_copy(
+                cache.at[0, :, :, columns], outs[k].at[:, part], sems.at[k, part]
+            )
+            copy.start()
+            copies.append(copy)
+    for copy in copies:
+        copy.wait()
+
+
+def pack(place, cache):
+    pairs = KV_HEADS
+    rows, tokens = cache.shape[1], cache.shape[2]
+    shape = jax.ShapeDtypeStruct((rows, 2, tokens, HEAD_DIM), cache.dtype)
+    return pl.pallas_call(
+        pack_kernel,
+        out_shape=[shape] * pairs,
+        in_specs=[SMEM, ANYWHERE],
+        out_specs=[ANYWHERE] * pairs,
+        scratch_shapes=[pltpu.SemaphoreType.DMA((pairs, 2))],
+        cost_estimate=pl.CostEstimate(flops=0, bytes_accessed=2 * cache.size * 2, transcendentals=0),
+        name="pack",
+    )(place, cache)
+
+
+def project_kernel(place, *refs):
+    count = 2 * KV_HEADS
+    parts, rest = refs[:count], refs[count:]
+    gain, wq, wk, wv, q_out, kv_out, cols_out, normed, wq_vm, wk_vm, wv_vm, sems = rest
+    chunks = sems.shape[0] - 2
+    depth = wq.shape[1] // chunks
+    pair, core = place[0], place[1]
+    copies = [
+        pltpu.make_async_copy(wk, wk_vm, sems.at[chunks]),
+        pltpu.make_async_copy(wv, wv_vm, sems.at[chunks + 1]),
+    ]
+    for i in range(chunks):
+        rows = pl.ds(i * depth, depth)
+        copies.append(pltpu.make_async_copy(wq.at[0, rows], wq_vm.at[rows], sems.at[i]))
+    for copy in copies:
+        copy.start()
+    first = core == 0
+    columns = pl.ds(pl.multiple_of((CORES * pair + core) * cols_out.shape[1], 128), cols_out.shape[1])
+    for k in range(KV_HEADS):
+        source = lax.rem(pair + KV_HEADS - k, KV_HEADS)
+        rows = pl.ds(pl.multiple_of(source * 16, 16), 16)
+        mine, other = parts[2 * k], parts[2 * k + 1]
+
+        def both(at):
+            a, b = mine[:, at].astype(jnp.float32), other[:, at].astype(jnp.float32)
+            return jnp.concatenate([jnp.where(first, a, b), jnp.where(first, b, a)], axis=0)
+
+        state = both(slice(None))
+        inverse = lax.rsqrt(jnp.mean(state * state, axis=-1, keepdims=True) + norm_eps)
+        normed[rows, :] = (state * inverse * gain[...]).astype(jnp.bfloat16)
+        cols_out[rows, :] = both(columns).astype(cols_out.dtype)
+    copies[0].wait()
+    key = matmul(normed[...], wk_vm[...], ((1,), (1,)))
+    copies[1].wait()
+    value = matmul(normed[...], wv_vm[...], ((1,), (1,)))
+    kv_out[...] = jnp.concatenate([key, value], axis=1).astype(kv_out.dtype)
+    total = jnp.zeros(q_out.shape, jnp.float32)
+    for i in range(chunks):
+        at = slice(i * depth, (i + 1) * depth)
+        copies[2 + i].wait()
+        total = total + matmul(normed[:, at], wq_vm[at, :])
+    q_out[...] = total.astype(q_out.dtype)
+
+
+def project(place, parts, gain, wq, wk, wv):
+    tokens = sum(p.shape[0] for p in parts)
+    width = parts[0].shape[1]
+    chunks = 8
+    bf16 = jnp.bfloat16
+    return pl.pallas_call(
+        project_kernel,
+        out_shape=[
+            jax.ShapeDtypeStruct((tokens, wq.shape[2]), bf16),
+            jax.ShapeDtypeStruct((tokens, 2 * wk.shape[0]), bf16),
+            jax.ShapeDtypeStruct((tokens, width // len(parts)), bf16),
+        ],
+        in_specs=[SMEM] + [VMEM] * (len(parts) + 1) + [ANYWHERE] * 3,
+        out_specs=[VMEM] * 3,
+        scratch_shapes=[
+            pltpu.VMEM((tokens, width), bf16),
+            pltpu.VMEM(wq.shape[1:], bf16),
+            pltpu.VMEM(wk.shape, bf16),
+            pltpu.VMEM(wv.shape, bf16),
+            pltpu.SemaphoreType.DMA((chunks + 2,)),
+        ],
+        compiler_params=pltpu.CompilerParams(vmem_limit_bytes=28 * MIB),
+        cost_estimate=pl.CostEstimate(
+            flops=2 * tokens * width * 640, bytes_accessed=2 * width * 640, transcendentals=0
+        ),
+        name="project",
+    )(place, *parts, gain, wq, wk, wv)
+
+
+def attend_kernel(place, table, meta, q, kv_mine, kv_other, *refs):
+    count = 2 * KV_HEADS
+    held, (out, blocks, placed, sems) = refs[:count], refs[count:]
+    requests = meta.shape[0]
+    listed = meta.shape[1] - 1
+    tokens = q.shape[0]
+    question = tokens // requests
+    heads = q.shape[1] // HEAD_DIM
+    group = heads * question
+    rows = held[0].shape[0]
+    pair, core = place[0], place[1]
+    copies = [pltpu.make_async_copy(held[i], blocks.at[i], sems.at[i]) for i in range(count)]
+    for copy in copies:
+        copy.start()
+    scale = HEAD_DIM ** (-0.5)
+    first = core == 0
+    half = HEAD_DIM // 2
+    a, b = kv_mine[...].astype(jnp.float32), kv_other[...].astype(jnp.float32)
+    lo, hi = jnp.where(first, a, b), jnp.where(first, b, a)
+    own_key = jnp.concatenate([lo[:, :half], hi[:, :half]], axis=1).astype(jnp.bfloat16)
+    own_value = jnp.concatenate([lo[:, half:], hi[:, half:]], axis=1).astype(jnp.bfloat16)
+    wide = q[...].astype(jnp.float32)
+    queries = []
+    for r in range(requests):
+        piece = wide[r * question : (r + 1) * question]
+        queries.append(
+            jnp.concatenate(
+                [piece[:, h * HEAD_DIM : (h + 1) * HEAD_DIM] for h in range(heads)], axis=0
+            ).astype(jnp.bfloat16)
+        )
+    stacked = jnp.concatenate(queries, axis=0)
+    scores = matmul(stacked, own_key, ((1,), (1,))) * scale
+    row = lax.broadcasted_iota(jnp.int32, scores.shape, 0)
+    column = lax.broadcasted_iota(jnp.int32, scores.shape, 1)
+    seen = (row // group == column // question) & (column % question <= row % question)
+    own_top = jnp.max(jnp.where(seen, scores, far_below), axis=-1, keepdims=True)
+    weights = jnp.where(seen, jnp.exp(scores - own_top), 0.0)
+    own_total = jnp.sum(weights, axis=-1, keepdims=True)
+    own_acc = matmul(weights.astype(jnp.bfloat16), own_value)
+    for copy in copies:
+        copy.wait()
+    for r in range(requests):
+        away = lax.rem(pair - r // CORES + KV_HEADS, KV_HEADS)
+        at = CORES * away + lax.rem(r + core, CORES)
+        live = meta[at, listed]
+        mine = slice(r * group, (r + 1) * group)
+        tops, totals, accs = [], [], []
+        for k in range(listed):
+            slot = table[meta[at, k]]
+            owner, line = slot // rows, lax.rem(slot, rows)
+            source = CORES * lax.rem(pair - owner // CORES + KV_HEADS, KV_HEADS) + lax.rem(owner + core, CORES)
+            part = matmul(queries[r], blocks[source, line, 0], ((1,), (1,))) * scale
+            top = jnp.max(part, axis=-1, keepdims=True)
+            weights = jnp.exp(part - top)
+            total = jnp.sum(weights, axis=-1, keepdims=True)
+            accs.append(matmul(weights.astype(jnp.bfloat16), blocks[source, line, 1]))
+            tops.append(jnp.where(k < live, top, far_below))
+            totals.append(total)
+        peak = own_top[mine]
+        for top in tops:
+            peak = jnp.maximum(peak, top)
+        factor = jnp.exp(own_top[mine] - peak)
+        numerator, denominator = own_acc[mine] * factor, own_total[mine] * factor
+        for k in range(listed):
+            factor = jnp.where(k < live, jnp.exp(tops[k] - peak), 0.0)
+            numerator = numerator + accs[k] * factor
+            denominator = denominator + totals[k] * factor
+        context = numerator / denominator
+        for h in range(heads):
+            placed[r * question : (r + 1) * question, h * HEAD_DIM : (h + 1) * HEAD_DIM] = context[
+                h * question : (h + 1) * question
+            ]
+    out[...] = placed[...].astype(out.dtype)
+
+
+def attend(place, table, meta, q, kv_mine, kv_other, held):
+    return pl.pallas_call(
+        attend_kernel,
+        out_shape=jax.ShapeDtypeStruct(q.shape, jnp.bfloat16),
+        in_specs=[SMEM] * 3 + [VMEM] * 3 + [ANYWHERE] * len(held),
+        out_specs=VMEM,
+        scratch_shapes=[
+            pltpu.VMEM((len(held), *held[0].shape), jnp.bfloat16),
+            pltpu.VMEM(q.shape, jnp.float32),
+            pltpu.SemaphoreType.DMA((len(held),)),
+        ],
+        compiler_params=pltpu.CompilerParams(vmem_limit_bytes=16 * MIB),
+        cost_estimate=pl.CostEstimate(
+            flops=1 << 28, bytes_accessed=2 * MIB, transcendentals=1 << 18
+        ),
+        name="attend",
+    )(place, table, meta, q, kv_mine, kv_other, *held)
+
+
+def finish_kernel(place, *refs):
+    count = 2 * KV_HEADS
+    parts, (cols, w_out, keep, give, w_vm, placed, sems) = refs[:count], refs[count:]
+    pair, core = place[0], place[1]
+    depth = parts[0].shape[1]
+    copies, spans = [], []
+    for i in range(count):
+        source = CORES * lax.rem(pair - i // CORES + KV_HEADS, KV_HEADS) + lax.rem(i + core, CORES)
+        span = pl.ds(pl.multiple_of(source * depth, depth), depth)
+        copy = pltpu.make_async_copy(w_out.at[0, span], w_vm.at[i], sems.at[i])
+        copy.start()
+        copies.append(copy)
+    total = cols[...].astype(jnp.float32) * 0.0
+    for i in range(count):
+        copies[i].wait()
+        total = total + matmul(parts[i][...], w_vm[i])
+    placed[...] = cols[...].astype(jnp.float32) + total
+    question = keep.shape[1]
+    for z in range(KV_HEADS):
+        lo = placed[z * 2 * question : (z * 2 + 1) * question]
+        hi = placed[(z * 2 + 1) * question : (z * 2 + 2) * question]
+        keep[z] = jnp.where(core == 0, lo, hi).astype(keep.dtype)
+        give[z] = jnp.where(core == 0, hi, lo).astype(give.dtype)
+
+
+def finish(place, parts, cols, w_out):
+    count = len(parts)
+    tokens, width = cols.shape
+    shape = jax.ShapeDtypeStruct((KV_HEADS, tokens // count, width), jnp.bfloat16)
+    return pl.pallas_call(
+        finish_kernel,
+        out_shape=[shape] * 2,
+        in_specs=[SMEM] + [VMEM] * (count + 1) + [ANYWHERE],
+        out_specs=[VMEM] * 2,
+        scratch_shapes=[
+            pltpu.VMEM((count, parts[0].shape[1], width), jnp.bfloat16),
+            pltpu.VMEM((tokens, width), jnp.float32),
+            pltpu.SemaphoreType.DMA((count,)),
+        ],
+        compiler_params=pltpu.CompilerParams(vmem_limit_bytes=24 * MIB),
+        cost_estimate=pl.CostEstimate(
+            flops=2 * tokens * w_out.size, bytes_accessed=2 * w_out.size, transcendentals=0
+        ),
+        name="finish",
+    )(place, *parts, cols, w_out)
+
+
+def place_kernel(place, *refs):
+    parts, out = refs[:-1], refs[-1]
+    pair, core = place[0], place[1]
+    width = parts[0].shape[2]
+    for k, part in enumerate(parts):
+        for p in range(CORES):
+            source = CORES * lax.rem(pair - k + KV_HEADS, KV_HEADS) + lax.rem(core + p, CORES)
+            out[0, :, pl.ds(pl.multiple_of(source * width, width), width)] = part[p]
+
+
+def place_columns(place, parts):
+    cores, rows, width = parts[0].shape
+    return pl.pallas_call(
+        place_kernel,
+        out_shape=jax.ShapeDtypeStruct((1, rows, width * cores * len(parts)), jnp.bfloat16),
+        in_specs=[SMEM] + [VMEM] * len(parts),
+        out_specs=VMEM,
+        name="place",
+    )(place, *parts)
+
+
+def by_head(hidden, gain, w_query, w_key, w_value, w_out, cache, block_slot, retrieved, counts):
+    size, sections = lax.axis_size("dev"), lax.axis_size("segment")
+    me = lax.axis_index("dev")
+    pair, core = me // CORES, me % CORES
+    place = jnp.stack([pair, core]).astype(jnp.int32)
+
+    state = hidden[0]
+    arrived = [state] + [to_pair(state, k) for k in range(1, KV_HEADS)]
+    parts = [p for a in arrived for p in (a, to_partner(a))]
+
+    packed = pack(place, cache)
+    held = [packed[0]]
+    for k in range(1, KV_HEADS):
+        mine = packed[k] if k == 1 else after(packed[k], arrived[3])
+        held.append(to_pair(mine, k))
+    held = [h for a in held for h in (a, to_partner(a))]
+
+    entry = jnp.concatenate([retrieved[0], counts], axis=1)
+    entries = [entry] + [to_pair(entry, k) for k in range(1, KV_HEADS)]
+    stacked = jnp.concatenate(entries, axis=0)
+    both = jnp.stack([stacked, to_partner(stacked)], axis=1)
+    meta = both.reshape(size, entry.shape[1])
+
+    q, kv, cols = project(
+        place, parts, gain, w_query, w_key[0].swapaxes(0, 1), w_value[0].swapaxes(0, 1)
+    )
+    context = attend(place, block_slot, meta, q, kv, to_partner(kv), held)
+    contexts = [context] + [to_pair(context, k) for k in range(1, KV_HEADS)]
+    contexts = [p for a in contexts for p in (a, to_partner(a))]
+    keep, give = finish(place, contexts, cols, w_out)
+    sent = jnp.stack([keep, to_partner(give)], axis=1)
+    final = []
+    for k in range(KV_HEADS):
+        piece = lax.dynamic_index_in_dim(sent, (pair + k) % KV_HEADS, 0, keepdims=False)
+        route = [
+            (s * size + d, (s + 1) % sections * size + (d + CORES * k) % size)
+            for s in range(sections)
+            for d in range(size)
+        ]
+        final.append(lax.ppermute(piece, ("segment", "dev"), route))
+    return place_columns(place, final)
+
+
 def solution(mesh):
+    heads_fit = mesh.shape["dev"] == CORES * KV_HEADS
     return jax.shard_map(
-        body,
+        by_head if heads_fit else general_body,
         mesh=mesh,
         in_specs=(
             P("segment", "dev", None),

time: 179 us -> 133 us (0.74)
  Pallas kernels: 0 us -> 55.8 us
  blocking collectives: 47.1 us -> 0 us
  waiting for transfers between devices: 64 us -> 33 us
  starting transfers between devices: 15.2 us -> 31 us
  matrix products: 14.7 us -> 0 us
  between operations: 14.3 us -> 0.79 us
  local copies, waits for them, and re-layouts: 17.5 us -> 8.72 us
  other arithmetic: 5.13 us -> 2.8 us
    all_to_all x4 -> x0, waiting for transfers between devices: 59.6 us -> none  [the longest x1 47.6 us: body(): lax.all_to_all(selected, 'dev', split_axis=0, concat_axis=0, tiled=True)]
    pallas_call x0 -> x5, Pallas kernels: none -> 55.8 us  [the longest x1 33.6 us: pack(): pl.pallas_call(pack_kernel, out_shape=[shape] * pairs, in_specs=[SMEM, AN...]
    ppermute x1 -> x31, starting transfers between devices: 1.56 us -> 31 us  [the longest x12 20.9 us: to_pair(): lax.ppermute(x, 'dev', [(d, (d + CORES * k) % size) for d in range(size)])]
    ppermute x1 -> x31, waiting for transfers between devices: 4.36 us -> 33 us  [the longest x12 25 us: to_pair(): lax.ppermute(x, 'dev', [(d, (d + CORES * k) % size) for d in range(size)])]
    all_gather x2 -> x0, blocking collectives: 24.2 us -> none  [the longest x1 14.9 us: body(): lax.all_gather(context, 'dev', axis=0, tiled=True)]
    dot_general x7 -> x0, matrix products: 14.7 us -> none  [the longest x1 6.66 us: body(): jnp.dot(lax.all_gather(normed, 'dev', axis=0, tiled=True), stacked, prefe...]
    all_to_all x4 -> x0, starting transfers between devices: 13.6 us -> none  [the longest x1 3.6 us: body(): lax.all_to_all(selected, 'dev', split_axis=0, concat_axis=0, tiled=True)]
    all_to_all x1 -> x0, blocking collectives: 12.1 us -> none  [body(): lax.all_to_all(branch_cols, 'dev', split_axis=0, concat_axis=1, tiled=True)]
  transfers between devices with their start and end apart: 6 -> 31, of which waited for: 5 -> 14; matrix products, arithmetic and copies ran while one was open for 8% -> 2% of each run, Pallas kernels for 0% -> 29%
where the time goes in v1:
time: 133 us; the launch traced here: 132 us
  Pallas kernels  55.8 us (42%)
  waiting for transfers between devices  33 us (25%)
  starting transfers between devices  31 us (23%)
  local copies, waits for them, and re-layouts  8.72 us (7%)
  other arithmetic  2.8 us (2%)
    pallas_call x1, Pallas kernels, pack(): pl.pallas_call(pack_kernel, out_shape=[shape] * pairs, in_specs=[SMEM, AN...  33.6 us
    ppermute x12, waiting for transfers between devices, to_pair(): lax.ppermute(x, 'dev', [(d, (d + CORES * k) % size) for d in range(size)])  25 us
    ppermute x12, starting transfers between devices, to_pair(): lax.ppermute(x, 'dev', [(d, (d + CORES * k) % size) for d in range(size)])  20.9 us
    pallas_call x1, Pallas kernels, attend(): pl.pallas_call(attend_kernel, out_shape=jax.ShapeDtypeStruct(q.shape, jnp...  12.5 us
    unnamed x26, local copies, waits for them, and re-layouts  8.71 us
    ppermute x4, starting transfers between devices, by_head(): final.append(lax.ppermute(piece, ('segment', 'dev'), route))  7.23 us
    pallas_call x1, Pallas kernels, project(): pl.pallas_call(project_kernel, out_shape=[jax.ShapeDtypeStruct((tokens, w...  5.23 us
    ppermute x4, waiting for transfers between devices, by_head(): final.append(lax.ppermute(piece, ('segment', 'dev'), route))  4.76 us
  transfers between devices with their start and end apart: 31, of which 14 were waited for; matrix products, arithmetic and copies ran while one was open for 2% of the time, Pallas kernels for 29%

profile of v1, /device:TPU:0, one launch (start us, length us, event | category | flops | bytes accessed | tf_op | source)
XLA Modules:
  0.0 132.1 jit_solution(3197376985760849738)
XLA Ops:
  0.5 4.6 %collective-permute-start.9 = (bf16[8,8192]{1,0:T(8,128)(2,1)}, bf16[8,8192]{1,0:T(8,128)(2,1)S(1)}, u32[]{:S(2)}, u32[]{:S(2)}) collective-permute-start(bf16[8,8192]{1,0:T(8,128)(2,1)} %bitcast.27), channel_id=1, source_target_pairs={{0,6},{1,7},{2,0},{3,1},{4,2},{5,3},{6,4},{7,5},{8,14},{9,15},{10,... | collective-permute-start | bytes 393224 | tf_op jit(solution)/shard_map/ppermute | solution.py:157
  6.9 1.6 %collective-permute-start.5 = (bf16[8,8192]{1,0:T(8,128)(2,1)}, bf16[8,8192]{1,0:T(8,128)(2,1)S(1)}, u32[]{:S(2)}, u32[]{:S(2)}) collective-permute-start(bf16[8,8192]{1,0:T(8,128)(2,1)} %bitcast.28), channel_id=1, source_target_pairs={{0,2},{1,3},{2,4},{3,5},{4,6},{5,7},{6,0},{7,1},{8,10},{9,11},{10,... | collective-permute-start | bytes 393224 | tf_op jit(solution)/shard_map/ppermute | solution.py:157
  9.1 33.6 %pack.1 = (bf16[4,2,128,128]{3,2,1,0:T(8,128)(2,1)}, bf16[4,2,128,128]{3,2,1,0:T(8,128)(2,1)}, bf16[4,2,128,128]{3,2,1,0:T(8,128)(2,1)}, bf16[4,2,128,128]{3,2,1,0:T(8,128)(2,1)}) custom-call(s32[2]{0:T(128)} %pad_add_fusion.2.place, bf16[1,4,128,1024]{3,2,1,0:T(8,128)(2,1)} %cache.1), custom_call_target="tpu_custom_call" | custom-call | bytes 2097152 | tf_op jit(solution)/shard_map/pack/pallas_call | solution.py:194
  42.7 2.0 %collective-permute-start = (s32[1,7]{1,0:T(1,128)S(1)}, s32[1,7]{1,0:T(1,128)S(1)}, u32[]{:S(2)}, u32[]{:S(2)}) collective-permute-start(s32[1,7]{1,0:T(1,128)S(1)} %pad_add_fusion.3), channel_id=1, source_target_pairs={{0,2},{1,3},{2,4},{3,5},{4,6},{5,7},{6,0},{7,1},{8,10},{9,11},{10,... | collective-permute-start | bytes 92 | tf_op jit(solution)/shard_map/ppermute | solution.py:157
  44.7 1.1 collective-permute-start.7
  45.8 1.4 %collective-permute-start.13 = (bf16[4,2,128,128]{3,2,1,0:T(8,128)(2,1)}, bf16[4,2,128,128]{3,2,1,0:T(8,128)(2,1)S(1)}, u32[]{:S(2)}, u32[]{:S(2)}) collective-permute-start(bf16[4,2,128,128]{3,2,1,0:T(8,128)(2,1)} %get-tuple-element.19), channel_id=1, source_target_pairs={{0,2},{1,3},{2,4},{3,5},{4,6},{5,7},{6,0},{7,1},{8,10},{9,11},{10,... | collective-permute-start | bytes 786440 | tf_op jit(solution)/shard_map/ppermute | solution.py:157
  47.2 0.9 collective-permute-done
  48.1 2.2 %collective-permute-start.15 = (bf16[4,2,128,128]{3,2,1,0:T(8,128)(2,1)}, bf16[4,2,128,128]{3,2,1,0:T(8,128)(2,1)S(1)}, u32[]{:S(2)}, u32[]{:S(2)}) collective-permute-start(bf16[4,2,128,128]{3,2,1,0:T(8,128)(2,1)} %get-tuple-element.21), channel_id=1, source_target_pairs={{0,4},{1,5},{2,6},{3,7},{4,0},{5,1},{6,2},{7,3},{8,12},{9,13},{10,... | collective-permute-start | bytes 786440 | tf_op jit(solution)/shard_map/ppermute | solution.py:157
  50.6 14.9 %collective-permute-done.7.refs_4_ = bf16[8,8192]{1,0:T(8,128)(2,1)S(1)} collective-permute-done((bf16[8,8192]{1,0:T(8,128)(2,1)}, bf16[8,8192]{1,0:T(8,128)(2,1)S(1)}, u32[]{:S(2)}, u32[]{:S(2)}) %collective-permute-start.7) | collective-permute-done | bytes 131104 | tf_op jit(solution)/shard_map/ppermute | solution.py:157
  67.4 3.8 %collective-permute-done.15.refs_4_ = bf16[4,2,128,128]{3,2,1,0:T(8,128)(2,1)S(1)} collective-permute-done((bf16[4,2,128,128]{3,2,1,0:T(8,128)(2,1)}, bf16[4,2,128,128]{3,2,1,0:T(8,128)(2,1)S(1)}, u32[]{:S(2)}, u32[]{:S(2)}) %collective-permute-start.15) | collective-permute-done | bytes 262176 | tf_op jit(solution)/shard_map/ppermute | solution.py:157
  72.4 3.4 %copy-done = bf16[1,8192,512]{2,1,0:T(8,128)(2,1)S(1)} copy-done((bf16[1,8192,512]{2,1,0:T(8,128)(2,1)S(1)}, bf16[1,8192,512]{2,1,0:T(8,128)(2,1)}, u32[]{:S(2)}) %copy-start) | copy-done | bytes 8388632
  75.8 1.2 copy-done.2
  77.0 1.2 copy-done.3
  78.2 0.9 copy-done.5
  79.1 0.8 copy-done.6
  80.5 5.2 %project.1 = (bf16[64,512]{1,0:T(8,128)(2,1)S(1)}, bf16[64,128]{1,0:T(8,128)(2,1)S(1)}, bf16[64,1024]{1,0:T(8,128)(2,1)S(1)}) custom-call(s32[2]{0:T(128)S(1)} %copy-done.7, bf16[8,8192]{1,0:T(8,128)(2,1)S(1)} %bitcast.30, bf16[8,8192]{1,0:T(8,128)(2,1)S(1)} %collective-permute-done.4.refs_1_, bf16[8,8192]{1,0:T(8,128)(2,1)S(1)} %collective-permute-done.5.refs_2_, ...), custom_call_target="tpu_custom_call" | custom-call | flops 671088640 | bytes 10485760 | tf_op jit(solution)/shard_map/project/pallas_call | solution.py:254
  86.3 0.8 collective-permute-done.11.kv_other
  87.2 12.5 %attend.1.refs_0_ = bf16[64,512]{1,0:T(8,128)(2,1)S(1)} custom-call(s32[2]{0:T(128)S(1)} %copy-done.7, s32[32]{0:T(128)S(1)} %copy-done.8, s32[8,7]{1,0:T(8,128)S(1)} %bitcast.32, bf16[64,512]{1,0:T(8,128)(2,1)S(1)} %get-tuple-element.16.q, bf16[64,128]{1,0:T(8,128)(2,1)S(1)} %get-tuple-element.17.kv_mine, ...), custom_call_target="tpu_custom_call" | custom-call | flops 268435456 | bytes 2097152 | tf_op jit(solution)/shard_map/attend/pallas_call | solution.py:354
  99.7 4.9 %collective-permute-start.20 = (bf16[64,512]{1,0:T(8,128)(2,1)S(1)}, bf16[64,512]{1,0:T(8,128)(2,1)S(1)}, u32[]{:S(2)}, u32[]{:S(2)}) collective-permute-start(bf16[64,512]{1,0:T(8,128)(2,1)S(1)} %attend.1.refs_0_), channel_id=1, source_target_pairs={{0,2},{1,3},{2,4},{3,5},{4,6},{5,7},{6,0},{7,1},{8,10},{9,11},{10,... | collective-permute-start | bytes 196616 | tf_op jit(solution)/shard_map/ppermute | solution.py:157
  104.6 2.4 %collective-permute-start.22 = (bf16[64,512]{1,0:T(8,128)(2,1)S(1)}, bf16[64,512]{1,0:T(8,128)(2,1)S(1)}, u32[]{:S(2)}, u32[]{:S(2)}) collective-permute-start(bf16[64,512]{1,0:T(8,128)(2,1)S(1)} %attend.1.refs_0_), channel_id=1, source_target_pairs={{0,4},{1,5},{2,6},{3,7},{4,0},{5,1},{6,2},{7,3},{8,12},{9,13},{10,... | collective-permute-start | bytes 196616 | tf_op jit(solution)/shard_map/ppermute | solution.py:157
  107.0 2.3 %collective-permute-done.20.refs_2_ = bf16[64,512]{1,0:T(8,128)(2,1)S(1)} collective-permute-done((bf16[64,512]{1,0:T(8,128)(2,1)S(1)}, bf16[64,512]{1,0:T(8,128)(2,1)S(1)}, u32[]{:S(2)}, u32[]{:S(2)}) %collective-permute-start.20) | collective-permute-done | bytes 65568 | tf_op jit(solution)/shard_map/ppermute | solution.py:157
  109.4 2.6 %collective-permute-done.22.refs_4_ = bf16[64,512]{1,0:T(8,128)(2,1)S(1)} collective-permute-done((bf16[64,512]{1,0:T(8,128)(2,1)S(1)}, bf16[64,512]{1,0:T(8,128)(2,1)S(1)}, u32[]{:S(2)}, u32[]{:S(2)}) %collective-permute-start.22) | collective-permute-done | bytes 65568 | tf_op jit(solution)/shard_map/ppermute | solution.py:157
  113.7 3.0 %finish.1 = (bf16[4,8,1024]{2,1,0:T(8,128)(2,1)S(1)}, bf16[4,8,1024]{2,1,0:T(8,128)(2,1)S(1)}) custom-call(s32[2]{0:T(128)S(1)} %copy-done.7, bf16[64,512]{1,0:T(8,128)(2,1)S(1)} %attend.1.refs_0_, bf16[64,512]{1,0:T(8,128)(2,1)S(1)} %collective-permute-done.19.refs_1_, bf16[64,512]{1,0:T(8,128)(2,1)S(1)} %collective-permute-done.20.refs_2_, ...), custom_call_target="tpu_custom_call" | custom-call | flops 536870912 | bytes 8388608 | tf_op jit(solution)/shard_map/finish/pallas_call | solution.py:401
  116.9 1.1 collective-permute-done.26
  118.0 1.5 %collective-permute-start.27 = (bf16[2,8,1024]{2,1,0:T(8,128)(2,1)S(1)}, bf16[2,8,1024]{2,1,0:T(8,128)(2,1)S(1)}, u32[]{:S(2)}, u32[]{:S(2)}) collective-permute-start(bf16[2,8,1024]{2,1,0:T(8,128)(2,1)S(1)} %get-tuple-element.28), channel_id=1, source_target_pairs={{0,8},{1,9},{2,10},{3,11},{4,12},{5,13},{6,14},{7,15},{8,16},{9,17... | collective-permute-start | bytes 98312 | tf_op jit(solution)/shard_map/ppermute | solution.py:479
  119.5 2.3 %collective-permute-start.28 = (bf16[2,8,1024]{2,1,0:T(8,128)(2,1)S(1)}, bf16[2,8,1024]{2,1,0:T(8,128)(2,1)S(1)}, u32[]{:S(2)}, u32[]{:S(2)}) collective-permute-start(bf16[2,8,1024]{2,1,0:T(8,128)(2,1)S(1)} %get-tuple-element.29), channel_id=1, source_target_pairs={{0,10},{1,11},{2,12},{3,13},{4,14},{5,15},{6,8},{7,9},{8,18},{9,19... | collective-permute-start | bytes 98312 | tf_op jit(solution)/shard_map/ppermute | solution.py:479
  121.8 2.4 %collective-permute-start.29 = (bf16[2,8,1024]{2,1,0:T(8,128)(2,1)S(1)}, bf16[2,8,1024]{2,1,0:T(8,128)(2,1)S(1)}, u32[]{:S(2)}, u32[]{:S(2)}) collective-permute-start(bf16[2,8,1024]{2,1,0:T(8,128)(2,1)S(1)} %get-tuple-element.30), channel_id=1, source_target_pairs={{0,12},{1,13},{2,14},{3,15},{4,8},{5,9},{6,10},{7,11},{8,20},{9,21... | collective-permute-start | bytes 98312 | tf_op jit(solution)/shard_map/ppermute | solution.py:479
  124.3 0.9 collective-permute-start.30
  125.2 1.9 %collective-permute-done.28.refs_1_ = bf16[2,8,1024]{2,1,0:T(8,128)(2,1)S(1)} collective-permute-done((bf16[2,8,1024]{2,1,0:T(8,128)(2,1)S(1)}, bf16[2,8,1024]{2,1,0:T(8,128)(2,1)S(1)}, u32[]{:S(2)}, u32[]{:S(2)}) %collective-permute-start.28) | collective-permute-done | bytes 32800 | tf_op jit(solution)/shard_map/ppermute | solution.py:479
  127.1 1.4 %collective-permute-done.29.refs_2_ = bf16[2,8,1024]{2,1,0:T(8,128)(2,1)S(1)} collective-permute-done((bf16[2,8,1024]{2,1,0:T(8,128)(2,1)S(1)}, bf16[2,8,1024]{2,1,0:T(8,128)(2,1)S(1)}, u32[]{:S(2)}, u32[]{:S(2)}) %collective-permute-start.29) | collective-permute-done | bytes 32800 | tf_op jit(solution)/shard_map/ppermute | solution.py:479
  128.5 1.5 %collective-permute-done.30.refs_3_ = bf16[2,8,1024]{2,1,0:T(8,128)(2,1)S(1)} collective-permute-done((bf16[2,8,1024]{2,1,0:T(8,128)(2,1)S(1)}, bf16[2,8,1024]{2,1,0:T(8,128)(2,1)S(1)}, u32[]{:S(2)}, u32[]{:S(2)}) %collective-permute-start.30) | collective-permute-done | bytes 32800 | tf_op jit(solution)/shard_map/ppermute | solution.py:479
  130.6 1.5 %place.1 = bf16[1,8,8192]{2,1,0:T(8,128)(2,1)} custom-call(s32[2]{0:T(128)} %pad_add_fusion.2.place, bf16[2,8,1024]{2,1,0:T(8,128)(2,1)} %copy-done.9, bf16[2,8,1024]{2,1,0:T(8,128)(2,1)} %copy-done.10, bf16[2,8,1024]{2,1,0:T(8,128)(2,1)} %copy-done.11, bf16[2,8,1024]{2,1,0:T(8,128)(2,1)} %copy-done.12), custom_call_target="tpu_custom_call" | custom-call | tf_op jit(solution)/shard_map/place/pallas_call | solution.py:431
  (68 shorter events, 9.5 us)
Async XLA Ops:
  0.0 87.1 %copy-start.8 = (s32[32]{0:T(128)S(1)}, s32[32]{0:T(128)}, u32[]{:S(2)}) copy-start(s32[32]{0:T(128)} %table.1) | copy-start | bytes 388
  0.0 50.3 %collective-permute-start.4 = (bf16[8,8192]{1,0:T(8,128)(2,1)}, bf16[8,8192]{1,0:T(8,128)(2,1)S(1)}, u32[]{:S(2)}, u32[]{:S(2)}) collective-permute-start(bf16[8,8192]{1,0:T(8,128)(2,1)} %bitcast.26), channel_id=1, source_target_pairs={{0,1},{1,0},{2,3},{3,2},{4,5},{5,4},{6,7},{7,6},{8,9},{9,8},{10,11... | collective-permute-start | bytes 393224 | tf_op jit(solution)/shard_map/ppermute | solution.py:161
  0.5 42.3 %collective-permute-start.9 = (bf16[8,8192]{1,0:T(8,128)(2,1)}, bf16[8,8192]{1,0:T(8,128)(2,1)S(1)}, u32[]{:S(2)}, u32[]{:S(2)}) collective-permute-start(bf16[8,8192]{1,0:T(8,128)(2,1)} %bitcast.27), channel_id=1, source_target_pairs={{0,6},{1,7},{2,0},{3,1},{4,2},{5,3},{6,4},{7,5},{8,14},{9,15},{10,... | collective-permute-start | bytes 393224 | tf_op jit(solution)/shard_map/ppermute | solution.py:157
  6.5 38.2 %collective-permute-start.2 = (s32[1,7]{1,0:T(1,128)S(1)}, s32[1,7]{1,0:T(1,128)S(1)}, u32[]{:S(2)}, u32[]{:S(2)}) collective-permute-start(s32[1,7]{1,0:T(1,128)S(1)} %pad_add_fusion.3), channel_id=1, source_target_pairs={{0,6},{1,7},{2,0},{3,1},{4,2},{5,3},{6,4},{7,5},{8,14},{9,15},{10,... | collective-permute-start | bytes 92 | tf_op jit(solution)/shard_map/ppermute | solution.py:157
  6.9 38.9 %collective-permute-start.1 = (s32[1,7]{1,0:T(1,128)S(1)}, s32[1,7]{1,0:T(1,128)S(1)}, u32[]{:S(2)}, u32[]{:S(2)}) collective-permute-start(s32[1,7]{1,0:T(1,128)S(1)} %pad_add_fusion.3), channel_id=1, source_target_pairs={{0,4},{1,5},{2,6},{3,7},{4,0},{5,1},{6,2},{7,3},{8,12},{9,13},{10,... | collective-permute-start | bytes 92 | tf_op jit(solution)/shard_map/ppermute | solution.py:157
  6.9 43.7 %collective-permute-start.5 = (bf16[8,8192]{1,0:T(8,128)(2,1)}, bf16[8,8192]{1,0:T(8,128)(2,1)S(1)}, u32[]{:S(2)}, u32[]{:S(2)}) collective-permute-start(bf16[8,8192]{1,0:T(8,128)(2,1)} %bitcast.28), channel_id=1, source_target_pairs={{0,2},{1,3},{2,4},{3,5},{4,6},{5,7},{6,0},{7,1},{8,10},{9,11},{10,... | collective-permute-start | bytes 393224 | tf_op jit(solution)/shard_map/ppermute | solution.py:157
  42.7 5.4 %collective-permute-start = (s32[1,7]{1,0:T(1,128)S(1)}, s32[1,7]{1,0:T(1,128)S(1)}, u32[]{:S(2)}, u32[]{:S(2)}) collective-permute-start(s32[1,7]{1,0:T(1,128)S(1)} %pad_add_fusion.3), channel_id=1, source_target_pairs={{0,2},{1,3},{2,4},{3,5},{4,6},{5,7},{6,0},{7,1},{8,10},{9,11},{10,... | collective-permute-start | bytes 92 | tf_op jit(solution)/shard_map/ppermute | solution.py:157
  44.7 20.8 %collective-permute-start.7 = (bf16[8,8192]{1,0:T(8,128)(2,1)}, bf16[8,8192]{1,0:T(8,128)(2,1)S(1)}, u32[]{:S(2)}, u32[]{:S(2)}) collective-permute-start(bf16[8,8192]{1,0:T(8,128)(2,1)} %bitcast.29), channel_id=1, source_target_pairs={{0,4},{1,5},{2,6},{3,7},{4,0},{5,1},{6,2},{7,3},{8,12},{9,13},{10,... | collective-permute-start | bytes 393224 | tf_op jit(solution)/shard_map/ppermute | solution.py:157
  45.8 21.2 %collective-permute-start.13 = (bf16[4,2,128,128]{3,2,1,0:T(8,128)(2,1)}, bf16[4,2,128,128]{3,2,1,0:T(8,128)(2,1)S(1)}, u32[]{:S(2)}, u32[]{:S(2)}) collective-permute-start(bf16[4,2,128,128]{3,2,1,0:T(8,128)(2,1)} %get-tuple-element.19), channel_id=1, source_target_pairs={{0,2},{1,3},{2,4},{3,5},{4,6},{5,7},{6,0},{7,1},{8,10},{9,11},{10,... | collective-permute-start | bytes 786440 | tf_op jit(solution)/shard_map/ppermute | solution.py:157
  48.1 23.0 %collective-permute-start.15 = (bf16[4,2,128,128]{3,2,1,0:T(8,128)(2,1)}, bf16[4,2,128,128]{3,2,1,0:T(8,128)(2,1)S(1)}, u32[]{:S(2)}, u32[]{:S(2)}) collective-permute-start(bf16[4,2,128,128]{3,2,1,0:T(8,128)(2,1)} %get-tuple-element.21), channel_id=1, source_target_pairs={{0,4},{1,5},{2,6},{3,7},{4,0},{5,1},{6,2},{7,3},{8,12},{9,13},{10,... | collective-permute-start | bytes 786440 | tf_op jit(solution)/shard_map/ppermute | solution.py:157
  50.3 20.8 %collective-permute-start.17 = (bf16[4,2,128,128]{3,2,1,0:T(8,128)(2,1)}, bf16[4,2,128,128]{3,2,1,0:T(8,128)(2,1)S(1)}, u32[]{:S(2)}, u32[]{:S(2)}) collective-permute-start(bf16[4,2,128,128]{3,2,1,0:T(8,128)(2,1)} %get-tuple-element.23), channel_id=1, source_target_pairs={{0,6},{1,7},{2,0},{3,1},{4,2},{5,3},{6,4},{7,5},{8,14},{9,15},{10,... | collective-permute-start | bytes 786440 | tf_op jit(solution)/shard_map/ppermute | solution.py:157
  50.6 14.9 %collective-permute-start.6 = (bf16[8,8192]{1,0:T(8,128)(2,1)S(1)}, bf16[8,8192]{1,0:T(8,128)(2,1)S(1)}, u32[]{:S(2)}, u32[]{:S(2)}) collective-permute-start(bf16[8,8192]{1,0:T(8,128)(2,1)S(1)} %collective-permute-done.5.refs_2_), channel_id=1, source_target_pairs={{0,1},{1,0},{2,3},{3,2},{4,5},{5,4},{6,7},{7,6},{8,9},{9,8},{10,11... | collective-permute-start | bytes 393224 | tf_op jit(solution)/shard_map/ppermute | solution.py:161
  65.5 1.3 %collective-permute-start.8 = (bf16[8,8192]{1,0:T(8,128)(2,1)S(1)}, bf16[8,8192]{1,0:T(8,128)(2,1)S(1)}, u32[]{:S(2)}, u32[]{:S(2)}) collective-permute-start(bf16[8,8192]{1,0:T(8,128)(2,1)S(1)} %collective-permute-done.7.refs_4_), channel_id=1, source_target_pairs={{0,1},{1,0},{2,3},{3,2},{4,5},{5,4},{6,7},{7,6},{8,9},{9,8},{10,11... | collective-permute-start | bytes 393224 | tf_op jit(solution)/shard_map/ppermute | solution.py:161
  65.5 6.9 %collective-permute-start.10 = (bf16[8,8192]{1,0:T(8,128)(2,1)S(1)}, bf16[8,8192]{1,0:T(8,128)(2,1)S(1)}, u32[]{:S(2)}, u32[]{:S(2)}) collective-permute-start(bf16[8,8192]{1,0:T(8,128)(2,1)S(1)} %collective-permute-done.9.refs_6_), channel_id=1, source_target_pairs={{0,1},{1,0},{2,3},{3,2},{4,5},{5,4},{6,7},{7,6},{8,9},{9,8},{10,11... | collective-permute-start | bytes 393224 | tf_op jit(solution)/shard_map/ppermute | solution.py:161
  66.8 19.5 %collective-permute-start.12 = (bf16[4,2,128,128]{3,2,1,0:T(8,128)(2,1)}, bf16[4,2,128,128]{3,2,1,0:T(8,128)(2,1)S(1)}, u32[]{:S(2)}, u32[]{:S(2)}) collective-permute-start(bf16[4,2,128,128]{3,2,1,0:T(8,128)(2,1)} %get-tuple-element.18.refs_0_), channel_id=1, source_target_pairs={{0,1},{1,0},{2,3},{3,2},{4,5},{5,4},{6,7},{7,6},{8,9},{9,8},{10,11... | collective-permute-start | bytes 786440 | tf_op jit(solution)/shard_map/ppermute | solution.py:161
  67.0 20.1 %collective-permute-start.14 = (bf16[4,2,128,128]{3,2,1,0:T(8,128)(2,1)S(1)}, bf16[4,2,128,128]{3,2,1,0:T(8,128)(2,1)S(1)}, u32[]{:S(2)}, u32[]{:S(2)}) collective-permute-start(bf16[4,2,128,128]{3,2,1,0:T(8,128)(2,1)S(1)} %collective-permute-done.13.refs_2_), channel_id=1, source_target_pairs={{0,1},{1,0},{2,3},{3,2},{4,5},{5,4},{6,7},{7,6},{8,9},{9,8},{10,11... | collective-permute-start | bytes 786440 | tf_op jit(solution)/shard_map/ppermute | solution.py:161
  71.1 16.0 %collective-permute-start.16 = (bf16[4,2,128,128]{3,2,1,0:T(8,128)(2,1)S(1)}, bf16[4,2,128,128]{3,2,1,0:T(8,128)(2,1)S(1)}, u32[]{:S(2)}, u32[]{:S(2)}) collective-permute-start(bf16[4,2,128,128]{3,2,1,0:T(8,128)(2,1)S(1)} %collective-permute-done.15.refs_4_), channel_id=1, source_target_pairs={{0,1},{1,0},{2,3},{3,2},{4,5},{5,4},{6,7},{7,6},{8,9},{9,8},{10,11... | collective-permute-start | bytes 786440 | tf_op jit(solution)/shard_map/ppermute | solution.py:161
  71.1 16.0 %collective-permute-start.18 = (bf16[4,2,128,128]{3,2,1,0:T(8,128)(2,1)S(1)}, bf16[4,2,128,128]{3,2,1,0:T(8,128)(2,1)S(1)}, u32[]{:S(2)}, u32[]{:S(2)}) collective-permute-start(bf16[4,2,128,128]{3,2,1,0:T(8,128)(2,1)S(1)} %collective-permute-done.17.refs_6_), channel_id=1, source_target_pairs={{0,1},{1,0},{2,3},{3,2},{4,5},{5,4},{6,7},{7,6},{8,9},{9,8},{10,11... | collective-permute-start | bytes 786440 | tf_op jit(solution)/shard_map/ppermute | solution.py:161
  72.4 13.4 %collective-permute-start.3 = (s32[4,7]{1,0:T(4,128)S(1)}, s32[4,7]{1,0:T(4,128)S(1)}, u32[]{:S(2)}, u32[]{:S(2)}) collective-permute-start(s32[4,7]{1,0:T(4,128)S(1)} %pad_add_fusion.1), channel_id=1, source_target_pairs={{0,1},{1,0},{2,3},{3,2},{4,5},{5,4},{6,7},{7,6},{8,9},{9,8},{10,11... | collective-permute-start | bytes 344 | tf_op jit(solution)/shard_map/ppermute | solution.py:161
  85.7 1.4 %collective-permute-start.11 = (bf16[64,128]{1,0:T(8,128)(2,1)S(1)}, bf16[64,128]{1,0:T(8,128)(2,1)S(1)}, u32[]{:S(2)}, u32[]{:S(2)}) collective-permute-start(bf16[64,128]{1,0:T(8,128)(2,1)S(1)} %get-tuple-element.17.kv_mine), channel_id=1, source_target_pairs={{0,1},{1,0},{2,3},{3,2},{4,5},{5,4},{6,7},{7,6},{8,9},{9,8},{10,11... | collective-permute-start | bytes 49160 | tf_op jit(solution)/shard_map/ppermute | solution.py:161
  99.7 9.6 %collective-permute-start.20 = (bf16[64,512]{1,0:T(8,128)(2,1)S(1)}, bf16[64,512]{1,0:T(8,128)(2,1)S(1)}, u32[]{:S(2)}, u32[]{:S(2)}) collective-permute-start(bf16[64,512]{1,0:T(8,128)(2,1)S(1)} %attend.1.refs_0_), channel_id=1, source_target_pairs={{0,2},{1,3},{2,4},{3,5},{4,6},{5,7},{6,0},{7,1},{8,10},{9,11},{10,... | collective-permute-start | bytes 196616 | tf_op jit(solution)/shard_map/ppermute | solution.py:157
  104.6 7.3 %collective-permute-start.22 = (bf16[64,512]{1,0:T(8,128)(2,1)S(1)}, bf16[64,512]{1,0:T(8,128)(2,1)S(1)}, u32[]{:S(2)}, u32[]{:S(2)}) collective-permute-start(bf16[64,512]{1,0:T(8,128)(2,1)S(1)} %attend.1.refs_0_), channel_id=1, source_target_pairs={{0,4},{1,5},{2,6},{3,7},{4,0},{5,1},{6,2},{7,3},{8,12},{9,13},{10,... | collective-permute-start | bytes 196616 | tf_op jit(solution)/shard_map/ppermute | solution.py:157
  107.0 5.5 %collective-permute-start.24 = (bf16[64,512]{1,0:T(8,128)(2,1)S(1)}, bf16[64,512]{1,0:T(8,128)(2,1)S(1)}, u32[]{:S(2)}, u32[]{:S(2)}) collective-permute-start(bf16[64,512]{1,0:T(8,128)(2,1)S(1)} %attend.1.refs_0_), channel_id=1, source_target_pairs={{0,6},{1,7},{2,0},{3,1},{4,2},{5,3},{6,4},{7,5},{8,14},{9,15},{10,... | collective-permute-start | bytes 196616 | tf_op jit(solution)/shard_map/ppermute | solution.py:157
  107.0 5.4 %collective-permute-start.19 = (bf16[64,512]{1,0:T(8,128)(2,1)S(1)}, bf16[64,512]{1,0:T(8,128)(2,1)S(1)}, u32[]{:S(2)}, u32[]{:S(2)}) collective-permute-start(bf16[64,512]{1,0:T(8,128)(2,1)S(1)} %attend.1.refs_0_), channel_id=1, source_target_pairs={{0,1},{1,0},{2,3},{3,2},{4,5},{5,4},{6,7},{7,6},{8,9},{9,8},{10,11... | collective-permute-start | bytes 196616 | tf_op jit(solution)/shard_map/ppermute | solution.py:161
  109.4 3.1 %collective-permute-start.21 = (bf16[64,512]{1,0:T(8,128)(2,1)S(1)}, bf16[64,512]{1,0:T(8,128)(2,1)S(1)}, u32[]{:S(2)}, u32[]{:S(2)}) collective-permute-start(bf16[64,512]{1,0:T(8,128)(2,1)S(1)} %collective-permute-done.20.refs_2_), channel_id=1, source_target_pairs={{0,1},{1,0},{2,3},{3,2},{4,5},{5,4},{6,7},{7,6},{8,9},{9,8},{10,11... | collective-permute-start | bytes 196616 | tf_op jit(solution)/shard_map/ppermute | solution.py:161
  112.0 1.3 collective-permute-start.23
  112.4 1.3 collective-permute-start.25
  116.6 1.3 collective-permute-start.26
  118.0 7.2 %collective-permute-start.27 = (bf16[2,8,1024]{2,1,0:T(8,128)(2,1)S(1)}, bf16[2,8,1024]{2,1,0:T(8,128)(2,1)S(1)}, u32[]{:S(2)}, u32[]{:S(2)}) collective-permute-start(bf16[2,8,1024]{2,1,0:T(8,128)(2,1)S(1)} %get-tuple-element.28), channel_id=1, source_target_pairs={{0,8},{1,9},{2,10},{3,11},{4,12},{5,13},{6,14},{7,15},{8,16},{9,17... | collective-permute-start | bytes 98312 | tf_op jit(solution)/shard_map/ppermute | solution.py:479
  119.5 7.5 %collective-permute-start.28 = (bf16[2,8,1024]{2,1,0:T(8,128)(2,1)S(1)}, bf16[2,8,1024]{2,1,0:T(8,128)(2,1)S(1)}, u32[]{:S(2)}, u32[]{:S(2)}) collective-permute-start(bf16[2,8,1024]{2,1,0:T(8,128)(2,1)S(1)} %get-tuple-element.29), channel_id=1, source_target_pairs={{0,10},{1,11},{2,12},{3,13},{4,14},{5,15},{6,8},{7,9},{8,18},{9,19... | collective-permute-start | bytes 98312 | tf_op jit(solution)/shard_map/ppermute | solution.py:479
  121.8 6.6 %collective-permute-start.29 = (bf16[2,8,1024]{2,1,0:T(8,128)(2,1)S(1)}, bf16[2,8,1024]{2,1,0:T(8,128)(2,1)S(1)}, u32[]{:S(2)}, u32[]{:S(2)}) collective-permute-start(bf16[2,8,1024]{2,1,0:T(8,128)(2,1)S(1)} %get-tuple-element.30), channel_id=1, source_target_pairs={{0,12},{1,13},{2,14},{3,15},{4,8},{5,9},{6,10},{7,11},{8,20},{9,21... | collective-permute-start | bytes 98312 | tf_op jit(solution)/shard_map/ppermute | solution.py:479
  124.3 5.7 %collective-permute-start.30 = (bf16[2,8,1024]{2,1,0:T(8,128)(2,1)S(1)}, bf16[2,8,1024]{2,1,0:T(8,128)(2,1)S(1)}, u32[]{:S(2)}, u32[]{:S(2)}) collective-permute-start(bf16[2,8,1024]{2,1,0:T(8,128)(2,1)S(1)} %get-tuple-element.27), channel_id=1, source_target_pairs={{0,14},{1,15},{2,8},{3,9},{4,10},{5,11},{6,12},{7,13},{8,22},{9,23... | collective-permute-start | bytes 98312 | tf_op jit(solution)/shard_map/ppermute | solution.py:479
  (12 other events, 57.8 us)

commit v2 on v1

--- a/solution.py
+++ b/solution.py
@@ -146,146 +146,175 @@
 
 
 CORES = 2
+TAIL = 16
 VMEM = pl.BlockSpec(memory_space=pltpu.VMEM)
 SMEM = pl.BlockSpec(memory_space=pltpu.SMEM)
 ANYWHERE = pl.BlockSpec(memory_space=pl.ANY)
+HBM = pl.BlockSpec(memory_space=pltpu.HBM)
 MIB = 1 << 20
 
 
 def to_pair(x, k):
     size = lax.axis_size("dev")
-    return lax.ppermute(x, "dev", [(d, (d + CORES * k) % size) for d in range(size)])
+    return lax.ppermute(x, "dev", [(d, d ^ (CORES * k)) for d in range(size)])
 
 
 def to_partner(x):
     return lax.ppermute(x, "dev", [(d, d ^ 1) for d in range(lax.axis_size("dev"))])
 
 
+def from_all(x):
+    arrived = [x] + [to_pair(x, k) for k in range(1, KV_HEADS)]
+    return [p for a in arrived for p in (a, to_partner(a))]
+
+
 def after(x, *others):
     return lax.optimization_barrier((x, *others))[0]
 
 
+def in_vmem(x):
+    return pltpu.with_memory_space_constraint(x, pltpu.VMEM)
+
+
 def matmul(a, b, dims=((1,), (0,))):
     return lax.dot_general(a, b, (dims, ((), ())), preferred_element_type=jnp.float32)
 
 
-def pack_kernel(place, cache, *rest):
-    outs, sems = rest[:-1], rest[-1]
-    pairs = len(outs)
-    width = cache.shape[3] // 2
+def load_kernel(count, *refs):
+    sources, targets, sems = refs[:count], refs[count : 2 * count], refs[2 * count]
     copies = []
-    for k in list(range(1, pairs)) + [0]:
-        head = lax.rem(place[0] + k, pairs)
-        for part in range(2):
-            columns = pl.ds(pl.multiple_of(part * width + head * HEAD_DIM, HEAD_DIM), HEAD_DIM)
-            copy = pltpu.make_async_copy(
-                cache.at[0, :, :, columns], outs[k].at[:, part], sems.at[k, part]
-            )
-            copy.start()
-            copies.append(copy)
+    for i in range(count):
+        parts = sems.shape[1]
+        depth = targets[i].shape[0] // parts
+        for j in range(parts):
+            rows = pl.ds(j * depth, depth)
+            source = sources[i].at[rows] if len(sources[i].shape) == 2 else sources[i].at[0, rows]
+            copies.append(pltpu.make_async_copy(source, targets[i].at[rows], sems.at[i, j]))
+    for copy in copies:
+        copy.start()
     for copy in copies:
         copy.wait()
 
 
-def pack(place, cache):
-    pairs = KV_HEADS
+def load(*arrays):
+    return pl.pallas_call(
+        functools.partial(load_kernel, len(arrays)),
+        out_shape=[pltpu.VMEM(a.shape[-2:], a.dtype) for a in arrays],
+        in_specs=[HBM] * len(arrays),
+        out_specs=[VMEM] * len(arrays),
+        scratch_shapes=[pltpu.SemaphoreType.DMA((len(arrays), 4))],
+        compiler_params=pltpu.CompilerParams(vmem_limit_bytes=2 * MIB),
+        cost_estimate=pl.CostEstimate(
+            flops=0, bytes_accessed=sum(a.size * 2 for a in arrays), transcendentals=0
+        ),
+        name="load",
+    )(*arrays)
+
+
+def pack_kernel(place, table, retrieved, counts, cache, *rest):
+    outs, (whole, sems) = rest[:-2], rest[-2:]
+    lines, tokens = whole.shape[0], whole.shape[1]
+    width = whole.shape[2] // 2
+    copies = [
+        pltpu.make_async_copy(cache.at[0, line], whole.at[line], sems.at[line]) for line in range(lines)
+    ]
+    for copy in copies:
+        copy.start()
+    listed = retrieved.shape[2]
+    lane = lax.broadcasted_iota(jnp.int32, (TAIL, HEAD_DIM), 1)
+    note = jnp.where(lane == listed, counts[0, 0], 0)
+    for k in range(listed):
+        note = jnp.where(lane == k, table[retrieved[0, 0, k]], note)
+    note = note.astype(jnp.float32).astype(jnp.bfloat16)
+    for out in outs:
+        out[lines * 2 * tokens :, :] = note
+    for line in range(lines):
+        copies[line].wait()
+        for k, out in enumerate(outs):
+            head = lax.bitwise_xor(place[0], k)
+            for part in range(2):
+                columns = pl.ds(pl.multiple_of(part * width + head * HEAD_DIM, HEAD_DIM), HEAD_DIM)
+                at = (line * 2 + part) * tokens
+                out[at : at + tokens, :] = whole[line, :, columns]
+
+
+def pack(place, table, retrieved, counts, cache):
     rows, tokens = cache.shape[1], cache.shape[2]
-    shape = jax.ShapeDtypeStruct((rows, 2, tokens, HEAD_DIM), cache.dtype)
     return pl.pallas_call(
         pack_kernel,
-        out_shape=[shape] * pairs,
-        in_specs=[SMEM, ANYWHERE],
-        out_specs=[ANYWHERE] * pairs,
-        scratch_shapes=[pltpu.SemaphoreType.DMA((pairs, 2))],
+        out_shape=[pltpu.VMEM((rows * 2 * tokens + TAIL, HEAD_DIM), cache.dtype)] * KV_HEADS,
+        in_specs=[SMEM] * 4 + [ANYWHERE],
+        out_specs=[VMEM] * KV_HEADS,
+        scratch_shapes=[
+            pltpu.VMEM(cache.shape[1:], cache.dtype),
+            pltpu.SemaphoreType.DMA((rows,)),
+        ],
+        compiler_params=pltpu.CompilerParams(vmem_limit_bytes=6 * MIB),
         cost_estimate=pl.CostEstimate(flops=0, bytes_accessed=2 * cache.size * 2, transcendentals=0),
         name="pack",
-    )(place, cache)
+    )(place, table, retrieved, counts, cache)
 
 
 def project_kernel(place, *refs):
     count = 2 * KV_HEADS
     parts, rest = refs[:count], refs[count:]
-    gain, wq, wk, wv, q_out, kv_out, cols_out, normed, wq_vm, wk_vm, wv_vm, sems = rest
-    chunks = sems.shape[0] - 2
-    depth = wq.shape[1] // chunks
+    gain, wq, wk, wv, q_out, kv_out, cols_out, normed = rest
     pair, core = place[0], place[1]
-    copies = [
-        pltpu.make_async_copy(wk, wk_vm, sems.at[chunks]),
-        pltpu.make_async_copy(wv, wv_vm, sems.at[chunks + 1]),
-    ]
-    for i in range(chunks):
-        rows = pl.ds(i * depth, depth)
-        copies.append(pltpu.make_async_copy(wq.at[0, rows], wq_vm.at[rows], sems.at[i]))
-    for copy in copies:
-        copy.start()
     first = core == 0
-    columns = pl.ds(pl.multiple_of((CORES * pair + core) * cols_out.shape[1], 128), cols_out.shape[1])
+    width = cols_out.shape[1]
+    columns = pl.ds(pl.multiple_of((CORES * pair + core) * width, 128), width)
     for k in range(KV_HEADS):
-        source = lax.rem(pair + KV_HEADS - k, KV_HEADS)
+        source = lax.bitwise_xor(pair, k)
         rows = pl.ds(pl.multiple_of(source * 16, 16), 16)
-        mine, other = parts[2 * k], parts[2 * k + 1]
 
         def both(at):
-            a, b = mine[:, at].astype(jnp.float32), other[:, at].astype(jnp.float32)
+            a, b = (parts[2 * k + p][:, at].astype(jnp.float32) for p in range(CORES))
             return jnp.concatenate([jnp.where(first, a, b), jnp.where(first, b, a)], axis=0)
 
         state = both(slice(None))
         inverse = lax.rsqrt(jnp.mean(state * state, axis=-1, keepdims=True) + norm_eps)
         normed[rows, :] = (state * inverse * gain[...]).astype(jnp.bfloat16)
         cols_out[rows, :] = both(columns).astype(cols_out.dtype)
-    copies[0].wait()
-    key = matmul(normed[...], wk_vm[...], ((1,), (1,)))
-    copies[1].wait()
-    value = matmul(normed[...], wv_vm[...], ((1,), (1,)))
+    key = matmul(normed[...], wk[...], ((1,), (1,)))
+    value = matmul(normed[...], wv[...], ((1,), (1,)))
     kv_out[...] = jnp.concatenate([key, value], axis=1).astype(kv_out.dtype)
-    total = jnp.zeros(q_out.shape, jnp.float32)
-    for i in range(chunks):
-        at = slice(i * depth, (i + 1) * depth)
-        copies[2 + i].wait()
-        total = total + matmul(normed[:, at], wq_vm[at, :])
-    q_out[...] = total.astype(q_out.dtype)
+    q_out[...] = matmul(normed[...], wq[...]).astype(q_out.dtype)
 
 
 def project(place, parts, gain, wq, wk, wv):
     tokens = sum(p.shape[0] for p in parts)
     width = parts[0].shape[1]
-    chunks = 8
     bf16 = jnp.bfloat16
     return pl.pallas_call(
         project_kernel,
         out_shape=[
-            jax.ShapeDtypeStruct((tokens, wq.shape[2]), bf16),
-            jax.ShapeDtypeStruct((tokens, 2 * wk.shape[0]), bf16),
-            jax.ShapeDtypeStruct((tokens, width // len(parts)), bf16),
+            pltpu.VMEM((tokens, wq.shape[1]), bf16),
+            pltpu.VMEM((tokens, 2 * wk.shape[0]), bf16),
+            pltpu.VMEM((tokens, width // len(parts)), bf16),
         ],
-        in_specs=[SMEM] + [VMEM] * (len(parts) + 1) + [ANYWHERE] * 3,
+        in_specs=[SMEM] + [VMEM] * (len(parts) + 4),
         out_specs=[VMEM] * 3,
-        scratch_shapes=[
-            pltpu.VMEM((tokens, width), bf16),
-            pltpu.VMEM(wq.shape[1:], bf16),
-            pltpu.VMEM(wk.shape, bf16),
-            pltpu.VMEM(wv.shape, bf16),
-            pltpu.SemaphoreType.DMA((chunks + 2,)),
-        ],
-        compiler_params=pltpu.CompilerParams(vmem_limit_bytes=28 * MIB),
+        scratch_shapes=[pltpu.VMEM((tokens, width), bf16)],
+        compiler_params=pltpu.CompilerParams(vmem_limit_bytes=16 * MIB),
         cost_estimate=pl.CostEstimate(
             flops=2 * tokens * width * 640, bytes_accessed=2 * width * 640, transcendentals=0
         ),
         name="project",
-    )(place, *parts, gain, wq, wk, wv)
-
-
-def attend_kernel(place, table, meta, q, kv_mine, kv_other, *refs):
+    )(place, *[in_vmem(p) for p in parts], gain, in_vmem(wq), in_vmem(wk), in_vmem(wv))
+
+
+def attend_kernel(place, q, kv_mine, kv_other, *refs):
     count = 2 * KV_HEADS
-    held, (out, blocks, placed, sems) = refs[:count], refs[count:]
-    requests = meta.shape[0]
-    listed = meta.shape[1] - 1
+    held, (out, blocks, placed, scored, notes, meta, sems, note_sem) = refs[:count], refs[count:]
+    requests, listed = scored.shape[:2]
     tokens = q.shape[0]
     question = tokens // requests
     heads = q.shape[1] // HEAD_DIM
     group = heads * question
-    rows = held[0].shape[0]
+    block = scored.shape[3]
+    rows = (blocks.shape[1] - TAIL) // (2 * block)
     pair, core = place[0], place[1]
+    me = CORES * pair + core
     copies = [pltpu.make_async_copy(held[i], blocks.at[i], sems.at[i]) for i in range(count)]
     for copy in copies:
         copy.start()
@@ -306,6 +335,14 @@
             ).astype(jnp.bfloat16)
         )
     stacked = jnp.concatenate(queries, axis=0)
+    for copy in copies:
+        copy.wait()
+    tail = slice(rows * 2 * block, rows * 2 * block + TAIL)
+    notes[...] = jnp.concatenate(
+        [blocks[i, tail, :].astype(jnp.float32)[:1] for i in range(count)], axis=0
+    ).astype(jnp.int32)
+    noted = pltpu.make_async_copy(notes, meta, note_sem)
+    noted.start()
     scores = matmul(stacked, own_key, ((1,), (1,))) * scale
     row = lax.broadcasted_iota(jnp.int32, scores.shape, 0)
     column = lax.broadcasted_iota(jnp.int32, scores.shape, 1)
@@ -314,34 +351,40 @@
     weights = jnp.where(seen, jnp.exp(scores - own_top), 0.0)
     own_total = jnp.sum(weights, axis=-1, keepdims=True)
     own_acc = matmul(weights.astype(jnp.bfloat16), own_value)
-    for copy in copies:
-        copy.wait()
+    noted.wait()
+    lives, places = [], []
     for r in range(requests):
-        away = lax.rem(pair - r // CORES + KV_HEADS, KV_HEADS)
-        at = CORES * away + lax.rem(r + core, CORES)
-        live = meta[at, listed]
+        at = lax.bitwise_xor(me, r)
+        lives.append(meta[at, listed])
+        for k in range(listed):
+            slot = meta[at, k]
+            source = lax.bitwise_xor(me, slot // rows)
+            key_at = pl.multiple_of(lax.rem(slot, rows) * 2 * block, block)
+            places.append((source, key_at))
+            scored[r, k] = matmul(queries[r], blocks[source, pl.ds(key_at, block), :], ((1,), (1,))) * scale
+    scores = scored[...]
+    tops = jnp.max(scores, axis=-1, keepdims=True)
+    weights = jnp.exp(scores - tops)
+    totals = jnp.sum(weights, axis=-1, keepdims=True)
+    scored[...] = weights
+    for r in range(requests):
         mine = slice(r * group, (r + 1) * group)
-        tops, totals, accs = [], [], []
+        live = lives[r]
+        accs, marks = [], []
         for k in range(listed):
-            slot = table[meta[at, k]]
-            owner, line = slot // rows, lax.rem(slot, rows)
-            source = CORES * lax.rem(pair - owner // CORES + KV_HEADS, KV_HEADS) + lax.rem(owner + core, CORES)
-            part = matmul(queries[r], blocks[source, line, 0], ((1,), (1,))) * scale
-            top = jnp.max(part, axis=-1, keepdims=True)
-            weights = jnp.exp(part - top)
-            total = jnp.sum(weights, axis=-1, keepdims=True)
-            accs.append(matmul(weights.astype(jnp.bfloat16), blocks[source, line, 1]))
-            tops.append(jnp.where(k < live, top, far_below))
-            totals.append(total)
+            source, key_at = places[r * listed + k]
+            values = blocks[source, pl.ds(key_at + block, block), :]
+            accs.append(matmul(scored[r, k].astype(jnp.bfloat16), values))
+            marks.append(jnp.where(k < live, tops[r, k], far_below))
         peak = own_top[mine]
-        for top in tops:
-            peak = jnp.maximum(peak, top)
+        for mark in marks:
+            peak = jnp.maximum(peak, mark)
         factor = jnp.exp(own_top[mine] - peak)
         numerator, denominator = own_acc[mine] * factor, own_total[mine] * factor
         for k in range(listed):
-            factor = jnp.where(k < live, jnp.exp(tops[k] - peak), 0.0)
+            factor = jnp.where(k < live, jnp.exp(marks[k] - peak), 0.0)
             numerator = numerator + accs[k] * factor
-            denominator = denominator + totals[k] * factor
+            denominator = denominator + totals[r, k] * factor
         context = numerator / denominator
         for h in range(heads):
             placed[r * question : (r + 1) * question, h * HEAD_DIM : (h + 1) * HEAD_DIM] = context[
@@ -350,41 +393,42 @@
     out[...] = placed[...].astype(out.dtype)
 
 
-def attend(place, table, meta, q, kv_mine, kv_other, held):
+def attend(place, q, kv_mine, kv_other, held, requests, listed, block):
+    count = len(held)
     return pl.pallas_call(
         attend_kernel,
-        out_shape=jax.ShapeDtypeStruct(q.shape, jnp.bfloat16),
-        in_specs=[SMEM] * 3 + [VMEM] * 3 + [ANYWHERE] * len(held),
+        out_shape=pltpu.VMEM(q.shape, jnp.bfloat16),
+        in_specs=[SMEM] + [VMEM] * 3 + [ANYWHERE] * count,
         out_specs=VMEM,
         scratch_shapes=[
-            pltpu.VMEM((len(held), *held[0].shape), jnp.bfloat16),
+            pltpu.VMEM((count, *held[0].shape), jnp.bfloat16),
             pltpu.VMEM(q.shape, jnp.float32),
-            pltpu.SemaphoreType.DMA((len(held),)),
+            pltpu.VMEM((requests, listed, q.size // HEAD_DIM // requests, block), jnp.float32),
+            pltpu.VMEM((count, HEAD_DIM), jnp.int32),
+            pltpu.SMEM((count, HEAD_DIM), jnp.int32),
+            pltpu.SemaphoreType.DMA((count,)),
+            pltpu.SemaphoreType.DMA,
         ],
         compiler_params=pltpu.CompilerParams(vmem_limit_bytes=16 * MIB),
         cost_estimate=pl.CostEstimate(
             flops=1 << 28, bytes_accessed=2 * MIB, transcendentals=1 << 18
         ),
         name="attend",
-    )(place, table, meta, q, kv_mine, kv_other, *held)
+    )(place, in_vmem(q), in_vmem(kv_mine), in_vmem(kv_other), *held)
 
 
 def finish_kernel(place, *refs):
     count = 2 * KV_HEADS
-    parts, (cols, w_out, keep, give, w_vm, placed, sems) = refs[:count], refs[count:]
+    parts, (cols, w_out, keep, give, placed) = refs[:count], refs[count:]
     pair, core = place[0], place[1]
+    me = CORES * pair + core
     depth = parts[0].shape[1]
-    copies, spans = [], []
+    total = None
     for i in range(count):
-        source = CORES * lax.rem(pair - i // CORES + KV_HEADS, KV_HEADS) + lax.rem(i + core, CORES)
+        source = lax.bitwise_xor(me, i)
         span = pl.ds(pl.multiple_of(source * depth, depth), depth)
-        copy = pltpu.make_async_copy(w_out.at[0, span], w_vm.at[i], sems.at[i])
-        copy.start()
-        copies.append(copy)
-    total = cols[...].astype(jnp.float32) * 0.0
-    for i in range(count):
-        copies[i].wait()
-        total = total + matmul(parts[i][...], w_vm[i])
+        product = matmul(parts[i][...], w_out[span, :])
+        total = product if total is None else total + product
     placed[...] = cols[...].astype(jnp.float32) + total
     question = keep.shape[1]
     for z in range(KV_HEADS):
@@ -397,32 +441,47 @@
 def finish(place, parts, cols, w_out):
     count = len(parts)
     tokens, width = cols.shape
-    shape = jax.ShapeDtypeStruct((KV_HEADS, tokens // count, width), jnp.bfloat16)
+    shape = pltpu.VMEM((KV_HEADS, tokens // count, width), jnp.bfloat16)
     return pl.pallas_call(
         finish_kernel,
         out_shape=[shape] * 2,
-        in_specs=[SMEM] + [VMEM] * (count + 1) + [ANYWHERE],
+        in_specs=[SMEM] + [VMEM] * (count + 2),
         out_specs=[VMEM] * 2,
-        scratch_shapes=[
-            pltpu.VMEM((count, parts[0].shape[1], width), jnp.bfloat16),
-            pltpu.VMEM((tokens, width), jnp.float32),
-            pltpu.SemaphoreType.DMA((count,)),
-        ],
-        compiler_params=pltpu.CompilerParams(vmem_limit_bytes=24 * MIB),
+        scratch_shapes=[pltpu.VMEM((tokens, width), jnp.float32)],
+        compiler_params=pltpu.CompilerParams(vmem_limit_bytes=16 * MIB),
         cost_estimate=pl.CostEstimate(
             flops=2 * tokens * w_out.size, bytes_accessed=2 * w_out.size, transcendentals=0
         ),
         name="finish",
-    )(place, *parts, cols, w_out)
+    )(place, *[in_vmem(p) for p in parts], in_vmem(cols), in_vmem(w_out))
+
+
+def route_kernel(place, keep, got, *outs):
+    for k, out in enumerate(outs):
+        target = lax.bitwise_xor(place[0], k)
+        out[0] = keep[target]
+        out[1] = got[target]
+
+
+def route_pieces(place, keep, got):
+    shape = pltpu.VMEM((CORES, *keep.shape[1:]), keep.dtype)
+    return pl.pallas_call(
+        route_kernel,
+        out_shape=[shape] * KV_HEADS,
+        in_specs=[SMEM] + [VMEM] * 2,
+        out_specs=[VMEM] * KV_HEADS,
+        compiler_params=pltpu.CompilerParams(vmem_limit_bytes=4 * MIB),
+        name="route",
+    )(place, in_vmem(keep), in_vmem(got))
 
 
 def place_kernel(place, *refs):
     parts, out = refs[:-1], refs[-1]
-    pair, core = place[0], place[1]
+    me = CORES * place[0] + place[1]
     width = parts[0].shape[2]
     for k, part in enumerate(parts):
         for p in range(CORES):
-            source = CORES * lax.rem(pair - k + KV_HEADS, KV_HEADS) + lax.rem(core + p, CORES)
+            source = lax.bitwise_xor(me, CORES * k + p)
             out[0, :, pl.ds(pl.multiple_of(source * width, width), width)] = part[p]
 
 
@@ -433,46 +492,39 @@
         out_shape=jax.ShapeDtypeStruct((1, rows, width * cores * len(parts)), jnp.bfloat16),
         in_specs=[SMEM] + [VMEM] * len(parts),
         out_specs=VMEM,
+        compiler_params=pltpu.CompilerParams(vmem_limit_bytes=4 * MIB),
         name="place",
-    )(place, *parts)
+    )(place, *[in_vmem(p) for p in parts])
 
 
 def by_head(hidden, gain, w_query, w_key, w_value, w_out, cache, block_slot, retrieved, counts):
     size, sections = lax.axis_size("dev"), lax.axis_size("segment")
     me = lax.axis_index("dev")
-    pair, core = me // CORES, me % CORES
-    place = jnp.stack([pair, core]).astype(jnp.int32)
+    place = jnp.stack([me // CORES, me % CORES]).astype(jnp.int32)
 
     state = hidden[0]
     arrived = [state] + [to_pair(state, k) for k in range(1, KV_HEADS)]
+    packed = pack(place, block_slot, retrieved, counts, cache)
+    wq, wk, wv = load(w_query, w_key[0].swapaxes(0, 1), w_value[0].swapaxes(0, 1))
+    arrived = [arrived[0]] + [after(a, wq) for a in arrived[1:]]
     parts = [p for a in arrived for p in (a, to_partner(a))]
 
-    packed = pack(place, cache)
     held = [packed[0]]
     for k in range(1, KV_HEADS):
-        mine = packed[k] if k == 1 else after(packed[k], arrived[3])
+        mine = packed[k] if k < 3 else after(packed[k], arrived[1])
         held.append(to_pair(mine, k))
     held = [h for a in held for h in (a, to_partner(a))]
 
-    entry = jnp.concatenate([retrieved[0], counts], axis=1)
-    entries = [entry] + [to_pair(entry, k) for k in range(1, KV_HEADS)]
-    stacked = jnp.concatenate(entries, axis=0)
-    both = jnp.stack([stacked, to_partner(stacked)], axis=1)
-    meta = both.reshape(size, entry.shape[1])
-
-    q, kv, cols = project(
-        place, parts, gain, w_query, w_key[0].swapaxes(0, 1), w_value[0].swapaxes(0, 1)
-    )
-    context = attend(place, block_slot, meta, q, kv, to_partner(kv), held)
-    contexts = [context] + [to_pair(context, k) for k in range(1, KV_HEADS)]
-    contexts = [p for a in contexts for p in (a, to_partner(a))]
-    keep, give = finish(place, contexts, cols, w_out)
-    sent = jnp.stack([keep, to_partner(give)], axis=1)
+    q, kv, cols = project(place, parts, gain, wq, wk, wv)
+    context = attend(
+        place, q, kv, to_partner(kv), held, size, retrieved.shape[2], cache.shape[2]
+    )
+    keep, give = finish(place, from_all(context), cols, w_out[0])
+    pieces = route_pieces(place, keep, to_partner(give))
     final = []
-    for k in range(KV_HEADS):
-        piece = lax.dynamic_index_in_dim(sent, (pair + k) % KV_HEADS, 0, keepdims=False)
+    for k, piece in enumerate(pieces):
         route = [
-            (s * size + d, (s + 1) % sections * size + (d + CORES * k) % size)
+            (s * size + d, (s + 1) % sections * size + (d ^ (CORES * k)))
             for s in range(sections)
             for d in range(size)
         ]

time: 133 us -> 87.3 us (0.66)
  Pallas kernels: 55.8 us -> 12.5 us
  waiting for transfers between devices: 33 us -> 39.2 us
  starting transfers between devices: 31 us -> 26.1 us
  other arithmetic: 2.8 us -> 0.08 us
    pallas_call x3 -> x5, Pallas kernels: 51.4 us -> 9.16 us  [the longest x1 3.58 us: project(): pl.pallas_call(project_kernel, out_shape=[pltpu.VMEM((tokens, wq.shape[1]...]
    ppermute x12 -> x9, starting transfers between devices: 20.9 us -> 15.1 us  [to_pair(): return lax.ppermute(x, 'dev', [(d, d ^ CORES * k) for d in range(size)])]
    ppermute x12 -> x9, waiting for transfers between devices: 25 us -> 27.8 us  [to_pair(): return lax.ppermute(x, 'dev', [(d, d ^ CORES * k) for d in range(size)])]
    ppermute x15 -> x14, waiting for transfers between devices: 3.26 us -> 5.37 us  [to_partner(): lax.ppermute(x, 'dev', [(d, d ^ 1) for d in range(lax.axis_size('dev'))])]
    concatenate x2 -> x0, other arithmetic: 1.46 us -> none  [the longest x1 0.73 us: by_head(): stacked = jnp.concatenate(entries, axis=0)]
    ppermute x15 -> x14, starting transfers between devices: 2.82 us -> 3.33 us  [to_partner(): lax.ppermute(x, 'dev', [(d, d ^ 1) for d in range(lax.axis_size('dev'))])]
    unnamed x26 -> x20, local copies, waits for them, and re-layouts: 8.71 us -> 8.38 us
  transfers between devices with their start and end apart: 31 -> 27, of which waited for: 14 -> 10; matrix products, arithmetic and copies ran while one was open for 2% -> 0% of each run, Pallas kernels for 29% -> 6%
where the time goes in v2:
time: 87.3 us; the launch traced here: 87 us
  waiting for transfers between devices  39.2 us (45%)
  starting transfers between devices  26.1 us (30%)
  Pallas kernels  12.5 us (14%)
  local copies, waits for them, and re-layouts  8.38 us (10%)
    ppermute x9, waiting for transfers between devices, to_pair(): return lax.ppermute(x, 'dev', [(d, d ^ CORES * k) for d in range(size)])  27.8 us
    ppermute x9, starting transfers between devices, to_pair(): return lax.ppermute(x, 'dev', [(d, d ^ CORES * k) for d in range(size)])  15.1 us
    unnamed x20, local copies, waits for them, and re-layouts  8.38 us
    ppermute x4, starting transfers between devices, by_head(): final.append(lax.ppermute(piece, ('segment', 'dev'), route))  7.7 us
    ppermute x4, waiting for transfers between devices, by_head(): final.append(lax.ppermute(piece, ('segment', 'dev'), route))  6.05 us
    ppermute x14, waiting for transfers between devices, to_partner(): lax.ppermute(x, 'dev', [(d, d ^ 1) for d in range(lax.axis_size('dev'))])  5.37 us
    pallas_call x1, Pallas kernels, project(): pl.pallas_call(project_kernel, out_shape=[pltpu.VMEM((tokens, wq.shape[1]...  3.58 us
    ppermute x14, starting transfers between devices, to_partner(): lax.ppermute(x, 'dev', [(d, d ^ 1) for d in range(lax.axis_size('dev'))])  3.33 us
  transfers between devices with their start and end apart: 27, of which 10 were waited for; matrix products, arithmetic and copies ran while one was open for 0% of the time, Pallas kernels for 6%

profile of v2, /device:TPU:0, one launch (start us, length us, event | category | flops | bytes accessed | tf_op | source)
XLA Modules:
  0.0 87.0 jit_solution(12390476400492317936)
XLA Ops:
  0.0 3.0 %collective-permute-start.1 = (bf16[8,8192]{1,0:T(8,128)(2,1)}, bf16[8,8192]{1,0:T(8,128)(2,1)S(1)}, u32[]{:S(2)}, u32[]{:S(2)}) collective-permute-start(bf16[8,8192]{1,0:T(8,128)(2,1)} %bitcast.15), channel_id=1, source_target_pairs={{0,2},{1,3},{2,0},{3,1},{4,6},{5,7},{6,4},{7,5},{8,10},{9,11},{10,... | collective-permute-start | bytes 393224 | tf_op jit(solution)/shard_map/ppermute | solution.py:159
  3.8 1.2 %copy-done.3 = bf16[1,4,128,1024]{3,2,1,0:T(8,128)(2,1)S(1)} copy-done((bf16[1,4,128,1024]{3,2,1,0:T(8,128)(2,1)S(1)}, bf16[1,4,128,1024]{3,2,1,0:T(8,128)(2,1)}, u32[]{:S(2)}) %copy-start.3) | copy-done | bytes 1048600
  5.0 0.7 copy-done.6
  6.3 1.0 %pack.1 = (bf16[1040,128]{1,0:T(8,128)(2,1)S(1)}, bf16[1040,128]{1,0:T(8,128)(2,1)S(1)}, bf16[1040,128]{1,0:T(8,128)(2,1)S(1)}, bf16[1040,128]{1,0:T(8,128)(2,1)S(1)}) custom-call(s32[2]{0:T(128)S(1)} %pad_add_fusion.place, s32[32]{0:T(128)S(1)} %copy-done.6, s32[1,1,6]{2,1,0:T(1,128)S(1)} %copy-done.7, s32[1,1]{1,0:T(1,128)S(6)} %copy.11.counts, ...), custom_call_target="tpu_custom_call" | custom-call | bytes 2097152 | tf_op jit(solution)/shard_map/pack/pallas_call | solution.py:243
  7.4 3.0 %collective-permute-start.11 = (bf16[1040,128]{1,0:T(8,128)(2,1)S(1)}, bf16[1040,128]{1,0:T(8,128)(2,1)S(1)}, u32[]{:S(2)}, u32[]{:S(2)}) collective-permute-start(bf16[1040,128]{1,0:T(8,128)(2,1)S(1)} %get-tuple-element.35), channel_id=1, source_target_pairs={{0,4},{1,5},{2,6},{3,7},{4,0},{5,1},{6,2},{7,3},{8,12},{9,13},{10,... | collective-permute-start | bytes 798728 | tf_op jit(solution)/shard_map/ppermute | solution.py:159
  10.4 3.4 %copy-done = bf16[1,8192,512]{2,1,0:T(8,128)(2,1)S(1)} copy-done((bf16[1,8192,512]{2,1,0:T(8,128)(2,1)S(1)}, bf16[1,8192,512]{2,1,0:T(8,128)(2,1)}, u32[]{:S(2)}) %copy-start) | copy-done | bytes 8388632
  13.8 1.2 %copy-done.1 = bf16[1,8192,64]{1,2,0:T(8,128)(2,1)S(1)} copy-done((bf16[1,8192,64]{1,2,0:T(8,128)(2,1)S(1)}, bf16[1,8192,64]{1,2,0:T(8,128)(2,1)}, u32[]{:S(2)}) %copy-start.1) | copy-done | bytes 1048600
  15.0 1.2 %copy-done.2 = bf16[1,8192,64]{1,2,0:T(8,128)(2,1)S(1)} copy-done((bf16[1,8192,64]{1,2,0:T(8,128)(2,1)S(1)}, bf16[1,8192,64]{1,2,0:T(8,128)(2,1)}, u32[]{:S(2)}) %copy-start.2) | copy-done | bytes 1048600
  16.2 0.8 load.1
  17.1 1.4 %collective-permute-start.13 = (bf16[1040,128]{1,0:T(8,128)(2,1)S(1)}, bf16[1040,128]{1,0:T(8,128)(2,1)S(1)}, u32[]{:S(2)}, u32[]{:S(2)}) collective-permute-start(bf16[1040,128]{1,0:T(8,128)(2,1)S(1)} %get-tuple-element.37), channel_id=1, source_target_pairs={{0,6},{1,7},{2,4},{3,5},{4,2},{5,3},{6,0},{7,1},{8,14},{9,15},{10,... | collective-permute-start | bytes 798728 | tf_op jit(solution)/shard_map/ppermute | solution.py:159
  18.5 1.7 %collective-permute-start.3 = (bf16[8,8192]{1,0:T(8,128)(2,1)S(1)}, bf16[8,8192]{1,0:T(8,128)(2,1)S(1)}, u32[]{:S(2)}, u32[]{:S(2)}) collective-permute-start(bf16[8,8192]{1,0:T(8,128)(2,1)S(1)} %bitcast.17), channel_id=1, source_target_pairs={{0,4},{1,5},{2,6},{3,7},{4,0},{5,1},{6,2},{7,3},{8,12},{9,13},{10,... | collective-permute-start | bytes 393224 | tf_op jit(solution)/shard_map/ppermute | solution.py:159
  20.2 1.0 %collective-permute-start.5 = (bf16[8,8192]{1,0:T(8,128)(2,1)S(1)}, bf16[8,8192]{1,0:T(8,128)(2,1)S(1)}, u32[]{:S(2)}, u32[]{:S(2)}) collective-permute-start(bf16[8,8192]{1,0:T(8,128)(2,1)S(1)} %bitcast.18), channel_id=1, source_target_pairs={{0,6},{1,7},{2,4},{3,5},{4,2},{5,3},{6,0},{7,1},{8,14},{9,15},{10,... | collective-permute-start | bytes 393224 | tf_op jit(solution)/shard_map/ppermute | solution.py:159
  21.2 22.6 %collective-permute-done.3.refs_4_ = bf16[8,8192]{1,0:T(8,128)(2,1)S(1)} collective-permute-done((bf16[8,8192]{1,0:T(8,128)(2,1)S(1)}, bf16[8,8192]{1,0:T(8,128)(2,1)S(1)}, u32[]{:S(2)}, u32[]{:S(2)}) %collective-permute-start.3) | collective-permute-done | bytes 131104 | tf_op jit(solution)/shard_map/ppermute | solution.py:159
  44.3 0.8 collective-permute-done.2.refs_3_
  46.3 1.7 %collective-permute-done.6.refs_7_ = bf16[8,8192]{1,0:T(8,128)(2,1)S(1)} collective-permute-done((bf16[8,8192]{1,0:T(8,128)(2,1)S(1)}, bf16[8,8192]{1,0:T(8,128)(2,1)S(1)}, u32[]{:S(2)}, u32[]{:S(2)}) %collective-permute-start.6) | collective-permute-done | bytes 131104 | tf_op jit(solution)/shard_map/ppermute | solution.py:163
  48.0 3.6 %project.1 = (bf16[64,512]{1,0:T(8,128)(2,1)S(1)}, bf16[64,128]{1,0:T(8,128)(2,1)S(1)}, bf16[64,1024]{1,0:T(8,128)(2,1)S(1)}) custom-call(s32[2]{0:T(128)S(1)} %pad_add_fusion.place, bf16[8,8192]{1,0:T(8,128)(2,1)S(1)} %bitcast.19, bf16[8,8192]{1,0:T(8,128)(2,1)S(1)} %collective-permute-done.refs_1_, bf16[8,8192]{1,0:T(8,128)(2,1)S(1)} %collective-permute-done.1.refs_2_, ...), custom_call_target="tpu_custom_call" | custom-call | flops 671088640 | bytes 10485760 | tf_op jit(solution)/shard_map/project/pallas_call | solution.py:288
  51.8 1.0 %collective-permute-done.7.kv_other = bf16[64,128]{1,0:T(8,128)(2,1)S(1)} collective-permute-done((bf16[64,128]{1,0:T(8,128)(2,1)S(1)}, bf16[64,128]{1,0:T(8,128)(2,1)S(1)}, u32[]{:S(2)}, u32[]{:S(2)}) %collective-permute-start.7) | collective-permute-done | bytes 16416 | tf_op jit(solution)/shard_map/ppermute | solution.py:163
  52.9 3.2 %attend.1.refs_0_ = bf16[64,512]{1,0:T(8,128)(2,1)S(1)} custom-call(s32[2]{0:T(128)S(1)} %pad_add_fusion.place, bf16[64,512]{1,0:T(8,128)(2,1)S(1)} %get-tuple-element.31.q, bf16[64,128]{1,0:T(8,128)(2,1)S(1)} %get-tuple-element.32.kv_mine, bf16[64,128]{1,0:T(8,128)(2,1)S(1)} %collective-permute-done.7.kv_other, ...), custom_call_target="tpu_custom_call" | custom-call | flops 268435456 | bytes 2097152 | tf_op jit(solution)/shard_map/attend/pallas_call | solution.py:398
  56.1 2.2 %collective-permute-start.16 = (bf16[64,512]{1,0:T(8,128)(2,1)S(1)}, bf16[64,512]{1,0:T(8,128)(2,1)S(1)}, u32[]{:S(2)}, u32[]{:S(2)}) collective-permute-start(bf16[64,512]{1,0:T(8,128)(2,1)S(1)} %attend.1.refs_0_), channel_id=1, source_target_pairs={{0,2},{1,3},{2,0},{3,1},{4,6},{5,7},{6,4},{7,5},{8,10},{9,11},{10,... | collective-permute-start | bytes 196616 | tf_op jit(solution)/shard_map/ppermute | solution.py:159
  58.3 1.7 %collective-permute-start.18 = (bf16[64,512]{1,0:T(8,128)(2,1)S(1)}, bf16[64,512]{1,0:T(8,128)(2,1)S(1)}, u32[]{:S(2)}, u32[]{:S(2)}) collective-permute-start(bf16[64,512]{1,0:T(8,128)(2,1)S(1)} %attend.1.refs_0_), channel_id=1, source_target_pairs={{0,4},{1,5},{2,6},{3,7},{4,0},{5,1},{6,2},{7,3},{8,12},{9,13},{10,... | collective-permute-start | bytes 196616 | tf_op jit(solution)/shard_map/ppermute | solution.py:159
  60.0 1.0 %collective-permute-start.20 = (bf16[64,512]{1,0:T(8,128)(2,1)S(1)}, bf16[64,512]{1,0:T(8,128)(2,1)S(1)}, u32[]{:S(2)}, u32[]{:S(2)}) collective-permute-start(bf16[64,512]{1,0:T(8,128)(2,1)S(1)} %attend.1.refs_0_), channel_id=1, source_target_pairs={{0,6},{1,7},{2,4},{3,5},{4,2},{5,3},{6,0},{7,1},{8,14},{9,15},{10,... | collective-permute-start | bytes 196616 | tf_op jit(solution)/shard_map/ppermute | solution.py:159
  61.5 5.1 %collective-permute-done.18.refs_4_ = bf16[64,512]{1,0:T(8,128)(2,1)S(1)} collective-permute-done((bf16[64,512]{1,0:T(8,128)(2,1)S(1)}, bf16[64,512]{1,0:T(8,128)(2,1)S(1)}, u32[]{:S(2)}, u32[]{:S(2)}) %collective-permute-start.18) | collective-permute-done | bytes 65568 | tf_op jit(solution)/shard_map/ppermute | solution.py:159
  67.2 0.7 collective-permute-done.19.refs_5_
  68.1 2.1 %finish.1 = (bf16[4,8,1024]{2,1,0:T(8,128)(2,1)S(1)}, bf16[4,8,1024]{2,1,0:T(8,128)(2,1)S(1)}) custom-call(s32[2]{0:T(128)S(1)} %pad_add_fusion.place, bf16[64,512]{1,0:T(8,128)(2,1)S(1)} %attend.1.refs_0_, bf16[64,512]{1,0:T(8,128)(2,1)S(1)} %collective-permute-done.15.refs_1_, bf16[64,512]{1,0:T(8,128)(2,1)S(1)} %collective-permute-done.16.refs_2_, ...), custom_call_target="tpu_custom_call" | custom-call | flops 536870912 | bytes 8388608 | tf_op jit(solution)/shard_map/finish/pallas_call | solution.py:445
  70.6 0.9 %collective-permute-done.22.got = bf16[4,8,1024]{2,1,0:T(8,128)(2,1)S(1)} collective-permute-done((bf16[4,8,1024]{2,1,0:T(8,128)(2,1)S(1)}, bf16[4,8,1024]{2,1,0:T(8,128)(2,1)S(1)}, u32[]{:S(2)}, u32[]{:S(2)}) %collective-permute-start.22) | collective-permute-done | bytes 65568 | tf_op jit(solution)/shard_map/ppermute | solution.py:163
  72.1 1.5 %collective-permute-start.23 = (bf16[2,8,1024]{2,1,0:T(8,128)(2,1)S(1)}, bf16[2,8,1024]{2,1,0:T(8,128)(2,1)S(1)}, u32[]{:S(2)}, u32[]{:S(2)}) collective-permute-start(bf16[2,8,1024]{2,1,0:T(8,128)(2,1)S(1)} %get-tuple-element.41), channel_id=1, source_target_pairs={{0,8},{1,9},{2,10},{3,11},{4,12},{5,13},{6,14},{7,15},{8,16},{9,17... | collective-permute-start | bytes 98312 | tf_op jit(solution)/shard_map/ppermute | solution.py:531
  73.6 2.3 %collective-permute-start.24 = (bf16[2,8,1024]{2,1,0:T(8,128)(2,1)S(1)}, bf16[2,8,1024]{2,1,0:T(8,128)(2,1)S(1)}, u32[]{:S(2)}, u32[]{:S(2)}) collective-permute-start(bf16[2,8,1024]{2,1,0:T(8,128)(2,1)S(1)} %get-tuple-element.42), channel_id=1, source_target_pairs={{0,10},{1,11},{2,8},{3,9},{4,14},{5,15},{6,12},{7,13},{8,18},{9,19... | collective-permute-start | bytes 98312 | tf_op jit(solution)/shard_map/ppermute | solution.py:531
  75.9 2.4 %collective-permute-start.25 = (bf16[2,8,1024]{2,1,0:T(8,128)(2,1)S(1)}, bf16[2,8,1024]{2,1,0:T(8,128)(2,1)S(1)}, u32[]{:S(2)}, u32[]{:S(2)}) collective-permute-start(bf16[2,8,1024]{2,1,0:T(8,128)(2,1)S(1)} %get-tuple-element.43), channel_id=1, source_target_pairs={{0,12},{1,13},{2,14},{3,15},{4,8},{5,9},{6,10},{7,11},{8,20},{9,21... | collective-permute-start | bytes 98312 | tf_op jit(solution)/shard_map/ppermute | solution.py:531
  78.3 1.5 %collective-permute-start.26 = (bf16[2,8,1024]{2,1,0:T(8,128)(2,1)S(1)}, bf16[2,8,1024]{2,1,0:T(8,128)(2,1)S(1)}, u32[]{:S(2)}, u32[]{:S(2)}) collective-permute-start(bf16[2,8,1024]{2,1,0:T(8,128)(2,1)S(1)} %get-tuple-element.44), channel_id=1, source_target_pairs={{0,14},{1,15},{2,12},{3,13},{4,10},{5,11},{6,8},{7,9},{8,22},{9,23... | collective-permute-start | bytes 98312 | tf_op jit(solution)/shard_map/ppermute | solution.py:531
  79.8 3.1 %collective-permute-done.25.refs_2_ = bf16[2,8,1024]{2,1,0:T(8,128)(2,1)S(1)} collective-permute-done((bf16[2,8,1024]{2,1,0:T(8,128)(2,1)S(1)}, bf16[2,8,1024]{2,1,0:T(8,128)(2,1)S(1)}, u32[]{:S(2)}, u32[]{:S(2)}) %collective-permute-start.25) | collective-permute-done | bytes 32800 | tf_op jit(solution)/shard_map/ppermute | solution.py:531
  82.9 2.9 %collective-permute-done.26.refs_3_ = bf16[2,8,1024]{2,1,0:T(8,128)(2,1)S(1)} collective-permute-done((bf16[2,8,1024]{2,1,0:T(8,128)(2,1)S(1)}, bf16[2,8,1024]{2,1,0:T(8,128)(2,1)S(1)}, u32[]{:S(2)}, u32[]{:S(2)}) %collective-permute-start.26) | collective-permute-done | bytes 32800 | tf_op jit(solution)/shard_map/ppermute | solution.py:531
  85.8 1.2 %place.1 = bf16[1,8,8192]{2,1,0:T(8,128)(2,1)} custom-call(s32[2]{0:T(128)S(1)} %pad_add_fusion.place, bf16[2,8,1024]{2,1,0:T(8,128)(2,1)S(1)} %collective-permute-done.23.refs_0_, bf16[2,8,1024]{2,1,0:T(8,128)(2,1)S(1)} %collective-permute-done.24.refs_1_, bf16[2,8,1024]{2,1,0:T(8,128)(2,1)S(1)} %collective-permute-done.25.refs_2_, ...), custom_call_target="tpu_custom_call" | custom-call | tf_op jit(solution)/shard_map/place/pallas_call | solution.py:490
  (51 shorter events, 5.0 us)
Async XLA Ops:
  0.0 48.0 %copy-start.5 = (f32[1,8192]{1,0:T(1,128)S(1)}, f32[1,8192]{1,0:T(1,128)}, u32[]{:S(2)}) copy-start(f32[1,8192]{1,0:T(1,128)} %refs_8_.1) | copy-start | bytes 98308
  0.0 17.1 %collective-permute-start.1 = (bf16[8,8192]{1,0:T(8,128)(2,1)}, bf16[8,8192]{1,0:T(8,128)(2,1)S(1)}, u32[]{:S(2)}, u32[]{:S(2)}) collective-permute-start(bf16[8,8192]{1,0:T(8,128)(2,1)} %bitcast.15), channel_id=1, source_target_pairs={{0,2},{1,3},{2,0},{3,1},{4,6},{5,7},{6,4},{7,5},{8,10},{9,11},{10,... | collective-permute-start | bytes 393224 | tf_op jit(solution)/shard_map/ppermute | solution.py:159
  3.0 17.1 %collective-permute-start = (bf16[8,8192]{1,0:T(8,128)(2,1)}, bf16[8,8192]{1,0:T(8,128)(2,1)S(1)}, u32[]{:S(2)}, u32[]{:S(2)}) collective-permute-start(bf16[8,8192]{1,0:T(8,128)(2,1)} %bitcast.16), channel_id=1, source_target_pairs={{0,1},{1,0},{2,3},{3,2},{4,5},{5,4},{6,7},{7,6},{8,9},{9,8},{10,11... | collective-permute-start | bytes 393224 | tf_op jit(solution)/shard_map/ppermute | solution.py:163
  6.3 12.2 %copy-start.4 = (bf16[1,8,8192]{2,1,0:T(8,128)(2,1)S(1)}, bf16[1,8,8192]{2,1,0:T(8,128)(2,1)}, u32[]{:S(2)}) copy-start(bf16[1,8,8192]{2,1,0:T(8,128)(2,1)} %param.10) | copy-start | bytes 393220
  7.3 38.0 %collective-permute-start.9 = (bf16[1040,128]{1,0:T(8,128)(2,1)S(1)}, bf16[1040,128]{1,0:T(8,128)(2,1)S(1)}, u32[]{:S(2)}, u32[]{:S(2)}) collective-permute-start(bf16[1040,128]{1,0:T(8,128)(2,1)S(1)} %get-tuple-element.34), channel_id=1, source_target_pairs={{0,2},{1,3},{2,0},{3,1},{4,6},{5,7},{6,4},{7,5},{8,10},{9,11},{10,... | collective-permute-start | bytes 798728 | tf_op jit(solution)/shard_map/ppermute | solution.py:159
  7.4 38.3 %collective-permute-start.11 = (bf16[1040,128]{1,0:T(8,128)(2,1)S(1)}, bf16[1040,128]{1,0:T(8,128)(2,1)S(1)}, u32[]{:S(2)}, u32[]{:S(2)}) collective-permute-start(bf16[1040,128]{1,0:T(8,128)(2,1)S(1)} %get-tuple-element.35), channel_id=1, source_target_pairs={{0,4},{1,5},{2,6},{3,7},{4,0},{5,1},{6,2},{7,3},{8,12},{9,13},{10,... | collective-permute-start | bytes 798728 | tf_op jit(solution)/shard_map/ppermute | solution.py:159
  10.4 3.4 %copy-start = (bf16[1,8192,512]{2,1,0:T(8,128)(2,1)S(1)}, bf16[1,8192,512]{2,1,0:T(8,128)(2,1)}, u32[]{:S(2)}) copy-start(bf16[1,8192,512]{2,1,0:T(8,128)(2,1)} %refs_0_.1) | copy-start | bytes 25165828
  16.2 51.9 %slice-start = ((s8[8388608]{0:T(1024)(128)(4,1)}), s8[4194304]{0:T(1024)(128)(4,1)S(1)}, s32[]{:S(2)}) async-start(s8[8388608]{0:T(1024)(128)(4,1)} %bitcast.10), calls=%async_computation | async-start | bytes 8388608
  17.1 28.8 %collective-permute-start.13 = (bf16[1040,128]{1,0:T(8,128)(2,1)S(1)}, bf16[1040,128]{1,0:T(8,128)(2,1)S(1)}, u32[]{:S(2)}, u32[]{:S(2)}) collective-permute-start(bf16[1040,128]{1,0:T(8,128)(2,1)S(1)} %get-tuple-element.37), channel_id=1, source_target_pairs={{0,6},{1,7},{2,4},{3,5},{4,2},{5,3},{6,0},{7,1},{8,14},{9,15},{10,... | collective-permute-start | bytes 798728 | tf_op jit(solution)/shard_map/ppermute | solution.py:159
  18.5 25.3 %collective-permute-start.3 = (bf16[8,8192]{1,0:T(8,128)(2,1)S(1)}, bf16[8,8192]{1,0:T(8,128)(2,1)S(1)}, u32[]{:S(2)}, u32[]{:S(2)}) collective-permute-start(bf16[8,8192]{1,0:T(8,128)(2,1)S(1)} %bitcast.17), channel_id=1, source_target_pairs={{0,4},{1,5},{2,6},{3,7},{4,0},{5,1},{6,2},{7,3},{8,12},{9,13},{10,... | collective-permute-start | bytes 393224 | tf_op jit(solution)/shard_map/ppermute | solution.py:159
  20.2 23.6 %collective-permute-start.5 = (bf16[8,8192]{1,0:T(8,128)(2,1)S(1)}, bf16[8,8192]{1,0:T(8,128)(2,1)S(1)}, u32[]{:S(2)}, u32[]{:S(2)}) collective-permute-start(bf16[8,8192]{1,0:T(8,128)(2,1)S(1)} %bitcast.18), channel_id=1, source_target_pairs={{0,6},{1,7},{2,4},{3,5},{4,2},{5,3},{6,0},{7,1},{8,14},{9,15},{10,... | collective-permute-start | bytes 393224 | tf_op jit(solution)/shard_map/ppermute | solution.py:159
  43.8 1.3 %collective-permute-start.2 = (bf16[8,8192]{1,0:T(8,128)(2,1)S(1)}, bf16[8,8192]{1,0:T(8,128)(2,1)S(1)}, u32[]{:S(2)}, u32[]{:S(2)}) collective-permute-start(bf16[8,8192]{1,0:T(8,128)(2,1)S(1)} %collective-permute-done.1.refs_2_), channel_id=1, source_target_pairs={{0,1},{1,0},{2,3},{3,2},{4,5},{5,4},{6,7},{7,6},{8,9},{9,8},{10,11... | collective-permute-start | bytes 393224 | tf_op jit(solution)/shard_map/ppermute | solution.py:163
  43.8 2.4 %collective-permute-start.4 = (bf16[8,8192]{1,0:T(8,128)(2,1)S(1)}, bf16[8,8192]{1,0:T(8,128)(2,1)S(1)}, u32[]{:S(2)}, u32[]{:S(2)}) collective-permute-start(bf16[8,8192]{1,0:T(8,128)(2,1)S(1)} %collective-permute-done.3.refs_4_), channel_id=1, source_target_pairs={{0,1},{1,0},{2,3},{3,2},{4,5},{5,4},{6,7},{7,6},{8,9},{9,8},{10,11... | collective-permute-start | bytes 393224 | tf_op jit(solution)/shard_map/ppermute | solution.py:163
  45.2 6.7 %collective-permute-start.8 = (bf16[1040,128]{1,0:T(8,128)(2,1)S(1)}, bf16[1040,128]{1,0:T(8,128)(2,1)S(1)}, u32[]{:S(2)}, u32[]{:S(2)}) collective-permute-start(bf16[1040,128]{1,0:T(8,128)(2,1)S(1)} %get-tuple-element.33.refs_0_), channel_id=1, source_target_pairs={{0,1},{1,0},{2,3},{3,2},{4,5},{5,4},{6,7},{7,6},{8,9},{9,8},{10,11... | collective-permute-start | bytes 798728 | tf_op jit(solution)/shard_map/ppermute | solution.py:163
  45.3 7.6 %collective-permute-start.10 = (bf16[1040,128]{1,0:T(8,128)(2,1)S(1)}, bf16[1040,128]{1,0:T(8,128)(2,1)S(1)}, u32[]{:S(2)}, u32[]{:S(2)}) collective-permute-start(bf16[1040,128]{1,0:T(8,128)(2,1)S(1)} %collective-permute-done.9.refs_2_), channel_id=1, source_target_pairs={{0,1},{1,0},{2,3},{3,2},{4,5},{5,4},{6,7},{7,6},{8,9},{9,8},{10,11... | collective-permute-start | bytes 798728 | tf_op jit(solution)/shard_map/ppermute | solution.py:163
  45.7 7.2 %collective-permute-start.12 = (bf16[1040,128]{1,0:T(8,128)(2,1)S(1)}, bf16[1040,128]{1,0:T(8,128)(2,1)S(1)}, u32[]{:S(2)}, u32[]{:S(2)}) collective-permute-start(bf16[1040,128]{1,0:T(8,128)(2,1)S(1)} %collective-permute-done.11.refs_4_), channel_id=1, source_target_pairs={{0,1},{1,0},{2,3},{3,2},{4,5},{5,4},{6,7},{7,6},{8,9},{9,8},{10,11... | collective-permute-start | bytes 798728 | tf_op jit(solution)/shard_map/ppermute | solution.py:163
  45.8 7.0 %collective-permute-start.14 = (bf16[1040,128]{1,0:T(8,128)(2,1)S(1)}, bf16[1040,128]{1,0:T(8,128)(2,1)S(1)}, u32[]{:S(2)}, u32[]{:S(2)}) collective-permute-start(bf16[1040,128]{1,0:T(8,128)(2,1)S(1)} %collective-permute-done.13.refs_6_), channel_id=1, source_target_pairs={{0,1},{1,0},{2,3},{3,2},{4,5},{5,4},{6,7},{7,6},{8,9},{9,8},{10,11... | collective-permute-start | bytes 798728 | tf_op jit(solution)/shard_map/ppermute | solution.py:163
  46.2 1.8 %collective-permute-start.6 = (bf16[8,8192]{1,0:T(8,128)(2,1)S(1)}, bf16[8,8192]{1,0:T(8,128)(2,1)S(1)}, u32[]{:S(2)}, u32[]{:S(2)}) collective-permute-start(bf16[8,8192]{1,0:T(8,128)(2,1)S(1)} %collective-permute-done.5.refs_6_), channel_id=1, source_target_pairs={{0,1},{1,0},{2,3},{3,2},{4,5},{5,4},{6,7},{7,6},{8,9},{9,8},{10,11... | collective-permute-start | bytes 393224 | tf_op jit(solution)/shard_map/ppermute | solution.py:163
  48.0 20.0 %slice-start.1 = ((s8[8388608]{0:T(1024)(128)(4,1)}), s8[4194304]{0:T(1024)(128)(4,1)S(1)}, s32[]{:S(2)}) async-start(s8[8388608]{0:T(1024)(128)(4,1)} %bitcast.10), calls=%async_computation.1 | async-start | bytes 8388608
  51.6 1.2 %collective-permute-start.7 = (bf16[64,128]{1,0:T(8,128)(2,1)S(1)}, bf16[64,128]{1,0:T(8,128)(2,1)S(1)}, u32[]{:S(2)}, u32[]{:S(2)}) collective-permute-start(bf16[64,128]{1,0:T(8,128)(2,1)S(1)} %get-tuple-element.32.kv_mine), channel_id=1, source_target_pairs={{0,1},{1,0},{2,3},{3,2},{4,5},{5,4},{6,7},{7,6},{8,9},{9,8},{10,11... | collective-permute-start | bytes 49160 | tf_op jit(solution)/shard_map/ppermute | solution.py:163
  56.1 4.9 %collective-permute-start.16 = (bf16[64,512]{1,0:T(8,128)(2,1)S(1)}, bf16[64,512]{1,0:T(8,128)(2,1)S(1)}, u32[]{:S(2)}, u32[]{:S(2)}) collective-permute-start(bf16[64,512]{1,0:T(8,128)(2,1)S(1)} %attend.1.refs_0_), channel_id=1, source_target_pairs={{0,2},{1,3},{2,0},{3,1},{4,6},{5,7},{6,4},{7,5},{8,10},{9,11},{10,... | collective-permute-start | bytes 196616 | tf_op jit(solution)/shard_map/ppermute | solution.py:159
  58.3 8.3 %collective-permute-start.18 = (bf16[64,512]{1,0:T(8,128)(2,1)S(1)}, bf16[64,512]{1,0:T(8,128)(2,1)S(1)}, u32[]{:S(2)}, u32[]{:S(2)}) collective-permute-start(bf16[64,512]{1,0:T(8,128)(2,1)S(1)} %attend.1.refs_0_), channel_id=1, source_target_pairs={{0,4},{1,5},{2,6},{3,7},{4,0},{5,1},{6,2},{7,3},{8,12},{9,13},{10,... | collective-permute-start | bytes 196616 | tf_op jit(solution)/shard_map/ppermute | solution.py:159
  60.0 6.6 %collective-permute-start.20 = (bf16[64,512]{1,0:T(8,128)(2,1)S(1)}, bf16[64,512]{1,0:T(8,128)(2,1)S(1)}, u32[]{:S(2)}, u32[]{:S(2)}) collective-permute-start(bf16[64,512]{1,0:T(8,128)(2,1)S(1)} %attend.1.refs_0_), channel_id=1, source_target_pairs={{0,6},{1,7},{2,4},{3,5},{4,2},{5,3},{6,0},{7,1},{8,14},{9,15},{10,... | collective-permute-start | bytes 196616 | tf_op jit(solution)/shard_map/ppermute | solution.py:159
  61.0 6.2 %collective-permute-start.15 = (bf16[64,512]{1,0:T(8,128)(2,1)S(1)}, bf16[64,512]{1,0:T(8,128)(2,1)S(1)}, u32[]{:S(2)}, u32[]{:S(2)}) collective-permute-start(bf16[64,512]{1,0:T(8,128)(2,1)S(1)} %attend.1.refs_0_), channel_id=1, source_target_pairs={{0,1},{1,0},{2,3},{3,2},{4,5},{5,4},{6,7},{7,6},{8,9},{9,8},{10,11... | collective-permute-start | bytes 196616 | tf_op jit(solution)/shard_map/ppermute | solution.py:163
  61.0 6.2 %collective-permute-start.17 = (bf16[64,512]{1,0:T(8,128)(2,1)S(1)}, bf16[64,512]{1,0:T(8,128)(2,1)S(1)}, u32[]{:S(2)}, u32[]{:S(2)}) collective-permute-start(bf16[64,512]{1,0:T(8,128)(2,1)S(1)} %collective-permute-done.16.refs_2_), channel_id=1, source_target_pairs={{0,1},{1,0},{2,3},{3,2},{4,5},{5,4},{6,7},{7,6},{8,9},{9,8},{10,11... | collective-permute-start | bytes 196616 | tf_op jit(solution)/shard_map/ppermute | solution.py:163
  66.7 1.3 %collective-permute-start.19 = (bf16[64,512]{1,0:T(8,128)(2,1)S(1)}, bf16[64,512]{1,0:T(8,128)(2,1)S(1)}, u32[]{:S(2)}, u32[]{:S(2)}) collective-permute-start(bf16[64,512]{1,0:T(8,128)(2,1)S(1)} %collective-permute-done.18.refs_4_), channel_id=1, source_target_pairs={{0,1},{1,0},{2,3},{3,2},{4,5},{5,4},{6,7},{7,6},{8,9},{9,8},{10,11... | collective-permute-start | bytes 196616 | tf_op jit(solution)/shard_map/ppermute | solution.py:163
  66.7 1.4 %collective-permute-start.21 = (bf16[64,512]{1,0:T(8,128)(2,1)S(1)}, bf16[64,512]{1,0:T(8,128)(2,1)S(1)}, u32[]{:S(2)}, u32[]{:S(2)}) collective-permute-start(bf16[64,512]{1,0:T(8,128)(2,1)S(1)} %collective-permute-done.20.refs_6_), channel_id=1, source_target_pairs={{0,1},{1,0},{2,3},{3,2},{4,5},{5,4},{6,7},{7,6},{8,9},{9,8},{10,11... | collective-permute-start | bytes 196616 | tf_op jit(solution)/shard_map/ppermute | solution.py:163
  70.2 1.3 %collective-permute-start.22 = (bf16[4,8,1024]{2,1,0:T(8,128)(2,1)S(1)}, bf16[4,8,1024]{2,1,0:T(8,128)(2,1)S(1)}, u32[]{:S(2)}, u32[]{:S(2)}) collective-permute-start(bf16[4,8,1024]{2,1,0:T(8,128)(2,1)S(1)} %get-tuple-element.40), channel_id=1, source_target_pairs={{0,1},{1,0},{2,3},{3,2},{4,5},{5,4},{6,7},{7,6},{8,9},{9,8},{10,11... | collective-permute-start | bytes 196616 | tf_op jit(solution)/shard_map/ppermute | solution.py:163
  72.1 7.7 %collective-permute-start.23 = (bf16[2,8,1024]{2,1,0:T(8,128)(2,1)S(1)}, bf16[2,8,1024]{2,1,0:T(8,128)(2,1)S(1)}, u32[]{:S(2)}, u32[]{:S(2)}) collective-permute-start(bf16[2,8,1024]{2,1,0:T(8,128)(2,1)S(1)} %get-tuple-element.41), channel_id=1, source_target_pairs={{0,8},{1,9},{2,10},{3,11},{4,12},{5,13},{6,14},{7,15},{8,16},{9,17... | collective-permute-start | bytes 98312 | tf_op jit(solution)/shard_map/ppermute | solution.py:531
  73.6 6.2 %collective-permute-start.24 = (bf16[2,8,1024]{2,1,0:T(8,128)(2,1)S(1)}, bf16[2,8,1024]{2,1,0:T(8,128)(2,1)S(1)}, u32[]{:S(2)}, u32[]{:S(2)}) collective-permute-start(bf16[2,8,1024]{2,1,0:T(8,128)(2,1)S(1)} %get-tuple-element.42), channel_id=1, source_target_pairs={{0,10},{1,11},{2,8},{3,9},{4,14},{5,15},{6,12},{7,13},{8,18},{9,19... | collective-permute-start | bytes 98312 | tf_op jit(solution)/shard_map/ppermute | solution.py:531
  75.9 7.0 %collective-permute-start.25 = (bf16[2,8,1024]{2,1,0:T(8,128)(2,1)S(1)}, bf16[2,8,1024]{2,1,0:T(8,128)(2,1)S(1)}, u32[]{:S(2)}, u32[]{:S(2)}) collective-permute-start(bf16[2,8,1024]{2,1,0:T(8,128)(2,1)S(1)} %get-tuple-element.43), channel_id=1, source_target_pairs={{0,12},{1,13},{2,14},{3,15},{4,8},{5,9},{6,10},{7,11},{8,20},{9,21... | collective-permute-start | bytes 98312 | tf_op jit(solution)/shard_map/ppermute | solution.py:531
  78.3 7.5 %collective-permute-start.26 = (bf16[2,8,1024]{2,1,0:T(8,128)(2,1)S(1)}, bf16[2,8,1024]{2,1,0:T(8,128)(2,1)S(1)}, u32[]{:S(2)}, u32[]{:S(2)}) collective-permute-start(bf16[2,8,1024]{2,1,0:T(8,128)(2,1)S(1)} %get-tuple-element.44), channel_id=1, source_target_pairs={{0,14},{1,15},{2,12},{3,13},{4,10},{5,11},{6,8},{7,9},{8,22},{9,23... | collective-permute-start | bytes 98312 | tf_op jit(solution)/shard_map/ppermute | solution.py:531
  (5 other events, 5.0 us)

commit v3 on v2

--- a/solution.py
+++ b/solution.py
@@ -147,6 +147,7 @@
 
 CORES = 2
 TAIL = 16
+LANES = 128
 VMEM = pl.BlockSpec(memory_space=pltpu.VMEM)
 SMEM = pl.BlockSpec(memory_space=pltpu.SMEM)
 ANYWHERE = pl.BlockSpec(memory_space=pl.ANY)
@@ -174,6 +175,11 @@
 
 def in_vmem(x):
     return pltpu.with_memory_space_constraint(x, pltpu.VMEM)
+
+
+def my_place():
+    me = lax.axis_index("dev")
+    return me, me // CORES, lax.rem(me, CORES)
 
 
 def matmul(a, b, dims=((1,), (0,))):
@@ -204,108 +210,164 @@
         out_specs=[VMEM] * len(arrays),
         scratch_shapes=[pltpu.SemaphoreType.DMA((len(arrays), 4))],
         compiler_params=pltpu.CompilerParams(vmem_limit_bytes=2 * MIB),
-        cost_estimate=pl.CostEstimate(
-            flops=0, bytes_accessed=sum(a.size * 2 for a in arrays), transcendentals=0
-        ),
+        cost_estimate=pl.CostEstimate(flops=0, bytes_accessed=0, transcendentals=0),
         name="load",
-    )(*arrays)
-
-
-def pack_kernel(place, table, retrieved, counts, cache, *rest):
-    outs, (whole, sems) = rest[:-2], rest[-2:]
+    )(*[pltpu.with_memory_space_constraint(a, pltpu.HBM) for a in arrays])
+
+
+def pack_kernel(counts, table_in, retrieved_in, state_in, cache, *rest):
+    outs, (whole, state, table, retrieved, sems, list_sems) = rest[:KV_HEADS], rest[KV_HEADS:]
+    _, pair, _ = my_place()
+    lists = [
+        pltpu.make_async_copy(source, target, list_sems.at[i])
+        for i, (source, target) in enumerate(
+            ((table_in, table), (retrieved_in, retrieved), (state_in, state))
+        )
+    ]
     lines, tokens = whole.shape[0], whole.shape[1]
     width = whole.shape[2] // 2
     copies = [
         pltpu.make_async_copy(cache.at[0, line], whole.at[line], sems.at[line]) for line in range(lines)
     ]
-    for copy in copies:
+    for copy in lists + copies:
         copy.start()
+    for copy in lists:
+        copy.wait()
     listed = retrieved.shape[2]
     lane = lax.broadcasted_iota(jnp.int32, (TAIL, HEAD_DIM), 1)
     note = jnp.where(lane == listed, counts[0, 0], 0)
     for k in range(listed):
         note = jnp.where(lane == k, table[retrieved[0, 0, k]], note)
     note = note.astype(jnp.float32).astype(jnp.bfloat16)
+    end = lines * 2 * tokens
     for out in outs:
-        out[lines * 2 * tokens :, :] = note
+        out[end : end + TAIL, :] = note
+    rows = state.shape[0]
+    for t in range(state.shape[1] // LANES // 2):
+        tile = jnp.concatenate(
+            [
+                state[:, i * LANES : (i + 1) * LANES].astype(jnp.float32)
+                for i in (2 * t, 2 * t + 1)
+            ],
+            axis=0,
+        ).astype(jnp.bfloat16)
+        at = end + TAIL + 2 * rows * t
+        for out in outs[:-1]:
+            out[at : at + 2 * rows, :] = tile
     for line in range(lines):
         copies[line].wait()
         for k, out in enumerate(outs):
-            head = lax.bitwise_xor(place[0], k)
+            head = lax.bitwise_xor(pair, k)
             for part in range(2):
                 columns = pl.ds(pl.multiple_of(part * width + head * HEAD_DIM, HEAD_DIM), HEAD_DIM)
                 at = (line * 2 + part) * tokens
                 out[at : at + tokens, :] = whole[line, :, columns]
 
 
-def pack(place, table, retrieved, counts, cache):
+def pack(table, retrieved, counts, state, cache):
     rows, tokens = cache.shape[1], cache.shape[2]
+    short = rows * 2 * tokens + TAIL
+    long = short + state.size // HEAD_DIM
     return pl.pallas_call(
         pack_kernel,
-        out_shape=[pltpu.VMEM((rows * 2 * tokens + TAIL, HEAD_DIM), cache.dtype)] * KV_HEADS,
-        in_specs=[SMEM] * 4 + [ANYWHERE],
+        out_shape=[
+            pltpu.VMEM((long if k < KV_HEADS - 1 else short, HEAD_DIM), cache.dtype)
+            for k in range(KV_HEADS)
+        ],
+        in_specs=[SMEM] + [HBM] * 4,
         out_specs=[VMEM] * KV_HEADS,
         scratch_shapes=[
             pltpu.VMEM(cache.shape[1:], cache.dtype),
+            pltpu.VMEM(state.shape, state.dtype),
+            pltpu.SMEM(table.shape, table.dtype),
+            pltpu.SMEM(retrieved.shape, retrieved.dtype),
             pltpu.SemaphoreType.DMA((rows,)),
+            pltpu.SemaphoreType.DMA((3,)),
         ],
         compiler_params=pltpu.CompilerParams(vmem_limit_bytes=6 * MIB),
-        cost_estimate=pl.CostEstimate(flops=0, bytes_accessed=2 * cache.size * 2, transcendentals=0),
+        cost_estimate=pl.CostEstimate(flops=0, bytes_accessed=0, transcendentals=0),
         name="pack",
-    )(place, table, retrieved, counts, cache)
-
-
-def project_kernel(place, *refs):
+    )(counts, *[pltpu.with_memory_space_constraint(a, pltpu.HBM) for a in (table, retrieved, state, cache)])
+
+
+def project_kernel(*refs):
     count = 2 * KV_HEADS
     parts, rest = refs[:count], refs[count:]
-    gain, wq, wk, wv, q_out, kv_out, cols_out, normed = rest
-    pair, core = place[0], place[1]
+    gain, wk, wv, normed, kv_out, cols_out = rest
+    me, pair, core = my_place()
     first = core == 0
-    width = cols_out.shape[1]
-    columns = pl.ds(pl.multiple_of((CORES * pair + core) * width, 128), width)
+    tiles = gain.shape[0]
+    rows = normed.shape[0] // count
+    mine = cols_out.shape[1] // LANES
     for k in range(KV_HEADS):
         source = lax.bitwise_xor(pair, k)
-        rows = pl.ds(pl.multiple_of(source * 16, 16), 16)
-
-        def both(at):
-            a, b = (parts[2 * k + p][:, at].astype(jnp.float32) for p in range(CORES))
-            return jnp.concatenate([jnp.where(first, a, b), jnp.where(first, b, a)], axis=0)
-
-        state = both(slice(None))
-        inverse = lax.rsqrt(jnp.mean(state * state, axis=-1, keepdims=True) + norm_eps)
-        normed[rows, :] = (state * inverse * gain[...]).astype(jnp.bfloat16)
-        cols_out[rows, :] = both(columns).astype(cols_out.dtype)
+        at = pl.ds(pl.multiple_of(source * 2 * rows, 2 * rows), 2 * rows)
+        pieces, selected = [], []
+        for p in range(CORES):
+            part = parts[2 * k + p]
+            start = part.shape[0] - tiles * rows
+            state = part[start:, :].astype(jnp.float32).reshape(tiles, rows, LANES)
+            square = jnp.sum(jnp.sum(state * state, axis=0), axis=-1, keepdims=True)
+            inverse = lax.rsqrt(square / (tiles * LANES) + norm_eps)
+            pieces.append(state * inverse[None] * gain[...][:, None, :])
+            offset = pl.multiple_of(start + me * mine * rows, 2 * rows)
+            selected.append(
+                part[pl.ds(offset, mine * rows), :].astype(jnp.float32).reshape(mine, rows, LANES)
+            )
+        low, high = jnp.where(first, *pieces), jnp.where(first, *pieces[::-1])
+        for t in range(tiles):
+            normed[at, t * LANES : (t + 1) * LANES] = jnp.concatenate([low[t], high[t]], axis=0).astype(
+                normed.dtype
+            )
+        low, high = jnp.where(first, *selected), jnp.where(first, *selected[::-1])
+        for t in range(mine):
+            cols_out[at, t * LANES : (t + 1) * LANES] = jnp.concatenate(
+                [low[t], high[t]], axis=0
+            ).astype(cols_out.dtype)
     key = matmul(normed[...], wk[...], ((1,), (1,)))
     value = matmul(normed[...], wv[...], ((1,), (1,)))
     kv_out[...] = jnp.concatenate([key, value], axis=1).astype(kv_out.dtype)
-    q_out[...] = matmul(normed[...], wq[...]).astype(q_out.dtype)
-
-
-def project(place, parts, gain, wq, wk, wv):
-    tokens = sum(p.shape[0] for p in parts)
-    width = parts[0].shape[1]
+
+
+def project(parts, gain, wk, wv, tokens):
+    width = wk.shape[1]
     bf16 = jnp.bfloat16
     return pl.pallas_call(
         project_kernel,
         out_shape=[
-            pltpu.VMEM((tokens, wq.shape[1]), bf16),
+            pltpu.VMEM((tokens, width), bf16),
             pltpu.VMEM((tokens, 2 * wk.shape[0]), bf16),
             pltpu.VMEM((tokens, width // len(parts)), bf16),
         ],
-        in_specs=[SMEM] + [VMEM] * (len(parts) + 4),
+        in_specs=[VMEM] * (len(parts) + 3),
         out_specs=[VMEM] * 3,
-        scratch_shapes=[pltpu.VMEM((tokens, width), bf16)],
-        compiler_params=pltpu.CompilerParams(vmem_limit_bytes=16 * MIB),
+        compiler_params=pltpu.CompilerParams(vmem_limit_bytes=12 * MIB),
+        cost_estimate=pl.CostEstimate(flops=0, bytes_accessed=0, transcendentals=0),
+        name="project",
+    )(*[in_vmem(p) for p in parts], gain.reshape(-1, LANES), in_vmem(wk), in_vmem(wv))
+
+
+def query_kernel(normed, wq, out):
+    out[...] = matmul(normed[...], wq[...]).astype(out.dtype)
+
+
+def query(normed, wq):
+    return pl.pallas_call(
+        query_kernel,
+        out_shape=pltpu.VMEM((normed.shape[0], wq.shape[1]), jnp.bfloat16),
+        in_specs=[VMEM] * 2,
+        out_specs=VMEM,
+        compiler_params=pltpu.CompilerParams(vmem_limit_bytes=12 * MIB),
         cost_estimate=pl.CostEstimate(
-            flops=2 * tokens * width * 640, bytes_accessed=2 * width * 640, transcendentals=0
+            flops=0, bytes_accessed=0, transcendentals=0
         ),
-        name="project",
-    )(place, *[in_vmem(p) for p in parts], gain, in_vmem(wq), in_vmem(wk), in_vmem(wv))
-
-
-def attend_kernel(place, q, kv_mine, kv_other, *refs):
+        name="query",
+    )(in_vmem(normed), in_vmem(wq))
+
+
+def attend_kernel(q, kv_mine, kv_other, *refs):
     count = 2 * KV_HEADS
-    held, (out, blocks, placed, scored, notes, meta, sems, note_sem) = refs[:count], refs[count:]
+    held, (out, blocks, placed, scored, notes, tail_vm, meta, sems, note_sems) = refs[:count], refs[count:]
     requests, listed = scored.shape[:2]
     tokens = q.shape[0]
     question = tokens // requests
@@ -313,10 +375,13 @@
     group = heads * question
     block = scored.shape[3]
     rows = (blocks.shape[1] - TAIL) // (2 * block)
-    pair, core = place[0], place[1]
-    me = CORES * pair + core
-    copies = [pltpu.make_async_copy(held[i], blocks.at[i], sems.at[i]) for i in range(count)]
-    for copy in copies:
+    me, pair, core = my_place()
+    tail, whole = pl.ds(rows * 2 * block, TAIL), pl.ds(0, rows * 2 * block + TAIL)
+    tails = [
+        pltpu.make_async_copy(held[i].at[tail], tail_vm.at[i], note_sems.at[i]) for i in range(count)
+    ]
+    copies = [pltpu.make_async_copy(held[i].at[whole], blocks.at[i], sems.at[i]) for i in range(count)]
+    for copy in tails + copies:
         copy.start()
     scale = HEAD_DIM ** (-0.5)
     first = core == 0
@@ -335,13 +400,12 @@
             ).astype(jnp.bfloat16)
         )
     stacked = jnp.concatenate(queries, axis=0)
-    for copy in copies:
+    for copy in tails:
         copy.wait()
-    tail = slice(rows * 2 * block, rows * 2 * block + TAIL)
     notes[...] = jnp.concatenate(
-        [blocks[i, tail, :].astype(jnp.float32)[:1] for i in range(count)], axis=0
+        [tail_vm[i].astype(jnp.float32)[:1] for i in range(count)], axis=0
     ).astype(jnp.int32)
-    noted = pltpu.make_async_copy(notes, meta, note_sem)
+    noted = pltpu.make_async_copy(notes, meta, note_sems.at[count])
     noted.start()
     scores = matmul(stacked, own_key, ((1,), (1,))) * scale
     row = lax.broadcasted_iota(jnp.int32, scores.shape, 0)
@@ -352,6 +416,8 @@
     own_total = jnp.sum(weights, axis=-1, keepdims=True)
     own_acc = matmul(weights.astype(jnp.bfloat16), own_value)
     noted.wait()
+    for copy in copies:
+        copy.wait()
     lives, places = [], []
     for r in range(requests):
         at = lax.bitwise_xor(me, r)
@@ -393,143 +459,149 @@
     out[...] = placed[...].astype(out.dtype)
 
 
-def attend(place, q, kv_mine, kv_other, held, requests, listed, block):
+def attend(q, kv_mine, kv_other, held, requests, listed, block):
     count = len(held)
     return pl.pallas_call(
         attend_kernel,
         out_shape=pltpu.VMEM(q.shape, jnp.bfloat16),
-        in_specs=[SMEM] + [VMEM] * 3 + [ANYWHERE] * count,
+        in_specs=[VMEM] * 3 + [ANYWHERE] * count,
         out_specs=VMEM,
         scratch_shapes=[
-            pltpu.VMEM((count, *held[0].shape), jnp.bfloat16),
+            pltpu.VMEM((count, *held[-1].shape), jnp.bfloat16),
             pltpu.VMEM(q.shape, jnp.float32),
             pltpu.VMEM((requests, listed, q.size // HEAD_DIM // requests, block), jnp.float32),
             pltpu.VMEM((count, HEAD_DIM), jnp.int32),
+            pltpu.VMEM((count, TAIL, HEAD_DIM), jnp.bfloat16),
             pltpu.SMEM((count, HEAD_DIM), jnp.int32),
             pltpu.SemaphoreType.DMA((count,)),
-            pltpu.SemaphoreType.DMA,
+            pltpu.SemaphoreType.DMA((count + 1,)),
         ],
         compiler_params=pltpu.CompilerParams(vmem_limit_bytes=16 * MIB),
         cost_estimate=pl.CostEstimate(
             flops=1 << 28, bytes_accessed=2 * MIB, transcendentals=1 << 18
         ),
         name="attend",
-    )(place, in_vmem(q), in_vmem(kv_mine), in_vmem(kv_other), *held)
-
-
-def finish_kernel(place, *refs):
-    count = 2 * KV_HEADS
-    parts, (cols, w_out, keep, give, placed) = refs[:count], refs[count:]
-    pair, core = place[0], place[1]
-    me = CORES * pair + core
+    )(in_vmem(q), in_vmem(kv_mine), in_vmem(kv_other), *held)
+
+
+def partial_kernel(*refs):
+    parts, (w_out, out) = refs[:-2], refs[-2:]
+    me, _, _ = my_place()
     depth = parts[0].shape[1]
     total = None
-    for i in range(count):
+    for i, part in enumerate(parts):
         source = lax.bitwise_xor(me, i)
         span = pl.ds(pl.multiple_of(source * depth, depth), depth)
-        product = matmul(parts[i][...], w_out[span, :])
+        product = matmul(part[...], w_out[span, :])
         total = product if total is None else total + product
+    out[...] = total
+
+
+def partial_branch(parts, w_out):
+    tokens, width = parts[0].shape[0], w_out.shape[1]
+    return pl.pallas_call(
+        partial_kernel,
+        out_shape=pltpu.VMEM((tokens, width), jnp.float32),
+        in_specs=[VMEM] * (len(parts) + 1),
+        out_specs=VMEM,
+        compiler_params=pltpu.CompilerParams(vmem_limit_bytes=12 * MIB),
+        cost_estimate=pl.CostEstimate(
+            flops=tokens * w_out.size, bytes_accessed=w_out.size, transcendentals=0
+        ),
+        name="partial",
+    )(*[in_vmem(p) for p in parts], in_vmem(w_out))
+
+
+def finish_kernel(*refs):
+    outs, placed = refs[-1 - KV_HEADS : -1], refs[-1]
+    parts, (before, cols, w_out) = refs[: -4 - KV_HEADS], refs[-4 - KV_HEADS : -1 - KV_HEADS]
+    me, pair, _ = my_place()
+    depth = parts[0].shape[1]
+    total = before[...]
+    for i, part in enumerate(parts):
+        source = lax.bitwise_xor(me, 2 * KV_HEADS - len(parts) + i)
+        span = pl.ds(pl.multiple_of(source * depth, depth), depth)
+        total = total + matmul(part[...], w_out[span, :])
     placed[...] = cols[...].astype(jnp.float32) + total
-    question = keep.shape[1]
-    for z in range(KV_HEADS):
-        lo = placed[z * 2 * question : (z * 2 + 1) * question]
-        hi = placed[(z * 2 + 1) * question : (z * 2 + 2) * question]
-        keep[z] = jnp.where(core == 0, lo, hi).astype(keep.dtype)
-        give[z] = jnp.where(core == 0, hi, lo).astype(give.dtype)
-
-
-def finish(place, parts, cols, w_out):
-    count = len(parts)
+    rows = outs[0].shape[0]
+    for k, out in enumerate(outs):
+        target = lax.bitwise_xor(pair, k)
+        out[...] = placed[pl.ds(pl.multiple_of(target * rows, rows), rows), :].astype(out.dtype)
+
+
+def finish(parts, before, cols, w_out):
     tokens, width = cols.shape
-    shape = pltpu.VMEM((KV_HEADS, tokens // count, width), jnp.bfloat16)
+    shape = pltpu.VMEM((tokens // KV_HEADS, width), jnp.bfloat16)
     return pl.pallas_call(
         finish_kernel,
-        out_shape=[shape] * 2,
-        in_specs=[SMEM] + [VMEM] * (count + 2),
-        out_specs=[VMEM] * 2,
+        out_shape=[shape] * KV_HEADS,
+        in_specs=[VMEM] * (len(parts) + 3),
+        out_specs=[VMEM] * KV_HEADS,
         scratch_shapes=[pltpu.VMEM((tokens, width), jnp.float32)],
-        compiler_params=pltpu.CompilerParams(vmem_limit_bytes=16 * MIB),
+        compiler_params=pltpu.CompilerParams(vmem_limit_bytes=12 * MIB),
         cost_estimate=pl.CostEstimate(
-            flops=2 * tokens * w_out.size, bytes_accessed=2 * w_out.size, transcendentals=0
+            flops=tokens * w_out.size, bytes_accessed=w_out.size, transcendentals=0
         ),
         name="finish",
-    )(place, *[in_vmem(p) for p in parts], in_vmem(cols), in_vmem(w_out))
-
-
-def route_kernel(place, keep, got, *outs):
-    for k, out in enumerate(outs):
-        target = lax.bitwise_xor(place[0], k)
-        out[0] = keep[target]
-        out[1] = got[target]
-
-
-def route_pieces(place, keep, got):
-    shape = pltpu.VMEM((CORES, *keep.shape[1:]), keep.dtype)
-    return pl.pallas_call(
-        route_kernel,
-        out_shape=[shape] * KV_HEADS,
-        in_specs=[SMEM] + [VMEM] * 2,
-        out_specs=[VMEM] * KV_HEADS,
-        compiler_params=pltpu.CompilerParams(vmem_limit_bytes=4 * MIB),
-        name="route",
-    )(place, in_vmem(keep), in_vmem(got))
-
-
-def place_kernel(place, *refs):
+    )(*[in_vmem(p) for p in parts], in_vmem(before), in_vmem(cols), in_vmem(w_out))
+
+
+def place_kernel(order, *refs):
     parts, out = refs[:-1], refs[-1]
-    me = CORES * place[0] + place[1]
-    width = parts[0].shape[2]
-    for k, part in enumerate(parts):
-        for p in range(CORES):
-            source = lax.bitwise_xor(me, CORES * k + p)
-            out[0, :, pl.ds(pl.multiple_of(source * width, width), width)] = part[p]
-
-
-def place_columns(place, parts):
-    cores, rows, width = parts[0].shape
-    return pl.pallas_call(
-        place_kernel,
-        out_shape=jax.ShapeDtypeStruct((1, rows, width * cores * len(parts)), jnp.bfloat16),
-        in_specs=[SMEM] + [VMEM] * len(parts),
+    me, _, core = my_place()
+    rows, width = out.shape[1], parts[0].shape[1]
+    for i, part in zip(order, parts, strict=True):
+        source = lax.bitwise_xor(me, i)
+        both = part[...].astype(jnp.float32)
+        mine = jnp.where(core == 0, both[:rows], both[rows:])
+        out[0, :, pl.ds(pl.multiple_of(source * width, width), width)] = mine.astype(out.dtype)
+
+
+def place_columns(parts):
+    order = sorted(parts, reverse=True)
+    rows, width = parts[0].shape
+    return pl.pallas_call(
+        functools.partial(place_kernel, order),
+        out_shape=jax.ShapeDtypeStruct((1, rows // CORES, width * len(parts)), jnp.bfloat16),
+        in_specs=[VMEM] * len(parts),
         out_specs=VMEM,
         compiler_params=pltpu.CompilerParams(vmem_limit_bytes=4 * MIB),
         name="place",
-    )(place, *[in_vmem(p) for p in parts])
+    )(*[in_vmem(parts[i]) for i in order])
 
 
 def by_head(hidden, gain, w_query, w_key, w_value, w_out, cache, block_slot, retrieved, counts):
     size, sections = lax.axis_size("dev"), lax.axis_size("segment")
-    me = lax.axis_index("dev")
-    place = jnp.stack([me // CORES, me % CORES]).astype(jnp.int32)
-
-    state = hidden[0]
-    arrived = [state] + [to_pair(state, k) for k in range(1, KV_HEADS)]
-    packed = pack(place, block_slot, retrieved, counts, cache)
-    wq, wk, wv = load(w_query, w_key[0].swapaxes(0, 1), w_value[0].swapaxes(0, 1))
-    arrived = [arrived[0]] + [after(a, wq) for a in arrived[1:]]
-    parts = [p for a in arrived for p in (a, to_partner(a))]
-
-    held = [packed[0]]
-    for k in range(1, KV_HEADS):
-        mine = packed[k] if k < 3 else after(packed[k], arrived[1])
-        held.append(to_pair(mine, k))
-    held = [h for a in held for h in (a, to_partner(a))]
-
-    q, kv, cols = project(place, parts, gain, wq, wk, wv)
-    context = attend(
-        place, q, kv, to_partner(kv), held, size, retrieved.shape[2], cache.shape[2]
-    )
-    keep, give = finish(place, from_all(context), cols, w_out[0])
-    pieces = route_pieces(place, keep, to_partner(give))
-    final = []
-    for k, piece in enumerate(pieces):
+    packed = pack(block_slot, retrieved, counts, hidden[0], cache)
+    weights = load(w_query, w_key[0].swapaxes(0, 1), w_value[0].swapaxes(0, 1))
+    second, first, far = to_pair(packed[2], 2), to_pair(packed[1], 1), to_pair(packed[3], 3)
+    second, weights = lax.optimization_barrier((second, weights))
+    crossed = to_pair(second[packed[3].shape[0] :], 1)
+    held = [h for a in (packed[0], first, second) for h in (a, to_partner(a))]
+    held, crossed, (wq, wk, wv) = lax.optimization_barrier((held, crossed, weights))
+    parts = [*held, crossed, to_partner(crossed)]
+    tokens = size * hidden.shape[1]
+    normed, kv, cols = project(parts, gain, wk, wv, tokens)
+    kv_other = to_partner(kv)
+    q = query(normed, wq)
+    far, q, kv_other = lax.optimization_barrier((far, q, kv_other))
+    held += [far, to_partner(far)]
+    context = attend(q, kv, kv_other, held, size, retrieved.shape[2], cache.shape[2])
+    contexts = {0: context, 2: to_pair(context, 2), 1: to_pair(context, 1)}
+    contexts[3] = to_pair(contexts[2], 1)
+    contexts = [p for k in range(KV_HEADS) for p in (contexts[k], to_partner(contexts[k]))]
+    before = partial_branch(contexts[:4], w_out[0])
+    pieces = finish(contexts[4:], before, cols, w_out[0])
+    final = {}
+    for k in (3, 2, 1, 0):
         route = [
             (s * size + d, (s + 1) % sections * size + (d ^ (CORES * k)))
             for s in range(sections)
             for d in range(size)
         ]
-        final.append(lax.ppermute(piece, ("segment", "dev"), route))
-    return place_columns(place, final)
+        final[2 * k] = lax.ppermute(pieces[k], ("segment", "dev"), route)
+        final[2 * k + 1] = to_partner(final[2 * k])
+    return place_columns(final)
 
 
 def solution(mesh):

time: 87.3 us -> 70.9 us (0.81)
  local copies, waits for them, and re-layouts: 8.38 us -> 0.02 us
  waiting for transfers between devices: 39.2 us -> 32.1 us
  starting transfers between devices: 26.1 us -> 24 us
  Pallas kernels: 12.5 us -> 13.8 us
    unnamed x20 -> x6, local copies, waits for them, and re-layouts: 8.38 us -> 0.01 us
    ppermute x9 -> x7, waiting for transfers between devices: 27.8 us -> 23.3 us  [to_pair(): return lax.ppermute(x, 'dev', [(d, d ^ CORES * k) for d in range(size)])]
    pallas_call x1, Pallas kernels: 0.83 us -> 4.04 us  [load(): pl.pallas_call(functools.partial(load_kernel, len(arrays)), out_shape=[pl...]
    ppermute x14, starting transfers between devices: 3.33 us -> 1.26 us  [to_partner(): lax.ppermute(x, 'dev', [(d, d ^ 1) for d in range(lax.axis_size('dev'))])]
    ppermute x4, waiting for transfers between devices: 6.05 us -> 4.35 us  [by_head(): final[2 * k] = lax.ppermute(pieces[k], ('segment', 'dev'), route)]
    pallas_call x5 -> x6, Pallas kernels: 8.43 us -> 7.01 us  [the longest x1 1.54 us: query(): pl.pallas_call(query_kernel, out_shape=pltpu.VMEM((normed.shape[0], wq.sh...]
    ppermute x14, waiting for transfers between devices: 5.37 us -> 4.44 us  [to_partner(): lax.ppermute(x, 'dev', [(d, d ^ 1) for d in range(lax.axis_size('dev'))])]
    ppermute x9 -> x7, starting transfers between devices: 15.1 us -> 15 us  [to_pair(): return lax.ppermute(x, 'dev', [(d, d ^ CORES * k) for d in range(size)])]
  transfers between devices with their start and end apart: 27 -> 25, of which waited for: 10 -> 13; matrix products, arithmetic and copies ran while one was open for 0% -> 0% of each run, Pallas kernels for 6% -> 11%
where the time goes in v3:
time: 70.9 us; the launch traced here: 70.7 us
  waiting for transfers between devices  32.1 us (45%)
  starting transfers between devices  24 us (34%)
  Pallas kernels  13.8 us (19%)
  between operations  0.79 us (1%)
    ppermute x7, waiting for transfers between devices, to_pair(): return lax.ppermute(x, 'dev', [(d, d ^ CORES * k) for d in range(size)])  23.3 us
    ppermute x7, starting transfers between devices, to_pair(): return lax.ppermute(x, 'dev', [(d, d ^ CORES * k) for d in range(size)])  15 us
    ppermute x4, starting transfers between devices, by_head(): final[2 * k] = lax.ppermute(pieces[k], ('segment', 'dev'), route)  7.7 us
    ppermute x14, waiting for transfers between devices, to_partner(): lax.ppermute(x, 'dev', [(d, d ^ 1) for d in range(lax.axis_size('dev'))])  4.44 us
    ppermute x4, waiting for transfers between devices, by_head(): final[2 * k] = lax.ppermute(pieces[k], ('segment', 'dev'), route)  4.35 us
    pallas_call x1, Pallas kernels, load(): pl.pallas_call(functools.partial(load_kernel, len(arrays)), out_shape=[pl...  4.04 us
    pallas_call x1, Pallas kernels, attend(): pl.pallas_call(attend_kernel, out_shape=pltpu.VMEM(q.shape, jnp.bfloat16)...  2.79 us
    pallas_call x1, Pallas kernels, query(): pl.pallas_call(query_kernel, out_shape=pltpu.VMEM((normed.shape[0], wq.sh...  1.54 us
  transfers between devices with their start and end apart: 25, of which 13 were waited for; matrix products, arithmetic and copies ran while one was open for 0% of the time, Pallas kernels for 11%

profile of v3, /device:TPU:0, one launch (start us, length us, event | category | flops | bytes accessed | tf_op | source)
XLA Modules:
  0.0 70.7 jit_solution(877238594006171304)
XLA Ops:
  0.7 1.5 %pack.1 = (bf16[1552,128]{1,0:T(8,128)(2,1)S(1)}, bf16[1552,128]{1,0:T(8,128)(2,1)S(1)}, bf16[1552,128]{1,0:T(8,128)(2,1)S(1)}, bf16[1040,128]{1,0:T(8,128)(2,1)S(1)}) custom-call(s32[1,1]{1,0:T(1,128)S(6)} %copy.11.counts, s32[32]{0:T(128)} %table_in.1, s32[1,1,6]{2,1,0:T(1,128)} %retrieved_in.1, bf16[8,8192]{1,0:T(8,128)(2,1)} %bitcast.16, ...), custom_call_target="tpu_custom_call" | custom-call | tf_op jit(solution)/shard_map/pack/pallas_call | solution.py:271
  2.2 4.1 %collective-permute-start.4 = (bf16[1552,128]{1,0:T(8,128)(2,1)S(1)}, bf16[1552,128]{1,0:T(8,128)(2,1)S(1)}, u32[]{:S(2)}, u32[]{:S(2)}) collective-permute-start(bf16[1552,128]{1,0:T(8,128)(2,1)S(1)} %get-tuple-element.39), channel_id=1, source_target_pairs={{0,4},{1,5},{2,6},{3,7},{4,0},{5,1},{6,2},{7,3},{8,12},{9,13},{10,... | collective-permute-start | bytes 1191944 | tf_op jit(solution)/shard_map/ppermute | solution.py:160
  6.3 1.6 %collective-permute-start.2 = (bf16[1552,128]{1,0:T(8,128)(2,1)S(1)}, bf16[1552,128]{1,0:T(8,128)(2,1)S(1)}, u32[]{:S(2)}, u32[]{:S(2)}) collective-permute-start(bf16[1552,128]{1,0:T(8,128)(2,1)S(1)} %get-tuple-element.38), channel_id=1, source_target_pairs={{0,2},{1,3},{2,0},{3,1},{4,6},{5,7},{6,4},{7,5},{8,10},{9,11},{10,... | collective-permute-start | bytes 1191944 | tf_op jit(solution)/shard_map/ppermute | solution.py:160
  7.9 4.0 %load.1 = (bf16[8192,512]{1,0:T(8,128)(2,1)S(1)}, bf16[64,8192]{1,0:T(8,128)(2,1)S(1)}, bf16[64,8192]{1,0:T(8,128)(2,1)S(1)}) custom-call(bf16[1,8192,512]{2,1,0:T(8,128)(2,1)} %refs_0_.1, bf16[64,8192]{1,0:T(8,128)(2,1)} %bitcast.14, bf16[64,8192]{1,0:T(8,128)(2,1)} %bitcast.15), custom_call_target="tpu_custom_call" | custom-call | tf_op jit(solution)/shard_map/load/pallas_call | solution.py:206
  11.9 12.2 %collective-permute-done.4.refs_4_ = bf16[1552,128]{1,0:T(8,128)(2,1)S(1)} collective-permute-done((bf16[1552,128]{1,0:T(8,128)(2,1)S(1)}, bf16[1552,128]{1,0:T(8,128)(2,1)S(1)}, u32[]{:S(2)}, u32[]{:S(2)}) %collective-permute-start.4) | collective-permute-done | bytes 397344 | tf_op jit(solution)/shard_map/ppermute | solution.py:160
  24.3 0.5 collective-permute-start.5
  24.8 1.6 %collective-permute-start.6 = (bf16[512,128]{1,0:T(8,128)(2,1)S(1)}, bf16[512,128]{1,0:T(8,128)(2,1)S(1)}, u32[]{:S(2)}, u32[]{:S(2)}) collective-permute-start(bf16[512,128]{1,0:T(8,128)(2,1)S(1)} %slice.3), channel_id=1, source_target_pairs={{0,2},{1,3},{2,0},{3,1},{4,6},{5,7},{6,4},{7,5},{8,10},{9,11},{10,... | collective-permute-start | bytes 393224 | tf_op jit(solution)/shard_map/ppermute | solution.py:160
  26.4 1.8 %collective-permute-start = (bf16[1040,128]{1,0:T(8,128)(2,1)S(1)}, bf16[1040,128]{1,0:T(8,128)(2,1)S(1)}, u32[]{:S(2)}, u32[]{:S(2)}) collective-permute-start(bf16[1040,128]{1,0:T(8,128)(2,1)S(1)} %get-tuple-element.36), channel_id=1, source_target_pairs={{0,6},{1,7},{2,4},{3,5},{4,2},{5,3},{6,0},{7,1},{8,14},{9,15},{10,... | collective-permute-start | bytes 798728 | tf_op jit(solution)/shard_map/ppermute | solution.py:160
  28.2 2.1 %collective-permute-done.6.refs_6_ = bf16[512,128]{1,0:T(8,128)(2,1)S(1)} collective-permute-done((bf16[512,128]{1,0:T(8,128)(2,1)S(1)}, bf16[512,128]{1,0:T(8,128)(2,1)S(1)}, u32[]{:S(2)}, u32[]{:S(2)}) %collective-permute-start.6) | collective-permute-done | bytes 131104 | tf_op jit(solution)/shard_map/ppermute | solution.py:160
  30.3 1.3 %collective-permute-done.7.refs_7_ = bf16[512,128]{1,0:T(8,128)(2,1)S(1)} collective-permute-done((bf16[512,128]{1,0:T(8,128)(2,1)S(1)}, bf16[512,128]{1,0:T(8,128)(2,1)S(1)}, u32[]{:S(2)}, u32[]{:S(2)}) %collective-permute-start.7) | collective-permute-done | bytes 131104 | tf_op jit(solution)/shard_map/ppermute | solution.py:164
  31.7 1.5 %project.1 = (bf16[64,8192]{1,0:T(8,128)(2,1)S(1)}, bf16[64,128]{1,0:T(8,128)(2,1)S(1)}, bf16[64,1024]{1,0:T(8,128)(2,1)S(1)}) custom-call(bf16[1552,128]{1,0:T(8,128)(2,1)S(1)} %get-tuple-element.47.refs_0_, bf16[1552,128]{1,0:T(8,128)(2,1)S(1)} %collective-permute-done.1.refs_1_, bf16[1552,128]{1,0:T(8,128)(2,1)S(1)} %collective-permute-done.2.refs_2_, ...), custom_call_target="tpu_custom_call" | custom-call | tf_op jit(solution)/shard_map/project/pallas_call | solution.py:335
  33.4 1.5 %query.1.q = bf16[64,512]{1,0:T(8,128)(2,1)S(1)} custom-call(bf16[64,8192]{1,0:T(8,128)(2,1)S(1)} %get-tuple-element.56.normed, bf16[8192,512]{1,0:T(8,128)(2,1)S(1)} %get-tuple-element.57.wq), custom_call_target="tpu_custom_call" | custom-call | tf_op jit(solution)/shard_map/query/pallas_call | solution.py:355
  35.0 2.7 %collective-permute-done.refs_6_ = bf16[1040,128]{1,0:T(8,128)(2,1)S(1)} collective-permute-done((bf16[1040,128]{1,0:T(8,128)(2,1)S(1)}, bf16[1040,128]{1,0:T(8,128)(2,1)S(1)}, u32[]{:S(2)}, u32[]{:S(2)}) %collective-permute-start) | collective-permute-done | bytes 266272 | tf_op jit(solution)/shard_map/ppermute | solution.py:160
  37.7 1.5 %collective-permute-done.9.refs_7_ = bf16[1040,128]{1,0:T(8,128)(2,1)S(1)} collective-permute-done((bf16[1040,128]{1,0:T(8,128)(2,1)S(1)}, bf16[1040,128]{1,0:T(8,128)(2,1)S(1)}, u32[]{:S(2)}, u32[]{:S(2)}) %collective-permute-start.9) | collective-permute-done | bytes 266272 | tf_op jit(solution)/shard_map/ppermute | solution.py:164
  39.2 2.8 %attend.1.refs_0_ = bf16[64,512]{1,0:T(8,128)(2,1)S(1)} custom-call(bf16[64,512]{1,0:T(8,128)(2,1)S(1)} %query.1.q, bf16[64,128]{1,0:T(8,128)(2,1)S(1)} %get-tuple-element.58.kv_mine, bf16[64,128]{1,0:T(8,128)(2,1)S(1)} %collective-permute-done.8.kv_other, bf16[1552,128]{1,0:T(8,128)(2,1)S(1)} %get-tuple-element.47.refs_0_, ...), custom_call_target="tpu_custom_call" | custom-call | flops 268435456 | bytes 2097152 | tf_op jit(solution)/shard_map/attend/pallas_call | solution.py:464
  42.0 4.9 %collective-permute-start.10 = (bf16[64,512]{1,0:T(8,128)(2,1)S(1)}, bf16[64,512]{1,0:T(8,128)(2,1)S(1)}, u32[]{:S(2)}, u32[]{:S(2)}) collective-permute-start(bf16[64,512]{1,0:T(8,128)(2,1)S(1)} %attend.1.refs_0_), channel_id=1, source_target_pairs={{0,4},{1,5},{2,6},{3,7},{4,0},{5,1},{6,2},{7,3},{8,12},{9,13},{10,... | collective-permute-start | bytes 196616 | tf_op jit(solution)/shard_map/ppermute | solution.py:160
  46.9 3.5 %collective-permute-done.10.refs_0_ = bf16[64,512]{1,0:T(8,128)(2,1)S(1)} collective-permute-done((bf16[64,512]{1,0:T(8,128)(2,1)S(1)}, bf16[64,512]{1,0:T(8,128)(2,1)S(1)}, u32[]{:S(2)}, u32[]{:S(2)}) %collective-permute-start.10) | collective-permute-done | bytes 65568 | tf_op jit(solution)/shard_map/ppermute | solution.py:160
  50.3 1.1 %collective-permute-start.12 = (bf16[64,512]{1,0:T(8,128)(2,1)S(1)}, bf16[64,512]{1,0:T(8,128)(2,1)S(1)}, u32[]{:S(2)}, u32[]{:S(2)}) collective-permute-start(bf16[64,512]{1,0:T(8,128)(2,1)S(1)} %collective-permute-done.10.refs_0_), channel_id=1, source_target_pairs={{0,2},{1,3},{2,0},{3,1},{4,6},{5,7},{6,4},{7,5},{8,10},{9,11},{10,... | collective-permute-start | bytes 196616 | tf_op jit(solution)/shard_map/ppermute | solution.py:160
  51.4 0.5 collective-permute-start.16
  51.9 2.7 %collective-permute-done.12.refs_2_ = bf16[64,512]{1,0:T(8,128)(2,1)S(1)} collective-permute-done((bf16[64,512]{1,0:T(8,128)(2,1)S(1)}, bf16[64,512]{1,0:T(8,128)(2,1)S(1)}, u32[]{:S(2)}, u32[]{:S(2)}) %collective-permute-start.12) | collective-permute-done | bytes 65568 | tf_op jit(solution)/shard_map/ppermute | solution.py:160
  54.6 0.9 %partial.1.refs_4_ = f32[64,1024]{1,0:T(8,128)S(1)} custom-call(bf16[64,512]{1,0:T(8,128)(2,1)S(1)} %attend.1.refs_0_, bf16[64,512]{1,0:T(8,128)(2,1)S(1)} %collective-permute-done.14.refs_1_, bf16[64,512]{1,0:T(8,128)(2,1)S(1)} %collective-permute-done.15.refs_2_, bf16[64,512]{1,0:T(8,128)(2,1)S(1)} %collective-permute-done.16.refs_3_, ...), custom_call_target="tpu_custom_call" | custom-call | flops 268435456 | bytes 4194304 | tf_op jit(solution)/shard_map/partial/pallas_call | solution.py:502
  55.5 0.4 collective-permute-done.13.refs_3_
  55.9 0.9 %finish.1 = (bf16[16,1024]{1,0:T(8,128)(2,1)S(1)}, bf16[16,1024]{1,0:T(8,128)(2,1)S(1)}, bf16[16,1024]{1,0:T(8,128)(2,1)S(1)}, bf16[16,1024]{1,0:T(8,128)(2,1)S(1)}) custom-call(bf16[64,512]{1,0:T(8,128)(2,1)S(1)} %collective-permute-done.10.refs_0_, bf16[64,512]{1,0:T(8,128)(2,1)S(1)} %collective-permute-done.11.refs_1_, ...), custom_call_target="tpu_custom_call" | custom-call | flops 268435456 | bytes 4194304 | tf_op jit(solution)/shard_map/finish/pallas_call | solution.py:535
  56.7 2.7 %collective-permute-start.17 = (bf16[16,1024]{1,0:T(8,128)(2,1)S(1)}, bf16[16,1024]{1,0:T(8,128)(2,1)S(1)}, u32[]{:S(2)}, u32[]{:S(2)}) collective-permute-start(bf16[16,1024]{1,0:T(8,128)(2,1)S(1)} %get-tuple-element.63), channel_id=1, source_target_pairs={{0,14},{1,15},{2,12},{3,13},{4,10},{5,11},{6,8},{7,9},{8,22},{9,23... | collective-permute-start | bytes 98312 | tf_op jit(solution)/shard_map/ppermute | solution.py:602
  59.4 1.8 %collective-permute-start.19 = (bf16[16,1024]{1,0:T(8,128)(2,1)S(1)}, bf16[16,1024]{1,0:T(8,128)(2,1)S(1)}, u32[]{:S(2)}, u32[]{:S(2)}) collective-permute-start(bf16[16,1024]{1,0:T(8,128)(2,1)S(1)} %get-tuple-element.64), channel_id=1, source_target_pairs={{0,12},{1,13},{2,14},{3,15},{4,8},{5,9},{6,10},{7,11},{8,20},{9,21... | collective-permute-start | bytes 98312 | tf_op jit(solution)/shard_map/ppermute | solution.py:602
  61.2 2.8 %collective-permute-start.21 = (bf16[16,1024]{1,0:T(8,128)(2,1)S(1)}, bf16[16,1024]{1,0:T(8,128)(2,1)S(1)}, u32[]{:S(2)}, u32[]{:S(2)}) collective-permute-start(bf16[16,1024]{1,0:T(8,128)(2,1)S(1)} %get-tuple-element.65), channel_id=1, source_target_pairs={{0,10},{1,11},{2,8},{3,9},{4,14},{5,15},{6,12},{7,13},{8,18},{9,19... | collective-permute-start | bytes 98312 | tf_op jit(solution)/shard_map/ppermute | solution.py:602
  64.0 0.5 collective-permute-start.23
  64.4 1.6 %collective-permute-done.19.refs_3_ = bf16[16,1024]{1,0:T(8,128)(2,1)S(1)} collective-permute-done((bf16[16,1024]{1,0:T(8,128)(2,1)S(1)}, bf16[16,1024]{1,0:T(8,128)(2,1)S(1)}, u32[]{:S(2)}, u32[]{:S(2)}) %collective-permute-start.19) | collective-permute-done | bytes 32800 | tf_op jit(solution)/shard_map/ppermute | solution.py:602
  66.0 0.9 %collective-permute-done.21.refs_5_ = bf16[16,1024]{1,0:T(8,128)(2,1)S(1)} collective-permute-done((bf16[16,1024]{1,0:T(8,128)(2,1)S(1)}, bf16[16,1024]{1,0:T(8,128)(2,1)S(1)}, u32[]{:S(2)}, u32[]{:S(2)}) %collective-permute-start.21) | collective-permute-done | bytes 32800 | tf_op jit(solution)/shard_map/ppermute | solution.py:602
  66.9 1.9 %collective-permute-done.23.refs_7_ = bf16[16,1024]{1,0:T(8,128)(2,1)S(1)} collective-permute-done((bf16[16,1024]{1,0:T(8,128)(2,1)S(1)}, bf16[16,1024]{1,0:T(8,128)(2,1)S(1)}, u32[]{:S(2)}, u32[]{:S(2)}) %collective-permute-start.23) | collective-permute-done | bytes 32800 | tf_op jit(solution)/shard_map/ppermute | solution.py:602
  68.8 1.2 %collective-permute-done.24.refs_6_ = bf16[16,1024]{1,0:T(8,128)(2,1)S(1)} collective-permute-done((bf16[16,1024]{1,0:T(8,128)(2,1)S(1)}, bf16[16,1024]{1,0:T(8,128)(2,1)S(1)}, u32[]{:S(2)}, u32[]{:S(2)}) %collective-permute-start.24) | collective-permute-done | bytes 32800 | tf_op jit(solution)/shard_map/ppermute | solution.py:164
  70.0 0.7 place.1
  (34 shorter events, 0.5 us)
Async XLA Ops:
  0.0 31.7 %copy-start = (f32[1,8192]{1,0:T(1,128)S(1)}, f32[1,8192]{1,0:T(1,128)}, u32[]{:S(2)}) copy-start(f32[1,8192]{1,0:T(1,128)} %param.11) | copy-start | bytes 98308
  2.2 21.9 %collective-permute-start.4 = (bf16[1552,128]{1,0:T(8,128)(2,1)S(1)}, bf16[1552,128]{1,0:T(8,128)(2,1)S(1)}, u32[]{:S(2)}, u32[]{:S(2)}) collective-permute-start(bf16[1552,128]{1,0:T(8,128)(2,1)S(1)} %get-tuple-element.39), channel_id=1, source_target_pairs={{0,4},{1,5},{2,6},{3,7},{4,0},{5,1},{6,2},{7,3},{8,12},{9,13},{10,... | collective-permute-start | bytes 1191944 | tf_op jit(solution)/shard_map/ppermute | solution.py:160
  6.3 18.0 %collective-permute-start.2 = (bf16[1552,128]{1,0:T(8,128)(2,1)S(1)}, bf16[1552,128]{1,0:T(8,128)(2,1)S(1)}, u32[]{:S(2)}, u32[]{:S(2)}) collective-permute-start(bf16[1552,128]{1,0:T(8,128)(2,1)S(1)} %get-tuple-element.38), channel_id=1, source_target_pairs={{0,2},{1,3},{2,0},{3,1},{4,6},{5,7},{6,4},{7,5},{8,10},{9,11},{10,... | collective-permute-start | bytes 1191944 | tf_op jit(solution)/shard_map/ppermute | solution.py:160
  7.9 20.4 %collective-permute-start.1 = (bf16[1552,128]{1,0:T(8,128)(2,1)S(1)}, bf16[1552,128]{1,0:T(8,128)(2,1)S(1)}, u32[]{:S(2)}, u32[]{:S(2)}) collective-permute-start(bf16[1552,128]{1,0:T(8,128)(2,1)S(1)} %get-tuple-element.47.refs_0_), channel_id=1, source_target_pairs={{0,1},{1,0},{2,3},{3,2},{4,5},{5,4},{6,7},{7,6},{8,9},{9,8},{10,11... | collective-permute-start | bytes 1191944 | tf_op jit(solution)/shard_map/ppermute | solution.py:164
  24.3 6.0 %collective-permute-start.3 = (bf16[1552,128]{1,0:T(8,128)(2,1)S(1)}, bf16[1552,128]{1,0:T(8,128)(2,1)S(1)}, u32[]{:S(2)}, u32[]{:S(2)}) collective-permute-start(bf16[1552,128]{1,0:T(8,128)(2,1)S(1)} %collective-permute-done.2.refs_2_), channel_id=1, source_target_pairs={{0,1},{1,0},{2,3},{3,2},{4,5},{5,4},{6,7},{7,6},{8,9},{9,8},{10,11... | collective-permute-start | bytes 1191944 | tf_op jit(solution)/shard_map/ppermute | solution.py:164
  24.3 6.0 %collective-permute-start.5 = (bf16[1552,128]{1,0:T(8,128)(2,1)S(1)}, bf16[1552,128]{1,0:T(8,128)(2,1)S(1)}, u32[]{:S(2)}, u32[]{:S(2)}) collective-permute-start(bf16[1552,128]{1,0:T(8,128)(2,1)S(1)} %collective-permute-done.4.refs_4_), channel_id=1, source_target_pairs={{0,1},{1,0},{2,3},{3,2},{4,5},{5,4},{6,7},{7,6},{8,9},{9,8},{10,11... | collective-permute-start | bytes 1191944 | tf_op jit(solution)/shard_map/ppermute | solution.py:164
  24.8 5.5 %collective-permute-start.6 = (bf16[512,128]{1,0:T(8,128)(2,1)S(1)}, bf16[512,128]{1,0:T(8,128)(2,1)S(1)}, u32[]{:S(2)}, u32[]{:S(2)}) collective-permute-start(bf16[512,128]{1,0:T(8,128)(2,1)S(1)} %slice.3), channel_id=1, source_target_pairs={{0,2},{1,3},{2,0},{3,1},{4,6},{5,7},{6,4},{7,5},{8,10},{9,11},{10,... | collective-permute-start | bytes 393224 | tf_op jit(solution)/shard_map/ppermute | solution.py:160
  26.4 11.2 %collective-permute-start = (bf16[1040,128]{1,0:T(8,128)(2,1)S(1)}, bf16[1040,128]{1,0:T(8,128)(2,1)S(1)}, u32[]{:S(2)}, u32[]{:S(2)}) collective-permute-start(bf16[1040,128]{1,0:T(8,128)(2,1)S(1)} %get-tuple-element.36), channel_id=1, source_target_pairs={{0,6},{1,7},{2,4},{3,5},{4,2},{5,3},{6,0},{7,1},{8,14},{9,15},{10,... | collective-permute-start | bytes 798728 | tf_op jit(solution)/shard_map/ppermute | solution.py:160
  30.3 1.4 %collective-permute-start.7 = (bf16[512,128]{1,0:T(8,128)(2,1)S(1)}, bf16[512,128]{1,0:T(8,128)(2,1)S(1)}, u32[]{:S(2)}, u32[]{:S(2)}) collective-permute-start(bf16[512,128]{1,0:T(8,128)(2,1)S(1)} %collective-permute-done.6.refs_6_), channel_id=1, source_target_pairs={{0,1},{1,0},{2,3},{3,2},{4,5},{5,4},{6,7},{7,6},{8,9},{9,8},{10,11... | collective-permute-start | bytes 393224 | tf_op jit(solution)/shard_map/ppermute | solution.py:164
  31.7 22.9 %slice-start = ((s8[8388608]{0:T(1024)(128)(4,1)}), s8[4194304]{0:T(1024)(128)(4,1)S(1)}, s32[]{:S(2)}) async-start(s8[8388608]{0:T(1024)(128)(4,1)} %bitcast.9), calls=%async_computation | async-start | bytes 8388608
  33.2 4.4 %collective-permute-start.8 = (bf16[64,128]{1,0:T(8,128)(2,1)S(1)}, bf16[64,128]{1,0:T(8,128)(2,1)S(1)}, u32[]{:S(2)}, u32[]{:S(2)}) collective-permute-start(bf16[64,128]{1,0:T(8,128)(2,1)S(1)} %get-tuple-element.58.kv_mine), channel_id=1, source_target_pairs={{0,1},{1,0},{2,3},{3,2},{4,5},{5,4},{6,7},{7,6},{8,9},{9,8},{10,11... | collective-permute-start | bytes 49160 | tf_op jit(solution)/shard_map/ppermute | solution.py:164
  33.4 21.2 %slice-start.1 = ((s8[8388608]{0:T(1024)(128)(4,1)}), s8[4194304]{0:T(1024)(128)(4,1)S(1)}, s32[]{:S(2)}) async-start(s8[8388608]{0:T(1024)(128)(4,1)} %bitcast.9), calls=%async_computation.1 | async-start | bytes 8388608
  37.6 1.5 %collective-permute-start.9 = (bf16[1040,128]{1,0:T(8,128)(2,1)S(1)}, bf16[1040,128]{1,0:T(8,128)(2,1)S(1)}, u32[]{:S(2)}, u32[]{:S(2)}) collective-permute-start(bf16[1040,128]{1,0:T(8,128)(2,1)S(1)} %collective-permute-done.refs_6_), channel_id=1, source_target_pairs={{0,1},{1,0},{2,3},{3,2},{4,5},{5,4},{6,7},{7,6},{8,9},{9,8},{10,11... | collective-permute-start | bytes 798728 | tf_op jit(solution)/shard_map/ppermute | solution.py:164
  42.0 8.4 %collective-permute-start.10 = (bf16[64,512]{1,0:T(8,128)(2,1)S(1)}, bf16[64,512]{1,0:T(8,128)(2,1)S(1)}, u32[]{:S(2)}, u32[]{:S(2)}) collective-permute-start(bf16[64,512]{1,0:T(8,128)(2,1)S(1)} %attend.1.refs_0_), channel_id=1, source_target_pairs={{0,4},{1,5},{2,6},{3,7},{4,0},{5,1},{6,2},{7,3},{8,12},{9,13},{10,... | collective-permute-start | bytes 196616 | tf_op jit(solution)/shard_map/ppermute | solution.py:160
  46.9 4.6 %collective-permute-start.15 = (bf16[64,512]{1,0:T(8,128)(2,1)S(1)}, bf16[64,512]{1,0:T(8,128)(2,1)S(1)}, u32[]{:S(2)}, u32[]{:S(2)}) collective-permute-start(bf16[64,512]{1,0:T(8,128)(2,1)S(1)} %attend.1.refs_0_), channel_id=1, source_target_pairs={{0,2},{1,3},{2,0},{3,1},{4,6},{5,7},{6,4},{7,5},{8,10},{9,11},{10,... | collective-permute-start | bytes 196616 | tf_op jit(solution)/shard_map/ppermute | solution.py:160
  50.3 4.3 %collective-permute-start.12 = (bf16[64,512]{1,0:T(8,128)(2,1)S(1)}, bf16[64,512]{1,0:T(8,128)(2,1)S(1)}, u32[]{:S(2)}, u32[]{:S(2)}) collective-permute-start(bf16[64,512]{1,0:T(8,128)(2,1)S(1)} %collective-permute-done.10.refs_0_), channel_id=1, source_target_pairs={{0,2},{1,3},{2,0},{3,1},{4,6},{5,7},{6,4},{7,5},{8,10},{9,11},{10,... | collective-permute-start | bytes 196616 | tf_op jit(solution)/shard_map/ppermute | solution.py:160
  51.4 3.2 %collective-permute-start.14 = (bf16[64,512]{1,0:T(8,128)(2,1)S(1)}, bf16[64,512]{1,0:T(8,128)(2,1)S(1)}, u32[]{:S(2)}, u32[]{:S(2)}) collective-permute-start(bf16[64,512]{1,0:T(8,128)(2,1)S(1)} %attend.1.refs_0_), channel_id=1, source_target_pairs={{0,1},{1,0},{2,3},{3,2},{4,5},{5,4},{6,7},{7,6},{8,9},{9,8},{10,11... | collective-permute-start | bytes 196616 | tf_op jit(solution)/shard_map/ppermute | solution.py:164
  51.4 3.2 %collective-permute-start.16 = (bf16[64,512]{1,0:T(8,128)(2,1)S(1)}, bf16[64,512]{1,0:T(8,128)(2,1)S(1)}, u32[]{:S(2)}, u32[]{:S(2)}) collective-permute-start(bf16[64,512]{1,0:T(8,128)(2,1)S(1)} %collective-permute-done.15.refs_2_), channel_id=1, source_target_pairs={{0,1},{1,0},{2,3},{3,2},{4,5},{5,4},{6,7},{7,6},{8,9},{9,8},{10,11... | collective-permute-start | bytes 196616 | tf_op jit(solution)/shard_map/ppermute | solution.py:164
  51.9 3.6 %collective-permute-start.11 = (bf16[64,512]{1,0:T(8,128)(2,1)S(1)}, bf16[64,512]{1,0:T(8,128)(2,1)S(1)}, u32[]{:S(2)}, u32[]{:S(2)}) collective-permute-start(bf16[64,512]{1,0:T(8,128)(2,1)S(1)} %collective-permute-done.10.refs_0_), channel_id=1, source_target_pairs={{0,1},{1,0},{2,3},{3,2},{4,5},{5,4},{6,7},{7,6},{8,9},{9,8},{10,11... | collective-permute-start | bytes 196616 | tf_op jit(solution)/shard_map/ppermute | solution.py:164
  54.6 1.3 %collective-permute-start.13 = (bf16[64,512]{1,0:T(8,128)(2,1)S(1)}, bf16[64,512]{1,0:T(8,128)(2,1)S(1)}, u32[]{:S(2)}, u32[]{:S(2)}) collective-permute-start(bf16[64,512]{1,0:T(8,128)(2,1)S(1)} %collective-permute-done.12.refs_2_), channel_id=1, source_target_pairs={{0,1},{1,0},{2,3},{3,2},{4,5},{5,4},{6,7},{7,6},{8,9},{9,8},{10,11... | collective-permute-start | bytes 196616 | tf_op jit(solution)/shard_map/ppermute | solution.py:164
  56.7 7.7 %collective-permute-start.17 = (bf16[16,1024]{1,0:T(8,128)(2,1)S(1)}, bf16[16,1024]{1,0:T(8,128)(2,1)S(1)}, u32[]{:S(2)}, u32[]{:S(2)}) collective-permute-start(bf16[16,1024]{1,0:T(8,128)(2,1)S(1)} %get-tuple-element.63), channel_id=1, source_target_pairs={{0,14},{1,15},{2,12},{3,13},{4,10},{5,11},{6,8},{7,9},{8,22},{9,23... | collective-permute-start | bytes 98312 | tf_op jit(solution)/shard_map/ppermute | solution.py:602
  59.4 6.6 %collective-permute-start.19 = (bf16[16,1024]{1,0:T(8,128)(2,1)S(1)}, bf16[16,1024]{1,0:T(8,128)(2,1)S(1)}, u32[]{:S(2)}, u32[]{:S(2)}) collective-permute-start(bf16[16,1024]{1,0:T(8,128)(2,1)S(1)} %get-tuple-element.64), channel_id=1, source_target_pairs={{0,12},{1,13},{2,14},{3,15},{4,8},{5,9},{6,10},{7,11},{8,20},{9,21... | collective-permute-start | bytes 98312 | tf_op jit(solution)/shard_map/ppermute | solution.py:602
  61.2 5.7 %collective-permute-start.21 = (bf16[16,1024]{1,0:T(8,128)(2,1)S(1)}, bf16[16,1024]{1,0:T(8,128)(2,1)S(1)}, u32[]{:S(2)}, u32[]{:S(2)}) collective-permute-start(bf16[16,1024]{1,0:T(8,128)(2,1)S(1)} %get-tuple-element.65), channel_id=1, source_target_pairs={{0,10},{1,11},{2,8},{3,9},{4,14},{5,15},{6,12},{7,13},{8,18},{9,19... | collective-permute-start | bytes 98312 | tf_op jit(solution)/shard_map/ppermute | solution.py:602
  64.0 4.8 %collective-permute-start.23 = (bf16[16,1024]{1,0:T(8,128)(2,1)S(1)}, bf16[16,1024]{1,0:T(8,128)(2,1)S(1)}, u32[]{:S(2)}, u32[]{:S(2)}) collective-permute-start(bf16[16,1024]{1,0:T(8,128)(2,1)S(1)} %get-tuple-element.66), channel_id=1, source_target_pairs={{0,8},{1,9},{2,10},{3,11},{4,12},{5,13},{6,14},{7,15},{8,16},{9,17... | collective-permute-start | bytes 98312 | tf_op jit(solution)/shard_map/ppermute | solution.py:602
  64.4 4.4 %collective-permute-start.18 = (bf16[16,1024]{1,0:T(8,128)(2,1)S(1)}, bf16[16,1024]{1,0:T(8,128)(2,1)S(1)}, u32[]{:S(2)}, u32[]{:S(2)}) collective-permute-start(bf16[16,1024]{1,0:T(8,128)(2,1)S(1)} %collective-permute-done.17.refs_1_), channel_id=1, source_target_pairs={{0,1},{1,0},{2,3},{3,2},{4,5},{5,4},{6,7},{7,6},{8,9},{9,8},{10,11... | collective-permute-start | bytes 98312 | tf_op jit(solution)/shard_map/ppermute | solution.py:164
  66.0 2.8 %collective-permute-start.20 = (bf16[16,1024]{1,0:T(8,128)(2,1)S(1)}, bf16[16,1024]{1,0:T(8,128)(2,1)S(1)}, u32[]{:S(2)}, u32[]{:S(2)}) collective-permute-start(bf16[16,1024]{1,0:T(8,128)(2,1)S(1)} %collective-permute-done.19.refs_3_), channel_id=1, source_target_pairs={{0,1},{1,0},{2,3},{3,2},{4,5},{5,4},{6,7},{7,6},{8,9},{9,8},{10,11... | collective-permute-start | bytes 98312 | tf_op jit(solution)/shard_map/ppermute | solution.py:164
  66.9 1.9 %collective-permute-start.22 = (bf16[16,1024]{1,0:T(8,128)(2,1)S(1)}, bf16[16,1024]{1,0:T(8,128)(2,1)S(1)}, u32[]{:S(2)}, u32[]{:S(2)}) collective-permute-start(bf16[16,1024]{1,0:T(8,128)(2,1)S(1)} %collective-permute-done.21.refs_5_), channel_id=1, source_target_pairs={{0,1},{1,0},{2,3},{3,2},{4,5},{5,4},{6,7},{7,6},{8,9},{9,8},{10,11... | collective-permute-start | bytes 98312 | tf_op jit(solution)/shard_map/ppermute | solution.py:164
  68.8 1.2 %collective-permute-start.24 = (bf16[16,1024]{1,0:T(8,128)(2,1)S(1)}, bf16[16,1024]{1,0:T(8,128)(2,1)S(1)}, u32[]{:S(2)}, u32[]{:S(2)}) collective-permute-start(bf16[16,1024]{1,0:T(8,128)(2,1)S(1)} %collective-permute-done.23.refs_7_), channel_id=1, source_target_pairs={{0,1},{1,0},{2,3},{3,2},{4,5},{5,4},{6,7},{7,6},{8,9},{9,8},{10,11... | collective-permute-start | bytes 98312 | tf_op jit(solution)/shard_map/ppermute | solution.py:164

commit v4 on v3

--- a/solution.py
+++ b/solution.py
@@ -147,7 +147,6 @@
 
 CORES = 2
 TAIL = 16
-LANES = 128
 VMEM = pl.BlockSpec(memory_space=pltpu.VMEM)
 SMEM = pl.BlockSpec(memory_space=pltpu.SMEM)
 ANYWHERE = pl.BlockSpec(memory_space=pl.ANY)
@@ -215,21 +214,22 @@
     )(*[pltpu.with_memory_space_constraint(a, pltpu.HBM) for a in arrays])
 
 
-def pack_kernel(counts, table_in, retrieved_in, state_in, cache, *rest):
-    outs, (whole, state, table, retrieved, sems, list_sems) = rest[:KV_HEADS], rest[KV_HEADS:]
-    _, pair, _ = my_place()
+def pack_kernel(counts, table_in, retrieved_in, cache, *rest):
+    outs, (whole, table, retrieved, sems, list_sems) = rest[:-5], rest[-5:]
     lists = [
         pltpu.make_async_copy(source, target, list_sems.at[i])
         for i, (source, target) in enumerate(
-            ((table_in, table), (retrieved_in, retrieved), (state_in, state))
+            ((table_in, table), (retrieved_in, retrieved))
         )
     ]
+    for copy in lists:
+        copy.start()
     lines, tokens = whole.shape[0], whole.shape[1]
     width = whole.shape[2] // 2
     copies = [
         pltpu.make_async_copy(cache.at[0, line], whole.at[line], sems.at[line]) for line in range(lines)
     ]
-    for copy in lists + copies:
+    for copy in copies:
         copy.start()
     for copy in lists:
         copy.wait()
@@ -239,98 +239,66 @@
     for k in range(listed):
         note = jnp.where(lane == k, table[retrieved[0, 0, k]], note)
     note = note.astype(jnp.float32).astype(jnp.bfloat16)
-    end = lines * 2 * tokens
     for out in outs:
-        out[end : end + TAIL, :] = note
-    rows = state.shape[0]
-    for t in range(state.shape[1] // LANES // 2):
-        tile = jnp.concatenate(
-            [
-                state[:, i * LANES : (i + 1) * LANES].astype(jnp.float32)
-                for i in (2 * t, 2 * t + 1)
-            ],
-            axis=0,
-        ).astype(jnp.bfloat16)
-        at = end + TAIL + 2 * rows * t
-        for out in outs[:-1]:
-            out[at : at + 2 * rows, :] = tile
+        out[lines * 2 * tokens :, :] = note
     for line in range(lines):
         copies[line].wait()
         for k, out in enumerate(outs):
-            head = lax.bitwise_xor(pair, k)
+            head = lax.bitwise_xor(my_place()[1], k)
             for part in range(2):
                 columns = pl.ds(pl.multiple_of(part * width + head * HEAD_DIM, HEAD_DIM), HEAD_DIM)
                 at = (line * 2 + part) * tokens
                 out[at : at + tokens, :] = whole[line, :, columns]
 
 
-def pack(table, retrieved, counts, state, cache):
+def pack(table, retrieved, counts, cache):
     rows, tokens = cache.shape[1], cache.shape[2]
-    short = rows * 2 * tokens + TAIL
-    long = short + state.size // HEAD_DIM
     return pl.pallas_call(
         pack_kernel,
-        out_shape=[
-            pltpu.VMEM((long if k < KV_HEADS - 1 else short, HEAD_DIM), cache.dtype)
-            for k in range(KV_HEADS)
-        ],
-        in_specs=[SMEM] + [HBM] * 4,
+        out_shape=[pltpu.VMEM((rows * 2 * tokens + TAIL, HEAD_DIM), cache.dtype)] * KV_HEADS,
+        in_specs=[SMEM] + [HBM] * 3,
         out_specs=[VMEM] * KV_HEADS,
         scratch_shapes=[
             pltpu.VMEM(cache.shape[1:], cache.dtype),
-            pltpu.VMEM(state.shape, state.dtype),
             pltpu.SMEM(table.shape, table.dtype),
             pltpu.SMEM(retrieved.shape, retrieved.dtype),
             pltpu.SemaphoreType.DMA((rows,)),
-            pltpu.SemaphoreType.DMA((3,)),
+            pltpu.SemaphoreType.DMA((2,)),
         ],
         compiler_params=pltpu.CompilerParams(vmem_limit_bytes=6 * MIB),
         cost_estimate=pl.CostEstimate(flops=0, bytes_accessed=0, transcendentals=0),
         name="pack",
-    )(counts, *[pltpu.with_memory_space_constraint(a, pltpu.HBM) for a in (table, retrieved, state, cache)])
+    )(counts, *[pltpu.with_memory_space_constraint(a, pltpu.HBM) for a in (table, retrieved, cache)])
 
 
 def project_kernel(*refs):
     count = 2 * KV_HEADS
     parts, rest = refs[:count], refs[count:]
     gain, wk, wv, normed, kv_out, cols_out = rest
-    me, pair, core = my_place()
+    _, pair, core = my_place()
     first = core == 0
-    tiles = gain.shape[0]
-    rows = normed.shape[0] // count
-    mine = cols_out.shape[1] // LANES
+    width = cols_out.shape[1]
+    columns = pl.ds(pl.multiple_of((CORES * pair + core) * width, 128), width)
     for k in range(KV_HEADS):
         source = lax.bitwise_xor(pair, k)
-        at = pl.ds(pl.multiple_of(source * 2 * rows, 2 * rows), 2 * rows)
-        pieces, selected = [], []
-        for p in range(CORES):
-            part = parts[2 * k + p]
-            start = part.shape[0] - tiles * rows
-            state = part[start:, :].astype(jnp.float32).reshape(tiles, rows, LANES)
-            square = jnp.sum(jnp.sum(state * state, axis=0), axis=-1, keepdims=True)
-            inverse = lax.rsqrt(square / (tiles * LANES) + norm_eps)
-            pieces.append(state * inverse[None] * gain[...][:, None, :])
-            offset = pl.multiple_of(start + me * mine * rows, 2 * rows)
-            selected.append(
-                part[pl.ds(offset, mine * rows), :].astype(jnp.float32).reshape(mine, rows, LANES)
-            )
-        low, high = jnp.where(first, *pieces), jnp.where(first, *pieces[::-1])
-        for t in range(tiles):
-            normed[at, t * LANES : (t + 1) * LANES] = jnp.concatenate([low[t], high[t]], axis=0).astype(
-                normed.dtype
-            )
-        low, high = jnp.where(first, *selected), jnp.where(first, *selected[::-1])
-        for t in range(mine):
-            cols_out[at, t * LANES : (t + 1) * LANES] = jnp.concatenate(
-                [low[t], high[t]], axis=0
-            ).astype(cols_out.dtype)
+        rows = pl.ds(pl.multiple_of(source * 16, 16), 16)
+
+        def both(at):
+            a, b = (parts[2 * k + p][:, at].astype(jnp.float32) for p in range(CORES))
+            return jnp.concatenate([jnp.where(first, a, b), jnp.where(first, b, a)], axis=0)
+
+        state = both(slice(None))
+        inverse = lax.rsqrt(jnp.mean(state * state, axis=-1, keepdims=True) + norm_eps)
+        normed[rows, :] = (state * inverse * gain[...]).astype(jnp.bfloat16)
+        cols_out[rows, :] = both(columns).astype(cols_out.dtype)
     key = matmul(normed[...], wk[...], ((1,), (1,)))
     value = matmul(normed[...], wv[...], ((1,), (1,)))
     kv_out[...] = jnp.concatenate([key, value], axis=1).astype(kv_out.dtype)
 
 
-def project(parts, gain, wk, wv, tokens):
-    width = wk.shape[1]
+def project(parts, gain, wk, wv):
+    tokens = sum(p.shape[0] for p in parts)
+    width = parts[0].shape[1]
     bf16 = jnp.bfloat16
     return pl.pallas_call(
         project_kernel,
@@ -342,9 +310,11 @@
         in_specs=[VMEM] * (len(parts) + 3),
         out_specs=[VMEM] * 3,
         compiler_params=pltpu.CompilerParams(vmem_limit_bytes=12 * MIB),
-        cost_estimate=pl.CostEstimate(flops=0, bytes_accessed=0, transcendentals=0),
+        cost_estimate=pl.CostEstimate(
+            flops=0, bytes_accessed=0, transcendentals=0
+        ),
         name="project",
-    )(*[in_vmem(p) for p in parts], gain.reshape(-1, LANES), in_vmem(wk), in_vmem(wv))
+    )(*[in_vmem(p) for p in parts], gain, in_vmem(wk), in_vmem(wv))
 
 
 def query_kernel(normed, wq, out):
@@ -376,11 +346,11 @@
     block = scored.shape[3]
     rows = (blocks.shape[1] - TAIL) // (2 * block)
     me, pair, core = my_place()
-    tail, whole = pl.ds(rows * 2 * block, TAIL), pl.ds(0, rows * 2 * block + TAIL)
+    tail = pl.ds(rows * 2 * block, TAIL)
     tails = [
         pltpu.make_async_copy(held[i].at[tail], tail_vm.at[i], note_sems.at[i]) for i in range(count)
     ]
-    copies = [pltpu.make_async_copy(held[i].at[whole], blocks.at[i], sems.at[i]) for i in range(count)]
+    copies = [pltpu.make_async_copy(held[i], blocks.at[i], sems.at[i]) for i in range(count)]
     for copy in tails + copies:
         copy.start()
     scale = HEAD_DIM ** (-0.5)
@@ -467,7 +437,7 @@
         in_specs=[VMEM] * 3 + [ANYWHERE] * count,
         out_specs=VMEM,
         scratch_shapes=[
-            pltpu.VMEM((count, *held[-1].shape), jnp.bfloat16),
+            pltpu.VMEM((count, *held[0].shape), jnp.bfloat16),
             pltpu.VMEM(q.shape, jnp.float32),
             pltpu.VMEM((requests, listed, q.size // HEAD_DIM // requests, block), jnp.float32),
             pltpu.VMEM((count, HEAD_DIM), jnp.int32),
@@ -512,10 +482,13 @@
     )(*[in_vmem(p) for p in parts], in_vmem(w_out))
 
 
+def away(turn, core):
+    return lax.bitwise_xor(3 * (1 - turn), core)
+
+
 def finish_kernel(*refs):
-    outs, placed = refs[-1 - KV_HEADS : -1], refs[-1]
-    parts, (before, cols, w_out) = refs[: -4 - KV_HEADS], refs[-4 - KV_HEADS : -1 - KV_HEADS]
-    me, pair, _ = my_place()
+    parts, (before, cols, w_out, *outs, placed) = refs[:-6], refs[-6:]
+    me, pair, core = my_place()
     depth = parts[0].shape[1]
     total = before[...]
     for i, part in enumerate(parts):
@@ -523,20 +496,23 @@
         span = pl.ds(pl.multiple_of(source * depth, depth), depth)
         total = total + matmul(part[...], w_out[span, :])
     placed[...] = cols[...].astype(jnp.float32) + total
-    rows = outs[0].shape[0]
-    for k, out in enumerate(outs):
-        target = lax.bitwise_xor(pair, k)
-        out[...] = placed[pl.ds(pl.multiple_of(target * rows, rows), rows), :].astype(out.dtype)
+    keep, give = outs
+    rows = keep.shape[0] // 2
+    for k in range(KV_HEADS):
+        target = lax.bitwise_xor(pair, away(k % 2, lax.bitwise_xor(core, k // 2)))
+        piece = placed[pl.ds(pl.multiple_of(target * rows, rows), rows), :]
+        out = (keep, give)[k // 2]
+        out[k % 2 * rows : (k % 2 + 1) * rows, :] = piece.astype(out.dtype)
 
 
 def finish(parts, before, cols, w_out):
     tokens, width = cols.shape
-    shape = pltpu.VMEM((tokens // KV_HEADS, width), jnp.bfloat16)
+    shape = pltpu.VMEM((tokens // 2, width), jnp.bfloat16)
     return pl.pallas_call(
         finish_kernel,
-        out_shape=[shape] * KV_HEADS,
+        out_shape=[shape] * 2,
         in_specs=[VMEM] * (len(parts) + 3),
-        out_specs=[VMEM] * KV_HEADS,
+        out_specs=[VMEM] * 2,
         scratch_shapes=[pltpu.VMEM((tokens, width), jnp.float32)],
         compiler_params=pltpu.CompilerParams(vmem_limit_bytes=12 * MIB),
         cost_estimate=pl.CostEstimate(
@@ -546,61 +522,86 @@
     )(*[in_vmem(p) for p in parts], in_vmem(before), in_vmem(cols), in_vmem(w_out))
 
 
-def place_kernel(order, *refs):
+def join_kernel(keep, got, *outs):
+    rows = keep.shape[0] // 2
+    for k, out in enumerate(outs):
+        out[0] = keep[k * rows : (k + 1) * rows, :]
+        out[1] = got[k * rows : (k + 1) * rows, :]
+
+
+def join(keep, got):
+    rows, width = keep.shape
+    return pl.pallas_call(
+        join_kernel,
+        out_shape=[pltpu.VMEM((CORES, rows // 2, width), keep.dtype)] * 2,
+        in_specs=[VMEM] * 2,
+        out_specs=[VMEM] * 2,
+        compiler_params=pltpu.CompilerParams(vmem_limit_bytes=4 * MIB),
+        name="join",
+    )(in_vmem(keep), in_vmem(got))
+
+
+def place_kernel(*refs):
     parts, out = refs[:-1], refs[-1]
     me, _, core = my_place()
-    rows, width = out.shape[1], parts[0].shape[1]
-    for i, part in zip(order, parts, strict=True):
-        source = lax.bitwise_xor(me, i)
-        both = part[...].astype(jnp.float32)
-        mine = jnp.where(core == 0, both[:rows], both[rows:])
-        out[0, :, pl.ds(pl.multiple_of(source * width, width), width)] = mine.astype(out.dtype)
+    rows, width = out.shape[1], parts[0].shape[2]
+    for i, part in enumerate(parts):
+        taker = lax.bitwise_xor(core, i % 2)
+        sender = lax.bitwise_xor(me - core + taker, CORES * away(i // 2, taker))
+        for p in range(CORES):
+            source = lax.bitwise_xor(sender, p)
+            both = part[p].astype(jnp.float32)
+            mine = jnp.where(core == 0, both[:rows], both[rows:])
+            out[0, :, pl.ds(pl.multiple_of(source * width, width), width)] = mine.astype(out.dtype)
 
 
 def place_columns(parts):
-    order = sorted(parts, reverse=True)
-    rows, width = parts[0].shape
-    return pl.pallas_call(
-        functools.partial(place_kernel, order),
-        out_shape=jax.ShapeDtypeStruct((1, rows // CORES, width * len(parts)), jnp.bfloat16),
+    cores, rows, width = parts[0].shape
+    return pl.pallas_call(
+        place_kernel,
+        out_shape=jax.ShapeDtypeStruct((1, rows // CORES, width * cores * len(parts)), jnp.bfloat16),
         in_specs=[VMEM] * len(parts),
         out_specs=VMEM,
         compiler_params=pltpu.CompilerParams(vmem_limit_bytes=4 * MIB),
         name="place",
-    )(*[in_vmem(parts[i]) for i in order])
+    )(*[in_vmem(part) for part in parts])
 
 
 def by_head(hidden, gain, w_query, w_key, w_value, w_out, cache, block_slot, retrieved, counts):
     size, sections = lax.axis_size("dev"), lax.axis_size("segment")
-    packed = pack(block_slot, retrieved, counts, hidden[0], cache)
+    state = hidden[0]
+    gathered = {2: to_pair(state, 2), 1: to_pair(state, 1)}
+    packed = pack(block_slot, retrieved, counts, cache)
     weights = load(w_query, w_key[0].swapaxes(0, 1), w_value[0].swapaxes(0, 1))
-    second, first, far = to_pair(packed[2], 2), to_pair(packed[1], 1), to_pair(packed[3], 3)
-    second, weights = lax.optimization_barrier((second, weights))
-    crossed = to_pair(second[packed[3].shape[0] :], 1)
-    held = [h for a in (packed[0], first, second) for h in (a, to_partner(a))]
-    held, crossed, (wq, wk, wv) = lax.optimization_barrier((held, crossed, weights))
-    parts = [*held, crossed, to_partner(crossed)]
-    tokens = size * hidden.shape[1]
-    normed, kv, cols = project(parts, gain, wk, wv, tokens)
+    blocks = {k: to_pair(packed[k], k) for k in (3, 2)}
+    gathered[2], packed = lax.optimization_barrier((gathered[2], packed))
+    gathered[3] = to_pair(gathered[2], 1)
+    near, gathered[1] = lax.optimization_barrier((packed[1], gathered[1]))
+    blocks[1] = to_pair(near, 1)
+    mine, gathered, weights = lax.optimization_barrier((state, gathered, weights))
+    wq, wk, wv = weights
+    parts = [p for a in (mine, *(gathered[k] for k in (1, 2, 3))) for p in (a, to_partner(a))]
+    normed, kv, cols = project(parts, gain, wk, wv)
     kv_other = to_partner(kv)
     q = query(normed, wq)
-    far, q, kv_other = lax.optimization_barrier((far, q, kv_other))
-    held += [far, to_partner(far)]
+    own, blocks, q = lax.optimization_barrier((packed[0], blocks, q))
+    blocks[0] = own
+    held = [h for k in range(KV_HEADS) for h in (blocks[k], to_partner(blocks[k]))]
     context = attend(q, kv, kv_other, held, size, retrieved.shape[2], cache.shape[2])
     contexts = {0: context, 2: to_pair(context, 2), 1: to_pair(context, 1)}
     contexts[3] = to_pair(contexts[2], 1)
     contexts = [p for k in range(KV_HEADS) for p in (contexts[k], to_partner(contexts[k]))]
     before = partial_branch(contexts[:4], w_out[0])
-    pieces = finish(contexts[4:], before, cols, w_out[0])
-    final = {}
-    for k in (3, 2, 1, 0):
+    keep, give = finish(contexts[4:], before, cols, w_out[0])
+    final = []
+    for k, piece in enumerate(join(keep, to_partner(give))):
         route = [
-            (s * size + d, (s + 1) % sections * size + (d ^ (CORES * k)))
+            (s * size + d, (s + 1) % sections * size + (d ^ (CORES * (3 * (1 - k) ^ d % CORES))))
             for s in range(sections)
             for d in range(size)
         ]
-        final[2 * k] = lax.ppermute(pieces[k], ("segment", "dev"), route)
-        final[2 * k + 1] = to_partner(final[2 * k])
+        piece = lax.ppermute(piece, ("segment", "dev"), route)
+        final += [piece, to_partner(piece)]
     return place_columns(final)
 
 

time: 70.9 us -> 67.7 us (0.955)
  waiting for transfers between devices: 32.1 us -> 27.5 us
  starting transfers between devices: 24 us -> 25.3 us
    ppermute x7 -> x9, waiting for transfers between devices: 23.3 us -> 16.3 us  [to_pair(): return lax.ppermute(x, 'dev', [(d, d ^ CORES * k) for d in range(size)])]
    ppermute x4 -> x2, starting transfers between devices: 7.7 us -> 4.42 us  [by_head(): piece = lax.ppermute(piece, ('segment', 'dev'), route)]
    ppermute x7 -> x9, starting transfers between devices: 15 us -> 18 us  [to_pair(): return lax.ppermute(x, 'dev', [(d, d ^ CORES * k) for d in range(size)])]
    ppermute x14 -> x16, waiting for transfers between devices: 4.44 us -> 6.22 us  [to_partner(): lax.ppermute(x, 'dev', [(d, d ^ 1) for d in range(lax.axis_size('dev'))])]
    ppermute x14 -> x16, starting transfers between devices: 1.26 us -> 2.89 us  [to_partner(): lax.ppermute(x, 'dev', [(d, d ^ 1) for d in range(lax.axis_size('dev'))])]
    ppermute x4 -> x2, waiting for transfers between devices: 4.35 us -> 5.01 us  [by_head(): piece = lax.ppermute(piece, ('segment', 'dev'), route)]
    pallas_call x3 -> x4, Pallas kernels: 3.09 us -> 2.87 us  [the longest x1 1.31 us: pack(): pl.pallas_call(pack_kernel, out_shape=[pltpu.VMEM((rows * 2 * tokens + TA...]
  transfers between devices with their start and end apart: 25 -> 27, of which waited for: 13 -> 14; matrix products, arithmetic and copies ran while one was open for 0% -> 0% of each run, Pallas kernels for 11% -> 14%
where the time goes in v4:
time: 67.7 us; the launch traced here: 67.6 us
  waiting for transfers between devices  27.5 us (41%)
  starting transfers between devices  25.3 us (37%)
  Pallas kernels  13.9 us (21%)
  between operations  0.81 us (1%)
    ppermute x9, starting transfers between devices, to_pair(): return lax.ppermute(x, 'dev', [(d, d ^ CORES * k) for d in range(size)])  18 us
    ppermute x9, waiting for transfers between devices, to_pair(): return lax.ppermute(x, 'dev', [(d, d ^ CORES * k) for d in range(size)])  16.3 us
    ppermute x16, waiting for transfers between devices, to_partner(): lax.ppermute(x, 'dev', [(d, d ^ 1) for d in range(lax.axis_size('dev'))])  6.22 us
    ppermute x2, waiting for transfers between devices, by_head(): piece = lax.ppermute(piece, ('segment', 'dev'), route)  5.01 us
    ppermute x2, starting transfers between devices, by_head(): piece = lax.ppermute(piece, ('segment', 'dev'), route)  4.42 us
    pallas_call x1, Pallas kernels, load(): pl.pallas_call(functools.partial(load_kernel, len(arrays)), out_shape=[pl...  4.19 us
    ppermute x16, starting transfers between devices, to_partner(): lax.ppermute(x, 'dev', [(d, d ^ 1) for d in range(lax.axis_size('dev'))])  2.89 us
    pallas_call x1, Pallas kernels, attend(): pl.pallas_call(attend_kernel, out_shape=pltpu.VMEM(q.shape, jnp.bfloat16)...  2.83 us
  transfers between devices with their start and end apart: 27, of which 14 were waited for; matrix products, arithmetic and copies ran while one was open for 0% of the time, Pallas kernels for 14%

profile of v4, /device:TPU:0, one launch (start us, length us, event | category | flops | bytes accessed | tf_op | source)
XLA Modules:
  0.0 67.6 jit_solution(5288753330936346087)
XLA Ops:
  0.0 4.0 %collective-permute-start = (bf16[8,8192]{1,0:T(8,128)(2,1)}, bf16[8,8192]{1,0:T(8,128)(2,1)S(1)}, u32[]{:S(2)}, u32[]{:S(2)}) collective-permute-start(bf16[8,8192]{1,0:T(8,128)(2,1)} %bitcast.12), channel_id=1, source_target_pairs={{0,4},{1,5},{2,6},{3,7},{4,0},{5,1},{6,2},{7,3},{8,12},{9,13},{10,... | collective-permute-start | bytes 393224 | tf_op jit(solution)/shard_map/ppermute | solution.py:159
  4.0 1.6 %collective-permute-start.1 = (bf16[8,8192]{1,0:T(8,128)(2,1)}, bf16[8,8192]{1,0:T(8,128)(2,1)S(1)}, u32[]{:S(2)}, u32[]{:S(2)}) collective-permute-start(bf16[8,8192]{1,0:T(8,128)(2,1)} %bitcast.13), channel_id=1, source_target_pairs={{0,2},{1,3},{2,0},{3,1},{4,6},{5,7},{6,4},{7,5},{8,10},{9,11},{10,... | collective-permute-start | bytes 393224 | tf_op jit(solution)/shard_map/ppermute | solution.py:159
  6.3 1.3 %pack.1 = (bf16[1040,128]{1,0:T(8,128)(2,1)S(1)}, bf16[1040,128]{1,0:T(8,128)(2,1)S(1)}, bf16[1040,128]{1,0:T(8,128)(2,1)S(1)}, bf16[1040,128]{1,0:T(8,128)(2,1)S(1)}) custom-call(s32[1,1]{1,0:T(1,128)S(6)} %copy.11.counts, s32[32]{0:T(128)} %table_in.1, s32[1,1,6]{2,1,0:T(1,128)} %retrieved_in.1, bf16[1,4,128,1024]{3,2,1,0:T(8,128)(2,1)} %cache.1), custom_call_target="tpu_custom_call" | custom-call | tf_op jit(solution)/shard_map/pack/pallas_call | solution.py:256
  7.6 3.1 %collective-permute-done.refs_4_ = bf16[8,8192]{1,0:T(8,128)(2,1)S(1)} collective-permute-done((bf16[8,8192]{1,0:T(8,128)(2,1)}, bf16[8,8192]{1,0:T(8,128)(2,1)S(1)}, u32[]{:S(2)}, u32[]{:S(2)}) %collective-permute-start) | collective-permute-done | bytes 131104 | tf_op jit(solution)/shard_map/ppermute | solution.py:159
  10.7 0.7 collective-permute-start.5
  11.4 3.3 %collective-permute-start.3 = (bf16[1040,128]{1,0:T(8,128)(2,1)S(1)}, bf16[1040,128]{1,0:T(8,128)(2,1)S(1)}, u32[]{:S(2)}, u32[]{:S(2)}) collective-permute-start(bf16[1040,128]{1,0:T(8,128)(2,1)S(1)} %get-tuple-element.38), channel_id=1, source_target_pairs={{0,4},{1,5},{2,6},{3,7},{4,0},{5,1},{6,2},{7,3},{8,12},{9,13},{10,... | collective-permute-start | bytes 798728 | tf_op jit(solution)/shard_map/ppermute | solution.py:159
  14.7 0.5 collective-permute-start.4
  15.2 4.2 %load.1 = (bf16[8192,512]{1,0:T(8,128)(2,1)S(1)}, bf16[64,8192]{1,0:T(8,128)(2,1)S(1)}, bf16[64,8192]{1,0:T(8,128)(2,1)S(1)}) custom-call(bf16[1,8192,512]{2,1,0:T(8,128)(2,1)} %refs_0_.1, bf16[64,8192]{1,0:T(8,128)(2,1)} %bitcast.16, bf16[64,8192]{1,0:T(8,128)(2,1)} %bitcast.17), custom_call_target="tpu_custom_call" | custom-call | tf_op jit(solution)/shard_map/load/pallas_call | solution.py:205
  19.5 0.5 collective-permute-start.7
  20.0 0.8 %collective-permute-done.6.refs_1_ = bf16[8,8192]{1,0:T(8,128)(2,1)S(1)} collective-permute-done((bf16[8,8192]{1,0:T(8,128)(2,1)S(1)}, bf16[8,8192]{1,0:T(8,128)(2,1)S(1)}, u32[]{:S(2)}, u32[]{:S(2)}) %collective-permute-start.6) | collective-permute-done | bytes 131104 | tf_op jit(solution)/shard_map/ppermute | solution.py:163
  21.4 0.8 %collective-permute-done.8.refs_5_ = bf16[8,8192]{1,0:T(8,128)(2,1)S(1)} collective-permute-done((bf16[8,8192]{1,0:T(8,128)(2,1)S(1)}, bf16[8,8192]{1,0:T(8,128)(2,1)S(1)}, u32[]{:S(2)}, u32[]{:S(2)}) %collective-permute-start.8) | collective-permute-done | bytes 131104 | tf_op jit(solution)/shard_map/ppermute | solution.py:163
  22.4 1.6 %project.1 = (bf16[64,8192]{1,0:T(8,128)(2,1)S(1)}, bf16[64,128]{1,0:T(8,128)(2,1)S(1)}, bf16[64,1024]{1,0:T(8,128)(2,1)S(1)}) custom-call(bf16[8,8192]{1,0:T(8,128)(2,1)S(1)} %bitcast.15, bf16[8,8192]{1,0:T(8,128)(2,1)S(1)} %collective-permute-done.6.refs_1_, bf16[8,8192]{1,0:T(8,128)(2,1)S(1)} %collective-permute-done.1.refs_2_, ...), custom_call_target="tpu_custom_call" | custom-call | tf_op jit(solution)/shard_map/project/pallas_call | solution.py:303
  24.0 1.5 %query.1.q = bf16[64,512]{1,0:T(8,128)(2,1)S(1)} custom-call(bf16[64,8192]{1,0:T(8,128)(2,1)S(1)} %get-tuple-element.54.normed, bf16[8192,512]{1,0:T(8,128)(2,1)S(1)} %get-tuple-element.55.wq), custom_call_target="tpu_custom_call" | custom-call | tf_op jit(solution)/shard_map/query/pallas_call | solution.py:325
  25.6 7.8 %collective-permute-done.3.refs_4_ = bf16[1040,128]{1,0:T(8,128)(2,1)S(1)} collective-permute-done((bf16[1040,128]{1,0:T(8,128)(2,1)S(1)}, bf16[1040,128]{1,0:T(8,128)(2,1)S(1)}, u32[]{:S(2)}, u32[]{:S(2)}) %collective-permute-start.3) | collective-permute-done | bytes 266272 | tf_op jit(solution)/shard_map/ppermute | solution.py:159
  33.4 0.5 collective-permute-start.12
  34.0 0.4 collective-permute-start.14
  34.5 1.6 %collective-permute-done.10.kv_other = bf16[64,128]{1,0:T(8,128)(2,1)S(1)} collective-permute-done((bf16[64,128]{1,0:T(8,128)(2,1)S(1)}, bf16[64,128]{1,0:T(8,128)(2,1)S(1)}, u32[]{:S(2)}, u32[]{:S(2)}) %collective-permute-start.10) | collective-permute-done | bytes 16416 | tf_op jit(solution)/shard_map/ppermute | solution.py:163
  36.1 2.8 %attend.1.refs_0_ = bf16[64,512]{1,0:T(8,128)(2,1)S(1)} custom-call(bf16[64,512]{1,0:T(8,128)(2,1)S(1)} %query.1.q, bf16[64,128]{1,0:T(8,128)(2,1)S(1)} %get-tuple-element.57.kv_mine, bf16[64,128]{1,0:T(8,128)(2,1)S(1)} %collective-permute-done.10.kv_other, bf16[1040,128]{1,0:T(8,128)(2,1)S(1)} %get-tuple-element.58.refs_0_, ...), custom_call_target="tpu_custom_call" | custom-call | flops 268435456 | bytes 2097152 | tf_op jit(solution)/shard_map/attend/pallas_call | solution.py:434
  39.0 6.3 %collective-permute-start.15 = (bf16[64,512]{1,0:T(8,128)(2,1)S(1)}, bf16[64,512]{1,0:T(8,128)(2,1)S(1)}, u32[]{:S(2)}, u32[]{:S(2)}) collective-permute-start(bf16[64,512]{1,0:T(8,128)(2,1)S(1)} %attend.1.refs_0_), channel_id=1, source_target_pairs={{0,4},{1,5},{2,6},{3,7},{4,0},{5,1},{6,2},{7,3},{8,12},{9,13},{10,... | collective-permute-start | bytes 196616 | tf_op jit(solution)/shard_map/ppermute | solution.py:159
  45.3 3.2 %collective-permute-done.15.refs_0_ = bf16[64,512]{1,0:T(8,128)(2,1)S(1)} collective-permute-done((bf16[64,512]{1,0:T(8,128)(2,1)S(1)}, bf16[64,512]{1,0:T(8,128)(2,1)S(1)}, u32[]{:S(2)}, u32[]{:S(2)}) %collective-permute-start.15) | collective-permute-done | bytes 65568 | tf_op jit(solution)/shard_map/ppermute | solution.py:159
  48.5 1.6 %collective-permute-start.17 = (bf16[64,512]{1,0:T(8,128)(2,1)S(1)}, bf16[64,512]{1,0:T(8,128)(2,1)S(1)}, u32[]{:S(2)}, u32[]{:S(2)}) collective-permute-start(bf16[64,512]{1,0:T(8,128)(2,1)S(1)} %collective-permute-done.15.refs_0_), channel_id=1, source_target_pairs={{0,2},{1,3},{2,0},{3,1},{4,6},{5,7},{6,4},{7,5},{8,10},{9,11},{10,... | collective-permute-start | bytes 196616 | tf_op jit(solution)/shard_map/ppermute | solution.py:159
  50.1 0.5 collective-permute-start.21
  50.6 2.1 %collective-permute-done.17.refs_2_ = bf16[64,512]{1,0:T(8,128)(2,1)S(1)} collective-permute-done((bf16[64,512]{1,0:T(8,128)(2,1)S(1)}, bf16[64,512]{1,0:T(8,128)(2,1)S(1)}, u32[]{:S(2)}, u32[]{:S(2)}) %collective-permute-start.17) | collective-permute-done | bytes 65568 | tf_op jit(solution)/shard_map/ppermute | solution.py:159
  52.8 0.8 %partial.1.refs_4_ = f32[64,1024]{1,0:T(8,128)S(1)} custom-call(bf16[64,512]{1,0:T(8,128)(2,1)S(1)} %attend.1.refs_0_, bf16[64,512]{1,0:T(8,128)(2,1)S(1)} %collective-permute-done.19.refs_1_, bf16[64,512]{1,0:T(8,128)(2,1)S(1)} %collective-permute-done.20.refs_2_, bf16[64,512]{1,0:T(8,128)(2,1)S(1)} %collective-permute-done.21.refs_3_, ...), custom_call_target="tpu_custom_call" | custom-call | flops 268435456 | bytes 4194304 | tf_op jit(solution)/shard_map/partial/pallas_call | solution.py:472
  54.0 0.9 %finish.1 = (bf16[32,1024]{1,0:T(8,128)(2,1)S(1)}, bf16[32,1024]{1,0:T(8,128)(2,1)S(1)}) custom-call(bf16[64,512]{1,0:T(8,128)(2,1)S(1)} %collective-permute-done.15.refs_0_, bf16[64,512]{1,0:T(8,128)(2,1)S(1)} %collective-permute-done.16.refs_1_, bf16[64,512]{1,0:T(8,128)(2,1)S(1)} %collective-permute-done.17.refs_2_, ...), custom_call_target="tpu_custom_call" | custom-call | flops 268435456 | bytes 4194304 | tf_op jit(solution)/shard_map/finish/pallas_call | solution.py:511
  55.1 1.1 %collective-permute-done.22.got = bf16[32,1024]{1,0:T(8,128)(2,1)S(1)} collective-permute-done((bf16[32,1024]{1,0:T(8,128)(2,1)S(1)}, bf16[32,1024]{1,0:T(8,128)(2,1)S(1)}, u32[]{:S(2)}, u32[]{:S(2)}) %collective-permute-start.22) | collective-permute-done | bytes 65568 | tf_op jit(solution)/shard_map/ppermute | solution.py:163
  56.2 2.9 %collective-permute-start.23 = (bf16[2,16,1024]{2,1,0:T(8,128)(2,1)S(1)}, bf16[2,16,1024]{2,1,0:T(8,128)(2,1)S(1)}, u32[]{:S(2)}, u32[]{:S(2)}) collective-permute-start(bf16[2,16,1024]{2,1,0:T(8,128)(2,1)S(1)} %get-tuple-element.65), channel_id=1, source_target_pairs={{0,14},{1,13},{2,12},{3,15},{4,10},{5,9},{6,8},{7,11},{8,22},{9,21... | collective-permute-start | bytes 196616 | tf_op jit(solution)/shard_map/ppermute | solution.py:603
  59.1 1.5 %collective-permute-start.25 = (bf16[2,16,1024]{2,1,0:T(8,128)(2,1)S(1)}, bf16[2,16,1024]{2,1,0:T(8,128)(2,1)S(1)}, u32[]{:S(2)}, u32[]{:S(2)}) collective-permute-start(bf16[2,16,1024]{2,1,0:T(8,128)(2,1)S(1)} %get-tuple-element.66), channel_id=1, source_target_pairs={{0,8},{1,11},{2,10},{3,9},{4,12},{5,15},{6,14},{7,13},{8,16},{9,19... | collective-permute-start | bytes 196616 | tf_op jit(solution)/shard_map/ppermute | solution.py:603
  60.6 4.1 %collective-permute-done.23.refs_0_ = bf16[2,16,1024]{2,1,0:T(8,128)(2,1)S(1)} collective-permute-done((bf16[2,16,1024]{2,1,0:T(8,128)(2,1)S(1)}, bf16[2,16,1024]{2,1,0:T(8,128)(2,1)S(1)}, u32[]{:S(2)}, u32[]{:S(2)}) %collective-permute-start.23) | collective-permute-done | bytes 65568 | tf_op jit(solution)/shard_map/ppermute | solution.py:603
  64.7 0.9 %collective-permute-done.25.refs_2_ = bf16[2,16,1024]{2,1,0:T(8,128)(2,1)S(1)} collective-permute-done((bf16[2,16,1024]{2,1,0:T(8,128)(2,1)S(1)}, bf16[2,16,1024]{2,1,0:T(8,128)(2,1)S(1)}, u32[]{:S(2)}, u32[]{:S(2)}) %collective-permute-start.25) | collective-permute-done | bytes 65568 | tf_op jit(solution)/shard_map/ppermute | solution.py:603
  65.9 0.9 %collective-permute-done.26.refs_3_ = bf16[2,16,1024]{2,1,0:T(8,128)(2,1)S(1)} collective-permute-done((bf16[2,16,1024]{2,1,0:T(8,128)(2,1)S(1)}, bf16[2,16,1024]{2,1,0:T(8,128)(2,1)S(1)}, u32[]{:S(2)}, u32[]{:S(2)}) %collective-permute-start.26) | collective-permute-done | bytes 65568 | tf_op jit(solution)/shard_map/ppermute | solution.py:163
  66.9 0.7 %place.1 = bf16[1,8,8192]{2,1,0:T(8,128)(2,1)} custom-call(bf16[2,16,1024]{2,1,0:T(8,128)(2,1)S(1)} %collective-permute-done.23.refs_0_, bf16[2,16,1024]{2,1,0:T(8,128)(2,1)S(1)} %collective-permute-done.24.refs_1_, bf16[2,16,1024]{2,1,0:T(8,128)(2,1)S(1)} %collective-permute-done.25.refs_2_, bf16[2,16,1024]{2,1,0:T(8,128)(2,1)S(1)} %collective-permute-done.26.refs_3_), custom_call_target="tpu_custom_call" | custom-call | tf_op jit(solution)/shard_map/place/pallas_call | solution.py:560
  (40 shorter events, 2.0 us)
Async XLA Ops:
  0.0 19.4 %copy-start = (bf16[1,8,8192]{2,1,0:T(8,128)(2,1)S(1)}, bf16[1,8,8192]{2,1,0:T(8,128)(2,1)}, u32[]{:S(2)}) copy-start(bf16[1,8,8192]{2,1,0:T(8,128)(2,1)} %param.10) | copy-start | bytes 393220
  0.0 22.4 %copy-start.1 = (f32[1,8192]{1,0:T(1,128)S(1)}, f32[1,8192]{1,0:T(1,128)}, u32[]{:S(2)}) copy-start(f32[1,8192]{1,0:T(1,128)} %refs_8_.1) | copy-start | bytes 98308
  0.0 10.7 %collective-permute-start = (bf16[8,8192]{1,0:T(8,128)(2,1)}, bf16[8,8192]{1,0:T(8,128)(2,1)S(1)}, u32[]{:S(2)}, u32[]{:S(2)}) collective-permute-start(bf16[8,8192]{1,0:T(8,128)(2,1)} %bitcast.12), channel_id=1, source_target_pairs={{0,4},{1,5},{2,6},{3,7},{4,0},{5,1},{6,2},{7,3},{8,12},{9,13},{10,... | collective-permute-start | bytes 393224 | tf_op jit(solution)/shard_map/ppermute | solution.py:159
  4.0 11.1 %collective-permute-start.1 = (bf16[8,8192]{1,0:T(8,128)(2,1)}, bf16[8,8192]{1,0:T(8,128)(2,1)S(1)}, u32[]{:S(2)}, u32[]{:S(2)}) collective-permute-start(bf16[8,8192]{1,0:T(8,128)(2,1)} %bitcast.13), channel_id=1, source_target_pairs={{0,2},{1,3},{2,0},{3,1},{4,6},{5,7},{6,4},{7,5},{8,10},{9,11},{10,... | collective-permute-start | bytes 393224 | tf_op jit(solution)/shard_map/ppermute | solution.py:159
  10.7 8.7 %collective-permute-start.5 = (bf16[8,8192]{1,0:T(8,128)(2,1)S(1)}, bf16[8,8192]{1,0:T(8,128)(2,1)S(1)}, u32[]{:S(2)}, u32[]{:S(2)}) collective-permute-start(bf16[8,8192]{1,0:T(8,128)(2,1)S(1)} %collective-permute-done.refs_4_), channel_id=1, source_target_pairs={{0,2},{1,3},{2,0},{3,1},{4,6},{5,7},{6,4},{7,5},{8,10},{9,11},{10,... | collective-permute-start | bytes 393224 | tf_op jit(solution)/shard_map/ppermute | solution.py:159
  11.4 22.0 %collective-permute-start.3 = (bf16[1040,128]{1,0:T(8,128)(2,1)S(1)}, bf16[1040,128]{1,0:T(8,128)(2,1)S(1)}, u32[]{:S(2)}, u32[]{:S(2)}) collective-permute-start(bf16[1040,128]{1,0:T(8,128)(2,1)S(1)} %get-tuple-element.38), channel_id=1, source_target_pairs={{0,4},{1,5},{2,6},{3,7},{4,0},{5,1},{6,2},{7,3},{8,12},{9,13},{10,... | collective-permute-start | bytes 798728 | tf_op jit(solution)/shard_map/ppermute | solution.py:159
  14.7 18.7 %collective-permute-start.4 = (bf16[1040,128]{1,0:T(8,128)(2,1)S(1)}, bf16[1040,128]{1,0:T(8,128)(2,1)S(1)}, u32[]{:S(2)}, u32[]{:S(2)}) collective-permute-start(bf16[1040,128]{1,0:T(8,128)(2,1)S(1)} %get-tuple-element.39), channel_id=1, source_target_pairs={{0,6},{1,7},{2,4},{3,5},{4,2},{5,3},{6,0},{7,1},{8,14},{9,15},{10,... | collective-permute-start | bytes 798728 | tf_op jit(solution)/shard_map/ppermute | solution.py:159
  15.1 18.3 %collective-permute-start.2 = (bf16[1040,128]{1,0:T(8,128)(2,1)S(1)}, bf16[1040,128]{1,0:T(8,128)(2,1)S(1)}, u32[]{:S(2)}, u32[]{:S(2)}) collective-permute-start(bf16[1040,128]{1,0:T(8,128)(2,1)S(1)} %get-tuple-element.42), channel_id=1, source_target_pairs={{0,2},{1,3},{2,0},{3,1},{4,6},{5,7},{6,4},{7,5},{8,10},{9,11},{10,... | collective-permute-start | bytes 798728 | tf_op jit(solution)/shard_map/ppermute | solution.py:159
  15.2 37.5 %slice-start = ((s8[8388608]{0:T(1024)(128)(4,1)}), s8[4194304]{0:T(1024)(128)(4,1)S(1)}, s32[]{:S(2)}) async-start(s8[8388608]{0:T(1024)(128)(4,1)} %bitcast.8), calls=%async_computation | async-start | bytes 8388608
  19.4 33.3 %slice-start.1 = ((s8[8388608]{0:T(1024)(128)(4,1)}), s8[4194304]{0:T(1024)(128)(4,1)S(1)}, s32[]{:S(2)}) async-start(s8[8388608]{0:T(1024)(128)(4,1)} %bitcast.8), calls=%async_computation.1 | async-start | bytes 8388608
  19.5 1.4 %collective-permute-start.6 = (bf16[8,8192]{1,0:T(8,128)(2,1)S(1)}, bf16[8,8192]{1,0:T(8,128)(2,1)S(1)}, u32[]{:S(2)}, u32[]{:S(2)}) collective-permute-start(bf16[8,8192]{1,0:T(8,128)(2,1)S(1)} %bitcast.14), channel_id=1, source_target_pairs={{0,1},{1,0},{2,3},{3,2},{4,5},{5,4},{6,7},{7,6},{8,9},{9,8},{10,11... | collective-permute-start | bytes 393224 | tf_op jit(solution)/shard_map/ppermute | solution.py:163
  19.5 1.5 %collective-permute-start.7 = (bf16[8,8192]{1,0:T(8,128)(2,1)S(1)}, bf16[8,8192]{1,0:T(8,128)(2,1)S(1)}, u32[]{:S(2)}, u32[]{:S(2)}) collective-permute-start(bf16[8,8192]{1,0:T(8,128)(2,1)S(1)} %collective-permute-done.1.refs_2_), channel_id=1, source_target_pairs={{0,1},{1,0},{2,3},{3,2},{4,5},{5,4},{6,7},{7,6},{8,9},{9,8},{10,11... | collective-permute-start | bytes 393224 | tf_op jit(solution)/shard_map/ppermute | solution.py:163
  20.9 1.3 %collective-permute-start.8 = (bf16[8,8192]{1,0:T(8,128)(2,1)S(1)}, bf16[8,8192]{1,0:T(8,128)(2,1)S(1)}, u32[]{:S(2)}, u32[]{:S(2)}) collective-permute-start(bf16[8,8192]{1,0:T(8,128)(2,1)S(1)} %collective-permute-done.refs_4_), channel_id=1, source_target_pairs={{0,1},{1,0},{2,3},{3,2},{4,5},{5,4},{6,7},{7,6},{8,9},{9,8},{10,11... | collective-permute-start | bytes 393224 | tf_op jit(solution)/shard_map/ppermute | solution.py:163
  21.1 1.3 %collective-permute-start.9 = (bf16[8,8192]{1,0:T(8,128)(2,1)S(1)}, bf16[8,8192]{1,0:T(8,128)(2,1)S(1)}, u32[]{:S(2)}, u32[]{:S(2)}) collective-permute-start(bf16[8,8192]{1,0:T(8,128)(2,1)S(1)} %collective-permute-done.5.refs_6_), channel_id=1, source_target_pairs={{0,1},{1,0},{2,3},{3,2},{4,5},{5,4},{6,7},{7,6},{8,9},{9,8},{10,11... | collective-permute-start | bytes 393224 | tf_op jit(solution)/shard_map/ppermute | solution.py:163
  33.4 2.7 %collective-permute-start.11 = (bf16[1040,128]{1,0:T(8,128)(2,1)S(1)}, bf16[1040,128]{1,0:T(8,128)(2,1)S(1)}, u32[]{:S(2)}, u32[]{:S(2)}) collective-permute-start(bf16[1040,128]{1,0:T(8,128)(2,1)S(1)} %get-tuple-element.58.refs_0_), channel_id=1, source_target_pairs={{0,1},{1,0},{2,3},{3,2},{4,5},{5,4},{6,7},{7,6},{8,9},{9,8},{10,11... | collective-permute-start | bytes 798728 | tf_op jit(solution)/shard_map/ppermute | solution.py:163
  33.4 2.7 %collective-permute-start.12 = (bf16[1040,128]{1,0:T(8,128)(2,1)S(1)}, bf16[1040,128]{1,0:T(8,128)(2,1)S(1)}, u32[]{:S(2)}, u32[]{:S(2)}) collective-permute-start(bf16[1040,128]{1,0:T(8,128)(2,1)S(1)} %collective-permute-done.2.refs_2_), channel_id=1, source_target_pairs={{0,1},{1,0},{2,3},{3,2},{4,5},{5,4},{6,7},{7,6},{8,9},{9,8},{10,11... | collective-permute-start | bytes 798728 | tf_op jit(solution)/shard_map/ppermute | solution.py:163
  33.9 2.2 %collective-permute-start.13 = (bf16[1040,128]{1,0:T(8,128)(2,1)S(1)}, bf16[1040,128]{1,0:T(8,128)(2,1)S(1)}, u32[]{:S(2)}, u32[]{:S(2)}) collective-permute-start(bf16[1040,128]{1,0:T(8,128)(2,1)S(1)} %collective-permute-done.3.refs_4_), channel_id=1, source_target_pairs={{0,1},{1,0},{2,3},{3,2},{4,5},{5,4},{6,7},{7,6},{8,9},{9,8},{10,11... | collective-permute-start | bytes 798728 | tf_op jit(solution)/shard_map/ppermute | solution.py:163
  34.0 2.1 %collective-permute-start.14 = (bf16[1040,128]{1,0:T(8,128)(2,1)S(1)}, bf16[1040,128]{1,0:T(8,128)(2,1)S(1)}, u32[]{:S(2)}, u32[]{:S(2)}) collective-permute-start(bf16[1040,128]{1,0:T(8,128)(2,1)S(1)} %collective-permute-done.4.refs_6_), channel_id=1, source_target_pairs={{0,1},{1,0},{2,3},{3,2},{4,5},{5,4},{6,7},{7,6},{8,9},{9,8},{10,11... | collective-permute-start | bytes 798728 | tf_op jit(solution)/shard_map/ppermute | solution.py:163
  34.4 1.7 %collective-permute-start.10 = (bf16[64,128]{1,0:T(8,128)(2,1)S(1)}, bf16[64,128]{1,0:T(8,128)(2,1)S(1)}, u32[]{:S(2)}, u32[]{:S(2)}) collective-permute-start(bf16[64,128]{1,0:T(8,128)(2,1)S(1)} %get-tuple-element.57.kv_mine), channel_id=1, source_target_pairs={{0,1},{1,0},{2,3},{3,2},{4,5},{5,4},{6,7},{7,6},{8,9},{9,8},{10,11... | collective-permute-start | bytes 49160 | tf_op jit(solution)/shard_map/ppermute | solution.py:163
  39.0 9.5 %collective-permute-start.15 = (bf16[64,512]{1,0:T(8,128)(2,1)S(1)}, bf16[64,512]{1,0:T(8,128)(2,1)S(1)}, u32[]{:S(2)}, u32[]{:S(2)}) collective-permute-start(bf16[64,512]{1,0:T(8,128)(2,1)S(1)} %attend.1.refs_0_), channel_id=1, source_target_pairs={{0,4},{1,5},{2,6},{3,7},{4,0},{5,1},{6,2},{7,3},{8,12},{9,13},{10,... | collective-permute-start | bytes 196616 | tf_op jit(solution)/shard_map/ppermute | solution.py:159
  45.3 4.8 %collective-permute-start.20 = (bf16[64,512]{1,0:T(8,128)(2,1)S(1)}, bf16[64,512]{1,0:T(8,128)(2,1)S(1)}, u32[]{:S(2)}, u32[]{:S(2)}) collective-permute-start(bf16[64,512]{1,0:T(8,128)(2,1)S(1)} %attend.1.refs_0_), channel_id=1, source_target_pairs={{0,2},{1,3},{2,0},{3,1},{4,6},{5,7},{6,4},{7,5},{8,10},{9,11},{10,... | collective-permute-start | bytes 196616 | tf_op jit(solution)/shard_map/ppermute | solution.py:159
  48.5 4.3 %collective-permute-start.17 = (bf16[64,512]{1,0:T(8,128)(2,1)S(1)}, bf16[64,512]{1,0:T(8,128)(2,1)S(1)}, u32[]{:S(2)}, u32[]{:S(2)}) collective-permute-start(bf16[64,512]{1,0:T(8,128)(2,1)S(1)} %collective-permute-done.15.refs_0_), channel_id=1, source_target_pairs={{0,2},{1,3},{2,0},{3,1},{4,6},{5,7},{6,4},{7,5},{8,10},{9,11},{10,... | collective-permute-start | bytes 196616 | tf_op jit(solution)/shard_map/ppermute | solution.py:159
  50.1 2.7 %collective-permute-start.19 = (bf16[64,512]{1,0:T(8,128)(2,1)S(1)}, bf16[64,512]{1,0:T(8,128)(2,1)S(1)}, u32[]{:S(2)}, u32[]{:S(2)}) collective-permute-start(bf16[64,512]{1,0:T(8,128)(2,1)S(1)} %attend.1.refs_0_), channel_id=1, source_target_pairs={{0,1},{1,0},{2,3},{3,2},{4,5},{5,4},{6,7},{7,6},{8,9},{9,8},{10,11... | collective-permute-start | bytes 196616 | tf_op jit(solution)/shard_map/ppermute | solution.py:163
  50.1 2.7 %collective-permute-start.21 = (bf16[64,512]{1,0:T(8,128)(2,1)S(1)}, bf16[64,512]{1,0:T(8,128)(2,1)S(1)}, u32[]{:S(2)}, u32[]{:S(2)}) collective-permute-start(bf16[64,512]{1,0:T(8,128)(2,1)S(1)} %collective-permute-done.20.refs_2_), channel_id=1, source_target_pairs={{0,1},{1,0},{2,3},{3,2},{4,5},{5,4},{6,7},{7,6},{8,9},{9,8},{10,11... | collective-permute-start | bytes 196616 | tf_op jit(solution)/shard_map/ppermute | solution.py:163
  50.6 3.0 %collective-permute-start.16 = (bf16[64,512]{1,0:T(8,128)(2,1)S(1)}, bf16[64,512]{1,0:T(8,128)(2,1)S(1)}, u32[]{:S(2)}, u32[]{:S(2)}) collective-permute-start(bf16[64,512]{1,0:T(8,128)(2,1)S(1)} %collective-permute-done.15.refs_0_), channel_id=1, source_target_pairs={{0,1},{1,0},{2,3},{3,2},{4,5},{5,4},{6,7},{7,6},{8,9},{9,8},{10,11... | collective-permute-start | bytes 196616 | tf_op jit(solution)/shard_map/ppermute | solution.py:163
  52.7 1.3 %collective-permute-start.18 = (bf16[64,512]{1,0:T(8,128)(2,1)S(1)}, bf16[64,512]{1,0:T(8,128)(2,1)S(1)}, u32[]{:S(2)}, u32[]{:S(2)}) collective-permute-start(bf16[64,512]{1,0:T(8,128)(2,1)S(1)} %collective-permute-done.17.refs_2_), channel_id=1, source_target_pairs={{0,1},{1,0},{2,3},{3,2},{4,5},{5,4},{6,7},{7,6},{8,9},{9,8},{10,11... | collective-permute-start | bytes 196616 | tf_op jit(solution)/shard_map/ppermute | solution.py:163
  54.9 1.3 %collective-permute-start.22 = (bf16[32,1024]{1,0:T(8,128)(2,1)S(1)}, bf16[32,1024]{1,0:T(8,128)(2,1)S(1)}, u32[]{:S(2)}, u32[]{:S(2)}) collective-permute-start(bf16[32,1024]{1,0:T(8,128)(2,1)S(1)} %get-tuple-element.64), channel_id=1, source_target_pairs={{0,1},{1,0},{2,3},{3,2},{4,5},{5,4},{6,7},{7,6},{8,9},{9,8},{10,11... | collective-permute-start | bytes 196616 | tf_op jit(solution)/shard_map/ppermute | solution.py:163
  56.2 8.5 %collective-permute-start.23 = (bf16[2,16,1024]{2,1,0:T(8,128)(2,1)S(1)}, bf16[2,16,1024]{2,1,0:T(8,128)(2,1)S(1)}, u32[]{:S(2)}, u32[]{:S(2)}) collective-permute-start(bf16[2,16,1024]{2,1,0:T(8,128)(2,1)S(1)} %get-tuple-element.65), channel_id=1, source_target_pairs={{0,14},{1,13},{2,12},{3,15},{4,10},{5,9},{6,8},{7,11},{8,22},{9,21... | collective-permute-start | bytes 196616 | tf_op jit(solution)/shard_map/ppermute | solution.py:603
  59.1 6.5 %collective-permute-start.25 = (bf16[2,16,1024]{2,1,0:T(8,128)(2,1)S(1)}, bf16[2,16,1024]{2,1,0:T(8,128)(2,1)S(1)}, u32[]{:S(2)}, u32[]{:S(2)}) collective-permute-start(bf16[2,16,1024]{2,1,0:T(8,128)(2,1)S(1)} %get-tuple-element.66), channel_id=1, source_target_pairs={{0,8},{1,11},{2,10},{3,9},{4,12},{5,15},{6,14},{7,13},{8,16},{9,19... | collective-permute-start | bytes 196616 | tf_op jit(solution)/shard_map/ppermute | solution.py:603
  64.7 1.3 %collective-permute-start.24 = (bf16[2,16,1024]{2,1,0:T(8,128)(2,1)S(1)}, bf16[2,16,1024]{2,1,0:T(8,128)(2,1)S(1)}, u32[]{:S(2)}, u32[]{:S(2)}) collective-permute-start(bf16[2,16,1024]{2,1,0:T(8,128)(2,1)S(1)} %collective-permute-done.23.refs_0_), channel_id=1, source_target_pairs={{0,1},{1,0},{2,3},{3,2},{4,5},{5,4},{6,7},{7,6},{8,9},{9,8},{10,11... | collective-permute-start | bytes 196616 | tf_op jit(solution)/shard_map/ppermute | solution.py:163
  65.6 1.3 %collective-permute-start.26 = (bf16[2,16,1024]{2,1,0:T(8,128)(2,1)S(1)}, bf16[2,16,1024]{2,1,0:T(8,128)(2,1)S(1)}, u32[]{:S(2)}, u32[]{:S(2)}) collective-permute-start(bf16[2,16,1024]{2,1,0:T(8,128)(2,1)S(1)} %collective-permute-done.25.refs_2_), channel_id=1, source_target_pairs={{0,1},{1,0},{2,3},{3,2},{4,5},{5,4},{6,7},{7,6},{8,9},{9,8},{10,11... | collective-permute-start | bytes 196616 | tf_op jit(solution)/shard_map/ppermute | solution.py:163

commit v5 on v4

--- a/solution.py
+++ b/solution.py
@@ -214,12 +214,12 @@
     )(*[pltpu.with_memory_space_constraint(a, pltpu.HBM) for a in arrays])
 
 
-def pack_kernel(counts, table_in, retrieved_in, cache, *rest):
-    outs, (whole, table, retrieved, sems, list_sems) = rest[:-5], rest[-5:]
+def pack_kernel(counts, other_counts, table_in, retrieved_in, cache, other_in, *rest):
+    outs, (whole, table, retrieved, other, sems, list_sems) = rest[:-6], rest[-6:]
     lists = [
         pltpu.make_async_copy(source, target, list_sems.at[i])
         for i, (source, target) in enumerate(
-            ((table_in, table), (retrieved_in, retrieved))
+            ((table_in, table), (retrieved_in, retrieved), (other_in, other))
         )
     ]
     for copy in lists:
@@ -234,41 +234,59 @@
     for copy in lists:
         copy.wait()
     listed = retrieved.shape[2]
-    lane = lax.broadcasted_iota(jnp.int32, (TAIL, HEAD_DIM), 1)
-    note = jnp.where(lane == listed, counts[0, 0], 0)
-    for k in range(listed):
-        note = jnp.where(lane == k, table[retrieved[0, 0, k]], note)
-    note = note.astype(jnp.float32).astype(jnp.bfloat16)
-    for out in outs:
-        out[lines * 2 * tokens :, :] = note
+    lane = lax.broadcasted_iota(jnp.int32, (TAIL // 2, HEAD_DIM), 1)
+    notes = []
+    for ids, count in ((retrieved, counts), (other, other_counts)):
+        note = jnp.where(lane == listed, count[0, 0], 0)
+        for k in range(listed):
+            note = jnp.where(lane == k, table[ids[0, 0, k]], note)
+        notes.append(note.astype(jnp.float32))
+    note = jnp.concatenate(notes, axis=0).astype(jnp.bfloat16)
+    for out in outs[:-1]:
+        out[out.shape[0] - TAIL :, :] = note
+    split = outs[-2].shape[0] - TAIL
+    targets = [(0, outs[0]), (1, outs[1]), (3, outs[2]), (2, outs[3])]
     for line in range(lines):
         copies[line].wait()
-        for k, out in enumerate(outs):
+        for k, whole_out in targets:
             head = lax.bitwise_xor(my_place()[1], k)
             for part in range(2):
                 columns = pl.ds(pl.multiple_of(part * width + head * HEAD_DIM, HEAD_DIM), HEAD_DIM)
-                at = (line * 2 + part) * tokens
+                at, out = (line * 2 + part) * tokens, whole_out
+                if k == 2 and at >= split:
+                    at, out = at - split, outs[-1]
                 out[at : at + tokens, :] = whole[line, :, columns]
 
 
-def pack(table, retrieved, counts, cache):
+def pack(table, retrieved, counts, other_retrieved, other_counts, cache):
     rows, tokens = cache.shape[1], cache.shape[2]
+    full = rows * 2 * tokens
+    early = full // tokens * 5 // 8 * tokens
     return pl.pallas_call(
         pack_kernel,
-        out_shape=[pltpu.VMEM((rows * 2 * tokens + TAIL, HEAD_DIM), cache.dtype)] * KV_HEADS,
-        in_specs=[SMEM] + [HBM] * 3,
-        out_specs=[VMEM] * KV_HEADS,
+        out_shape=[
+            pltpu.VMEM((height, HEAD_DIM), cache.dtype)
+            for height in [full + TAIL] * (KV_HEADS - 1) + [early + TAIL, full - early]
+        ],
+        in_specs=[SMEM] * 2 + [HBM] * 3 + [ANYWHERE],
+        out_specs=[VMEM] * (KV_HEADS + 1),
         scratch_shapes=[
             pltpu.VMEM(cache.shape[1:], cache.dtype),
             pltpu.SMEM(table.shape, table.dtype),
             pltpu.SMEM(retrieved.shape, retrieved.dtype),
+            pltpu.SMEM(retrieved.shape, retrieved.dtype),
             pltpu.SemaphoreType.DMA((rows,)),
-            pltpu.SemaphoreType.DMA((2,)),
+            pltpu.SemaphoreType.DMA((3,)),
         ],
         compiler_params=pltpu.CompilerParams(vmem_limit_bytes=6 * MIB),
         cost_estimate=pl.CostEstimate(flops=0, bytes_accessed=0, transcendentals=0),
         name="pack",
-    )(counts, *[pltpu.with_memory_space_constraint(a, pltpu.HBM) for a in (table, retrieved, cache)])
+    )(
+        counts,
+        other_counts,
+        *[pltpu.with_memory_space_constraint(a, pltpu.HBM) for a in (table, retrieved, cache)],
+        other_retrieved,
+    )
 
 
 def project_kernel(*refs):
@@ -335,24 +353,31 @@
     )(in_vmem(normed), in_vmem(wq))
 
 
-def attend_kernel(q, kv_mine, kv_other, *refs):
-    count = 2 * KV_HEADS
-    held, (out, blocks, placed, scored, notes, tail_vm, meta, sems, note_sems) = refs[:count], refs[count:]
-    requests, listed = scored.shape[:2]
-    tokens = q.shape[0]
+def attend_kernel(listed, requests, q_mine, q_other, kv_mine, kv_other, *refs):
+    *held, late = refs[: KV_HEADS + 1]
+    mine, give, scored, notes, meta, line_of, live_of, joined, note_sem, sems = refs[KV_HEADS + 1 :]
+    early = held[2].shape[0] - TAIL
+    copies = [
+        pltpu.make_async_copy(held[2].at[pl.ds(0, early)], joined.at[pl.ds(0, early)], sems.at[0]),
+        pltpu.make_async_copy(late, joined.at[pl.ds(early, late.shape[0])], sems.at[1]),
+    ]
+    for copy in copies:
+        copy.start()
+    tokens = q_mine.shape[0]
     question = tokens // requests
-    heads = q.shape[1] // HEAD_DIM
+    heads = q_mine.shape[1] // HEAD_DIM
     group = heads * question
     block = scored.shape[3]
-    rows = (blocks.shape[1] - TAIL) // (2 * block)
+    end = held[0].shape[0] - TAIL
+    rows = end // (2 * block)
     me, pair, core = my_place()
-    tail = pl.ds(rows * 2 * block, TAIL)
-    tails = [
-        pltpu.make_async_copy(held[i].at[tail], tail_vm.at[i], note_sems.at[i]) for i in range(count)
-    ]
-    copies = [pltpu.make_async_copy(held[i], blocks.at[i], sems.at[i]) for i in range(count)]
-    for copy in tails + copies:
-        copy.start()
+    tails = [h[h.shape[0] - TAIL :, :].astype(jnp.float32) for h in held]
+    held[2] = joined
+    notes[...] = jnp.concatenate(
+        [tail[at : at + 1] for tail in tails for at in (0, TAIL // 2)], axis=0
+    ).astype(jnp.int32)
+    noted = pltpu.make_async_copy(notes, meta, note_sem)
+    noted.start()
     scale = HEAD_DIM ** (-0.5)
     first = core == 0
     half = HEAD_DIM // 2
@@ -360,23 +385,17 @@
     lo, hi = jnp.where(first, a, b), jnp.where(first, b, a)
     own_key = jnp.concatenate([lo[:, :half], hi[:, :half]], axis=1).astype(jnp.bfloat16)
     own_value = jnp.concatenate([lo[:, half:], hi[:, half:]], axis=1).astype(jnp.bfloat16)
-    wide = q[...].astype(jnp.float32)
-    queries = []
-    for r in range(requests):
-        piece = wide[r * question : (r + 1) * question]
-        queries.append(
-            jnp.concatenate(
-                [piece[:, h * HEAD_DIM : (h + 1) * HEAD_DIM] for h in range(heads)], axis=0
-            ).astype(jnp.bfloat16)
-        )
-    stacked = jnp.concatenate(queries, axis=0)
-    for copy in tails:
-        copy.wait()
-    notes[...] = jnp.concatenate(
-        [tail_vm[i].astype(jnp.float32)[:1] for i in range(count)], axis=0
-    ).astype(jnp.int32)
-    noted = pltpu.make_async_copy(notes, meta, note_sems.at[count])
-    noted.start()
+    wide = [q_mine[...].astype(jnp.float32), q_other[...].astype(jnp.float32)]
+
+    def rows_of(side, r):
+        piece = wide[side][r * question : (r + 1) * question]
+        return [piece[:, h * HEAD_DIM : (h + 1) * HEAD_DIM] for h in range(heads)]
+
+    queries = [
+        jnp.concatenate(rows_of(0, r) + rows_of(1, r), axis=0).astype(jnp.bfloat16)
+        for r in range(requests)
+    ]
+    stacked = jnp.concatenate([query[:group] for query in queries], axis=0)
     scores = matmul(stacked, own_key, ((1,), (1,))) * scale
     row = lax.broadcasted_iota(jnp.int32, scores.shape, 0)
     column = lax.broadcasted_iota(jnp.int32, scores.shape, 1)
@@ -385,73 +404,113 @@
     weights = jnp.where(seen, jnp.exp(scores - own_top), 0.0)
     own_total = jnp.sum(weights, axis=-1, keepdims=True)
     own_acc = matmul(weights.astype(jnp.bfloat16), own_value)
+    for i in range(requests * KV_HEADS):
+        line_of[i] = 0
+        live_of[i] = 0
     noted.wait()
+    for r in range(requests):
+        at = lax.bitwise_xor(me, r)
+        live = meta[at, listed]
+        for k in range(listed):
+            slot = meta[at, k]
+            owner = lax.div(slot, rows)
+            away = lax.bitwise_xor(lax.div(owner, CORES), pair)
+            i = jnp.where(lax.rem(owner, CORES) == core, r * KV_HEADS + away, requests * KV_HEADS)
+            line_of[i] = lax.rem(slot, rows)
+            live_of[i] = (k < live).astype(jnp.int32)
     for copy in copies:
         copy.wait()
-    lives, places = [], []
     for r in range(requests):
-        at = lax.bitwise_xor(me, r)
-        lives.append(meta[at, listed])
-        for k in range(listed):
-            slot = meta[at, k]
-            source = lax.bitwise_xor(me, slot // rows)
-            key_at = pl.multiple_of(lax.rem(slot, rows) * 2 * block, block)
-            places.append((source, key_at))
-            scored[r, k] = matmul(queries[r], blocks[source, pl.ds(key_at, block), :], ((1,), (1,))) * scale
+        for j in range(KV_HEADS):
+            at = pl.multiple_of(line_of[r * KV_HEADS + j] * 2 * block, block)
+            scored[r, j] = matmul(queries[r], held[j][pl.ds(at, block), :], ((1,), (1,))) * scale
     scores = scored[...]
     tops = jnp.max(scores, axis=-1, keepdims=True)
     weights = jnp.exp(scores - tops)
     totals = jnp.sum(weights, axis=-1, keepdims=True)
     scored[...] = weights
+    lane = lax.broadcasted_iota(jnp.int32, (group, HEAD_DIM), 1)
     for r in range(requests):
-        mine = slice(r * group, (r + 1) * group)
-        live = lives[r]
-        accs, marks = [], []
-        for k in range(listed):
-            source, key_at = places[r * listed + k]
-            values = blocks[source, pl.ds(key_at + block, block), :]
-            accs.append(matmul(scored[r, k].astype(jnp.bfloat16), values))
-            marks.append(jnp.where(k < live, tops[r, k], far_below))
-        peak = own_top[mine]
-        for mark in marks:
-            peak = jnp.maximum(peak, mark)
-        factor = jnp.exp(own_top[mine] - peak)
-        numerator, denominator = own_acc[mine] * factor, own_total[mine] * factor
-        for k in range(listed):
-            factor = jnp.where(k < live, jnp.exp(marks[k] - peak), 0.0)
-            numerator = numerator + accs[k] * factor
-            denominator = denominator + totals[r, k] * factor
-        context = numerator / denominator
-        for h in range(heads):
-            placed[r * question : (r + 1) * question, h * HEAD_DIM : (h + 1) * HEAD_DIM] = context[
-                h * question : (h + 1) * question
-            ]
-    out[...] = placed[...].astype(out.dtype)
-
-
-def attend(q, kv_mine, kv_other, held, requests, listed, block):
-    count = len(held)
-    return pl.pallas_call(
-        attend_kernel,
-        out_shape=pltpu.VMEM(q.shape, jnp.bfloat16),
-        in_specs=[VMEM] * 3 + [ANYWHERE] * count,
-        out_specs=VMEM,
+        span = slice(r * group, (r + 1) * group)
+        accs, marks, lives = [], [], []
+        for j in range(KV_HEADS):
+            at = pl.multiple_of(line_of[r * KV_HEADS + j] * 2 * block + block, block)
+            accs.append(matmul(scored[r, j].astype(jnp.bfloat16), held[j][pl.ds(at, block), :]))
+            lives.append(live_of[r * KV_HEADS + j] > 0)
+            marks.append(jnp.where(lives[j], tops[r, j], far_below))
+        highest = functools.reduce(jnp.maximum, marks)
+        for side, out in enumerate((mine, give)):
+            part = slice(side * group, (side + 1) * group)
+            peak = highest[part]
+            if side == 0:
+                peak = jnp.maximum(peak, own_top[span])
+                factor = jnp.exp(own_top[span] - peak)
+                numerator, denominator = own_acc[span] * factor, own_total[span] * factor
+            else:
+                numerator, denominator = jnp.zeros((group, HEAD_DIM), jnp.float32), jnp.zeros_like(peak)
+            for j in range(KV_HEADS):
+                factor = jnp.where(lives[j], jnp.exp(marks[j][part] - peak), 0.0)
+                numerator = numerator + accs[j][part] * factor
+                denominator = denominator + totals[r, j][part] * factor
+            out[span, :] = numerator
+            stats = slice(requests * group + r * group, requests * group + (r + 1) * group)
+            out[stats, :] = jnp.where(lane == 0, peak, denominator)
+
+
+def attend(q_mine, q_other, kv_mine, kv_other, held, requests, listed, block):
+    rows = q_mine.size // HEAD_DIM
+    shape = pltpu.VMEM((2 * rows, HEAD_DIM), jnp.float32)
+    return pl.pallas_call(
+        functools.partial(attend_kernel, listed, requests),
+        out_shape=[shape] * 2,
+        in_specs=[VMEM] * (4 + len(held)),
+        out_specs=[VMEM] * 2,
         scratch_shapes=[
-            pltpu.VMEM((count, *held[0].shape), jnp.bfloat16),
-            pltpu.VMEM(q.shape, jnp.float32),
-            pltpu.VMEM((requests, listed, q.size // HEAD_DIM // requests, block), jnp.float32),
-            pltpu.VMEM((count, HEAD_DIM), jnp.int32),
-            pltpu.VMEM((count, TAIL, HEAD_DIM), jnp.bfloat16),
-            pltpu.SMEM((count, HEAD_DIM), jnp.int32),
-            pltpu.SemaphoreType.DMA((count,)),
-            pltpu.SemaphoreType.DMA((count + 1,)),
+            pltpu.VMEM((requests, KV_HEADS, 2 * rows // requests, block), jnp.float32),
+            pltpu.VMEM((requests, HEAD_DIM), jnp.int32),
+            pltpu.SMEM((requests, HEAD_DIM), jnp.int32),
+            pltpu.SMEM((requests * KV_HEADS + 1,), jnp.int32),
+            pltpu.SMEM((requests * KV_HEADS + 1,), jnp.int32),
+            pltpu.VMEM((held[0].shape[0] - TAIL, HEAD_DIM), jnp.bfloat16),
+            pltpu.SemaphoreType.DMA,
+            pltpu.SemaphoreType.DMA((2,)),
         ],
-        compiler_params=pltpu.CompilerParams(vmem_limit_bytes=16 * MIB),
+        compiler_params=pltpu.CompilerParams(vmem_limit_bytes=12 * MIB),
         cost_estimate=pl.CostEstimate(
             flops=1 << 28, bytes_accessed=2 * MIB, transcendentals=1 << 18
         ),
         name="attend",
-    )(in_vmem(q), in_vmem(kv_mine), in_vmem(kv_other), *held)
+    )(*[in_vmem(a) for a in (q_mine, q_other, kv_mine, kv_other, *held)])
+
+
+def merge_kernel(requests, mine, got, out, placed):
+    rows = mine.shape[0] // 2
+    question = out.shape[0] // requests
+    heads = out.shape[1] // HEAD_DIM
+    (sum_a, stat_a), (sum_b, stat_b) = ((a[:rows, :], a[rows:, :]) for a in (mine, got))
+    peak = jnp.maximum(stat_a[:, :1], stat_b[:, :1])
+    factor_a, factor_b = jnp.exp(stat_a[:, :1] - peak), jnp.exp(stat_b[:, :1] - peak)
+    total = stat_a[:, 1:2] * factor_a + stat_b[:, 1:2] * factor_b
+    context = (sum_a * factor_a + sum_b * factor_b) / total
+    for r in range(requests):
+        for h in range(heads):
+            at = (r * heads + h) * question
+            placed[r * question : (r + 1) * question, h * HEAD_DIM : (h + 1) * HEAD_DIM] = context[
+                at : at + question
+            ]
+    out[...] = placed[...].astype(out.dtype)
+
+
+def merge(mine, got, requests, q):
+    return pl.pallas_call(
+        functools.partial(merge_kernel, requests),
+        out_shape=pltpu.VMEM(q.shape, jnp.bfloat16),
+        in_specs=[VMEM] * 2,
+        out_specs=VMEM,
+        scratch_shapes=[pltpu.VMEM(q.shape, jnp.float32)],
+        compiler_params=pltpu.CompilerParams(vmem_limit_bytes=6 * MIB),
+        name="merge",
+    )(in_vmem(mine), in_vmem(got))
 
 
 def partial_kernel(*refs):
@@ -571,23 +630,27 @@
     size, sections = lax.axis_size("dev"), lax.axis_size("segment")
     state = hidden[0]
     gathered = {2: to_pair(state, 2), 1: to_pair(state, 1)}
-    packed = pack(block_slot, retrieved, counts, cache)
+    packed = pack(block_slot, retrieved, counts, to_partner(retrieved), to_partner(counts), cache)
     weights = load(w_query, w_key[0].swapaxes(0, 1), w_value[0].swapaxes(0, 1))
-    blocks = {k: to_pair(packed[k], k) for k in (3, 2)}
+    early = to_pair(packed[3], 2)
     gathered[2], packed = lax.optimization_barrier((gathered[2], packed))
     gathered[3] = to_pair(gathered[2], 1)
+    late = to_pair(packed[4], 2)
+    blocks = {3: to_pair(packed[2], 3)}
     near, gathered[1] = lax.optimization_barrier((packed[1], gathered[1]))
     blocks[1] = to_pair(near, 1)
+    gathered[3], early, late = lax.optimization_barrier((gathered[3], early, late))
     mine, gathered, weights = lax.optimization_barrier((state, gathered, weights))
     wq, wk, wv = weights
     parts = [p for a in (mine, *(gathered[k] for k in (1, 2, 3))) for p in (a, to_partner(a))]
     normed, kv, cols = project(parts, gain, wk, wv)
-    kv_other = to_partner(kv)
     q = query(normed, wq)
-    own, blocks, q = lax.optimization_barrier((packed[0], blocks, q))
-    blocks[0] = own
-    held = [h for k in range(KV_HEADS) for h in (blocks[k], to_partner(blocks[k]))]
-    context = attend(q, kv, kv_other, held, size, retrieved.shape[2], cache.shape[2])
+    blocks, q = lax.optimization_barrier((blocks, q))
+    held = [packed[0], blocks[1], early, blocks[3], late]
+    mine, give = attend(
+        q, to_partner(q), kv, to_partner(kv), held, size, retrieved.shape[2], cache.shape[2]
+    )
+    context = merge(mine, to_partner(give), size, q)
     contexts = {0: context, 2: to_pair(context, 2), 1: to_pair(context, 1)}
     contexts[3] = to_pair(contexts[2], 1)
     contexts = [p for k in range(KV_HEADS) for p in (contexts[k], to_partner(contexts[k]))]

time: 67.7 us -> 67 us (0.990)
  waiting for transfers between devices: 27.5 us -> 19.7 us
  starting transfers between devices: 25.3 us -> 31.3 us
  Pallas kernels: 13.9 us -> 15 us
    ppermute x9 -> x10, waiting for transfers between devices: 16.3 us -> 8.52 us  [to_pair(): return lax.ppermute(x, 'dev', [(d, d ^ CORES * k) for d in range(size)])]
    ppermute x9 -> x10, starting transfers between devices: 18 us -> 23.6 us  [to_pair(): return lax.ppermute(x, 'dev', [(d, d ^ CORES * k) for d in range(size)])]
    pallas_call x2 -> x3, Pallas kernels: 4.14 us -> 5.25 us  [the longest x1 3.06 us: attend(): pl.pallas_call(functools.partial(attend_kernel, listed, requests), out_sh...]
    ppermute x2, waiting for transfers between devices: 5.01 us -> 4.09 us  [by_head(): piece = lax.ppermute(piece, ('segment', 'dev'), route)]
    ppermute x16, waiting for transfers between devices: 6.22 us -> 7.1 us  [to_partner(): lax.ppermute(x, 'dev', [(d, d ^ 1) for d in range(lax.axis_size('dev'))])]
  transfers between devices with their start and end apart: 27 -> 28, of which waited for: 14 -> 16; matrix products, arithmetic and copies ran while one was open for 0% -> 0% of each run, Pallas kernels for 14% -> 15%
where the time goes in v5:
time: 67 us; the launch traced here: 66.9 us
  starting transfers between devices  31.3 us (47%)
  waiting for transfers between devices  19.7 us (29%)
  Pallas kernels  15 us (22%)
  between operations  0.83 us (1%)
    ppermute x10, starting transfers between devices, to_pair(): return lax.ppermute(x, 'dev', [(d, d ^ CORES * k) for d in range(size)])  23.6 us
    ppermute x10, waiting for transfers between devices, to_pair(): return lax.ppermute(x, 'dev', [(d, d ^ CORES * k) for d in range(size)])  8.52 us
    ppermute x16, waiting for transfers between devices, to_partner(): lax.ppermute(x, 'dev', [(d, d ^ 1) for d in range(lax.axis_size('dev'))])  7.1 us
    ppermute x2, starting transfers between devices, by_head(): piece = lax.ppermute(piece, ('segment', 'dev'), route)  4.69 us
    pallas_call x1, Pallas kernels, load(): pl.pallas_call(functools.partial(load_kernel, len(arrays)), out_shape=[pl...  4.19 us
    ppermute x2, waiting for transfers between devices, by_head(): piece = lax.ppermute(piece, ('segment', 'dev'), route)  4.09 us
    pallas_call x1, Pallas kernels, attend(): pl.pallas_call(functools.partial(attend_kernel, listed, requests), out_sh...  3.06 us
    ppermute x16, starting transfers between devices, to_partner(): lax.ppermute(x, 'dev', [(d, d ^ 1) for d in range(lax.axis_size('dev'))])  3.01 us
  transfers between devices with their start and end apart: 28, of which 16 were waited for; matrix products, arithmetic and copies ran while one was open for 0% of the time, Pallas kernels for 15%

profile of v5, /device:TPU:0, one launch (start us, length us, event | category | flops | bytes accessed | tf_op | source)
XLA Modules:
  0.0 66.9 jit_solution(9352565181845458928)
XLA Ops:
  0.0 4.0 %collective-permute-start = (bf16[8,8192]{1,0:T(8,128)(2,1)}, bf16[8,8192]{1,0:T(8,128)(2,1)S(1)}, u32[]{:S(2)}, u32[]{:S(2)}) collective-permute-start(bf16[8,8192]{1,0:T(8,128)(2,1)} %bitcast.12), channel_id=1, source_target_pairs={{0,4},{1,5},{2,6},{3,7},{4,0},{5,1},{6,2},{7,3},{8,12},{9,13},{10,... | collective-permute-start | bytes 393224 | tf_op jit(solution)/shard_map/ppermute | solution.py:159
  4.0 0.5 collective-permute-start.1
  5.6 1.9 %pack.1 = (bf16[1040,128]{1,0:T(8,128)(2,1)S(1)}, bf16[1040,128]{1,0:T(8,128)(2,1)S(1)}, bf16[1040,128]{1,0:T(8,128)(2,1)S(1)}, bf16[656,128]{1,0:T(8,128)(2,1)S(1)}, bf16[384,128]{1,0:T(8,128)(2,1)S(1)}) custom-call(s32[1,1]{1,0:T(1,128)S(6)} %copy.11.counts, s32[1,1]{1,0:T(1,128)} %collective-permute-done.1.other_counts, s32[32]{0:T(128)} %table_in.1, ...), custom_call_target="tpu_custom_call" | custom-call | tf_op jit(solution)/shard_map/pack/pallas_call | solution.py:265
  7.7 1.8 %collective-permute-start.3 = (bf16[8,8192]{1,0:T(8,128)(2,1)}, bf16[8,8192]{1,0:T(8,128)(2,1)S(1)}, u32[]{:S(2)}, u32[]{:S(2)}) collective-permute-start(bf16[8,8192]{1,0:T(8,128)(2,1)} %bitcast.13), channel_id=1, source_target_pairs={{0,2},{1,3},{2,0},{3,1},{4,6},{5,7},{6,4},{7,5},{8,10},{9,11},{10,... | collective-permute-start | bytes 393224 | tf_op jit(solution)/shard_map/ppermute | solution.py:159
  9.6 1.1 %collective-permute-done.refs_4_ = bf16[8,8192]{1,0:T(8,128)(2,1)S(1)} collective-permute-done((bf16[8,8192]{1,0:T(8,128)(2,1)}, bf16[8,8192]{1,0:T(8,128)(2,1)S(1)}, u32[]{:S(2)}, u32[]{:S(2)}) %collective-permute-start) | collective-permute-done | bytes 131104 | tf_op jit(solution)/shard_map/ppermute | solution.py:159
  10.6 4.5 %collective-permute-start.6 = (bf16[8,8192]{1,0:T(8,128)(2,1)S(1)}, bf16[8,8192]{1,0:T(8,128)(2,1)S(1)}, u32[]{:S(2)}, u32[]{:S(2)}) collective-permute-start(bf16[8,8192]{1,0:T(8,128)(2,1)S(1)} %collective-permute-done.refs_4_), channel_id=1, source_target_pairs={{0,2},{1,3},{2,0},{3,1},{4,6},{5,7},{6,4},{7,5},{8,10},{9,11},{10,... | collective-permute-start | bytes 393224 | tf_op jit(solution)/shard_map/ppermute | solution.py:159
  15.1 3.3 %collective-permute-start.8 = (bf16[384,128]{1,0:T(8,128)(2,1)S(1)}, bf16[384,128]{1,0:T(8,128)(2,1)S(1)}, u32[]{:S(2)}, u32[]{:S(2)}) collective-permute-start(bf16[384,128]{1,0:T(8,128)(2,1)S(1)} %get-tuple-element.52), channel_id=1, source_target_pairs={{0,4},{1,5},{2,6},{3,7},{4,0},{5,1},{6,2},{7,3},{8,12},{9,13},{10,... | collective-permute-start | bytes 294920 | tf_op jit(solution)/shard_map/ppermute | solution.py:159
  18.5 5.8 %collective-permute-start.5 = (bf16[1040,128]{1,0:T(8,128)(2,1)S(1)}, bf16[1040,128]{1,0:T(8,128)(2,1)S(1)}, u32[]{:S(2)}, u32[]{:S(2)}) collective-permute-start(bf16[1040,128]{1,0:T(8,128)(2,1)S(1)} %get-tuple-element.49), channel_id=1, source_target_pairs={{0,6},{1,7},{2,4},{3,5},{4,2},{5,3},{6,0},{7,1},{8,14},{9,15},{10,... | collective-permute-start | bytes 798728 | tf_op jit(solution)/shard_map/ppermute | solution.py:159
  24.3 4.2 %load.1 = (bf16[8192,512]{1,0:T(8,128)(2,1)S(1)}, bf16[64,8192]{1,0:T(8,128)(2,1)S(1)}, bf16[64,8192]{1,0:T(8,128)(2,1)S(1)}) custom-call(bf16[1,8192,512]{2,1,0:T(8,128)(2,1)} %refs_0_.1, bf16[64,8192]{1,0:T(8,128)(2,1)} %bitcast.16, bf16[64,8192]{1,0:T(8,128)(2,1)} %bitcast.17), custom_call_target="tpu_custom_call" | custom-call | tf_op jit(solution)/shard_map/load/pallas_call | solution.py:205
  28.6 0.5 collective-permute-start.10
  29.2 0.8 %collective-permute-done.9.refs_1_ = bf16[8,8192]{1,0:T(8,128)(2,1)S(1)} collective-permute-done((bf16[8,8192]{1,0:T(8,128)(2,1)S(1)}, bf16[8,8192]{1,0:T(8,128)(2,1)S(1)}, u32[]{:S(2)}, u32[]{:S(2)}) %collective-permute-start.9) | collective-permute-done | bytes 131104 | tf_op jit(solution)/shard_map/ppermute | solution.py:163
  30.5 0.8 %collective-permute-done.12.refs_7_ = bf16[8,8192]{1,0:T(8,128)(2,1)S(1)} collective-permute-done((bf16[8,8192]{1,0:T(8,128)(2,1)S(1)}, bf16[8,8192]{1,0:T(8,128)(2,1)S(1)}, u32[]{:S(2)}, u32[]{:S(2)}) %collective-permute-start.12) | collective-permute-done | bytes 131104 | tf_op jit(solution)/shard_map/ppermute | solution.py:163
  31.3 1.6 %project.1 = (bf16[64,8192]{1,0:T(8,128)(2,1)S(1)}, bf16[64,128]{1,0:T(8,128)(2,1)S(1)}, bf16[64,1024]{1,0:T(8,128)(2,1)S(1)}) custom-call(bf16[8,8192]{1,0:T(8,128)(2,1)S(1)} %bitcast.15, bf16[8,8192]{1,0:T(8,128)(2,1)S(1)} %collective-permute-done.9.refs_1_, bf16[8,8192]{1,0:T(8,128)(2,1)S(1)} %collective-permute-done.3.refs_2_, ...), custom_call_target="tpu_custom_call" | custom-call | tf_op jit(solution)/shard_map/project/pallas_call | solution.py:321
  32.9 1.5 %query.1.q_mine = bf16[64,512]{1,0:T(8,128)(2,1)S(1)} custom-call(bf16[64,8192]{1,0:T(8,128)(2,1)S(1)} %get-tuple-element.63.normed, bf16[8192,512]{1,0:T(8,128)(2,1)S(1)} %get-tuple-element.64.wq), custom_call_target="tpu_custom_call" | custom-call | tf_op jit(solution)/shard_map/query/pallas_call | solution.py:343
  34.5 0.8 %collective-permute-done.5.refs_3_ = bf16[1040,128]{1,0:T(8,128)(2,1)S(1)} collective-permute-done((bf16[1040,128]{1,0:T(8,128)(2,1)S(1)}, bf16[1040,128]{1,0:T(8,128)(2,1)S(1)}, u32[]{:S(2)}, u32[]{:S(2)}) %collective-permute-start.5) | collective-permute-done | bytes 266272 | tf_op jit(solution)/shard_map/ppermute | solution.py:159
  35.3 0.5 collective-permute-start.14
  35.8 0.8 %collective-permute-done.14.kv_other = bf16[64,128]{1,0:T(8,128)(2,1)S(1)} collective-permute-done((bf16[64,128]{1,0:T(8,128)(2,1)S(1)}, bf16[64,128]{1,0:T(8,128)(2,1)S(1)}, u32[]{:S(2)}, u32[]{:S(2)}) %collective-permute-start.14) | collective-permute-done | bytes 16416 | tf_op jit(solution)/shard_map/ppermute | solution.py:163
  36.6 3.1 %attend.1 = (f32[512,128]{1,0:T(8,128)S(1)}, f32[512,128]{1,0:T(8,128)S(1)}) custom-call(bf16[64,512]{1,0:T(8,128)(2,1)S(1)} %query.1.q_mine, bf16[64,512]{1,0:T(8,128)(2,1)S(1)} %collective-permute-done.13.q_other, bf16[64,128]{1,0:T(8,128)(2,1)S(1)} %get-tuple-element.66.kv_mine, bf16[64,128]{1,0:T(8,128)(2,1)S(1)} %collective-permute-done.14.kv_other, ...), custom_call_target="tpu_custom_call" | custom-call | flops 268435456 | bytes 2097152 | tf_op jit(solution)/shard_map/attend/pallas_call | solution.py:463
  40.1 1.2 %collective-permute-done.15.got = f32[512,128]{1,0:T(8,128)S(1)} collective-permute-done((f32[512,128]{1,0:T(8,128)S(1)}, f32[512,128]{1,0:T(8,128)S(1)}, u32[]{:S(2)}, u32[]{:S(2)}) %collective-permute-start.15) | collective-permute-done | bytes 262176 | tf_op jit(solution)/shard_map/ppermute | solution.py:163
  41.6 1.5 %collective-permute-start.16 = (bf16[64,512]{1,0:T(8,128)(2,1)S(1)}, bf16[64,512]{1,0:T(8,128)(2,1)S(1)}, u32[]{:S(2)}, u32[]{:S(2)}) collective-permute-start(bf16[64,512]{1,0:T(8,128)(2,1)S(1)} %merge.1.refs_0_), channel_id=1, source_target_pairs={{0,4},{1,5},{2,6},{3,7},{4,0},{5,1},{6,2},{7,3},{8,12},{9,13},{10,... | collective-permute-start | bytes 196616 | tf_op jit(solution)/shard_map/ppermute | solution.py:159
  43.0 2.4 %collective-permute-start.21 = (bf16[64,512]{1,0:T(8,128)(2,1)S(1)}, bf16[64,512]{1,0:T(8,128)(2,1)S(1)}, u32[]{:S(2)}, u32[]{:S(2)}) collective-permute-start(bf16[64,512]{1,0:T(8,128)(2,1)S(1)} %merge.1.refs_0_), channel_id=1, source_target_pairs={{0,2},{1,3},{2,0},{3,1},{4,6},{5,7},{6,4},{7,5},{8,10},{9,11},{10,... | collective-permute-start | bytes 196616 | tf_op jit(solution)/shard_map/ppermute | solution.py:159
  45.4 3.0 %collective-permute-done.16.refs_0_ = bf16[64,512]{1,0:T(8,128)(2,1)S(1)} collective-permute-done((bf16[64,512]{1,0:T(8,128)(2,1)S(1)}, bf16[64,512]{1,0:T(8,128)(2,1)S(1)}, u32[]{:S(2)}, u32[]{:S(2)}) %collective-permute-start.16) | collective-permute-done | bytes 65568 | tf_op jit(solution)/shard_map/ppermute | solution.py:159
  49.0 3.7 %collective-permute-done.18.refs_2_ = bf16[64,512]{1,0:T(8,128)(2,1)S(1)} collective-permute-done((bf16[64,512]{1,0:T(8,128)(2,1)S(1)}, bf16[64,512]{1,0:T(8,128)(2,1)S(1)}, u32[]{:S(2)}, u32[]{:S(2)}) %collective-permute-start.18) | collective-permute-done | bytes 65568 | tf_op jit(solution)/shard_map/ppermute | solution.py:159
  52.7 0.8 %partial.1.refs_4_ = f32[64,1024]{1,0:T(8,128)S(1)} custom-call(bf16[64,512]{1,0:T(8,128)(2,1)S(1)} %merge.1.refs_0_, bf16[64,512]{1,0:T(8,128)(2,1)S(1)} %collective-permute-done.20.refs_1_, bf16[64,512]{1,0:T(8,128)(2,1)S(1)} %collective-permute-done.21.refs_2_, bf16[64,512]{1,0:T(8,128)(2,1)S(1)} %collective-permute-done.22.refs_3_, ...), custom_call_target="tpu_custom_call" | custom-call | flops 268435456 | bytes 4194304 | tf_op jit(solution)/shard_map/partial/pallas_call | solution.py:531
  53.9 0.9 %finish.1 = (bf16[32,1024]{1,0:T(8,128)(2,1)S(1)}, bf16[32,1024]{1,0:T(8,128)(2,1)S(1)}) custom-call(bf16[64,512]{1,0:T(8,128)(2,1)S(1)} %collective-permute-done.16.refs_0_, bf16[64,512]{1,0:T(8,128)(2,1)S(1)} %collective-permute-done.17.refs_1_, bf16[64,512]{1,0:T(8,128)(2,1)S(1)} %collective-permute-done.18.refs_2_, ...), custom_call_target="tpu_custom_call" | custom-call | flops 268435456 | bytes 4194304 | tf_op jit(solution)/shard_map/finish/pallas_call | solution.py:570
  55.0 1.1 %collective-permute-done.23.got = bf16[32,1024]{1,0:T(8,128)(2,1)S(1)} collective-permute-done((bf16[32,1024]{1,0:T(8,128)(2,1)S(1)}, bf16[32,1024]{1,0:T(8,128)(2,1)S(1)}, u32[]{:S(2)}, u32[]{:S(2)}) %collective-permute-start.23) | collective-permute-done | bytes 65568 | tf_op jit(solution)/shard_map/ppermute | solution.py:163
  56.1 3.2 %collective-permute-start.24 = (bf16[2,16,1024]{2,1,0:T(8,128)(2,1)S(1)}, bf16[2,16,1024]{2,1,0:T(8,128)(2,1)S(1)}, u32[]{:S(2)}, u32[]{:S(2)}) collective-permute-start(bf16[2,16,1024]{2,1,0:T(8,128)(2,1)S(1)} %get-tuple-element.77), channel_id=1, source_target_pairs={{0,14},{1,13},{2,12},{3,15},{4,10},{5,9},{6,8},{7,11},{8,22},{9,21... | collective-permute-start | bytes 196616 | tf_op jit(solution)/shard_map/ppermute | solution.py:666
  59.3 1.5 %collective-permute-start.26 = (bf16[2,16,1024]{2,1,0:T(8,128)(2,1)S(1)}, bf16[2,16,1024]{2,1,0:T(8,128)(2,1)S(1)}, u32[]{:S(2)}, u32[]{:S(2)}) collective-permute-start(bf16[2,16,1024]{2,1,0:T(8,128)(2,1)S(1)} %get-tuple-element.78), channel_id=1, source_target_pairs={{0,8},{1,11},{2,10},{3,9},{4,12},{5,15},{6,14},{7,13},{8,16},{9,19... | collective-permute-start | bytes 196616 | tf_op jit(solution)/shard_map/ppermute | solution.py:666
  60.8 3.6 %collective-permute-done.24.refs_0_ = bf16[2,16,1024]{2,1,0:T(8,128)(2,1)S(1)} collective-permute-done((bf16[2,16,1024]{2,1,0:T(8,128)(2,1)S(1)}, bf16[2,16,1024]{2,1,0:T(8,128)(2,1)S(1)}, u32[]{:S(2)}, u32[]{:S(2)}) %collective-permute-start.24) | collective-permute-done | bytes 65568 | tf_op jit(solution)/shard_map/ppermute | solution.py:666
  64.9 0.7 %collective-permute-done.25.refs_1_ = bf16[2,16,1024]{2,1,0:T(8,128)(2,1)S(1)} collective-permute-done((bf16[2,16,1024]{2,1,0:T(8,128)(2,1)S(1)}, bf16[2,16,1024]{2,1,0:T(8,128)(2,1)S(1)}, u32[]{:S(2)}, u32[]{:S(2)}) %collective-permute-start.25) | collective-permute-done | bytes 65568 | tf_op jit(solution)/shard_map/ppermute | solution.py:163
  65.7 0.5 collective-permute-done.27.refs_3_
  66.2 0.7 %place.1 = bf16[1,8,8192]{2,1,0:T(8,128)(2,1)} custom-call(bf16[2,16,1024]{2,1,0:T(8,128)(2,1)S(1)} %collective-permute-done.24.refs_0_, bf16[2,16,1024]{2,1,0:T(8,128)(2,1)S(1)} %collective-permute-done.25.refs_1_, bf16[2,16,1024]{2,1,0:T(8,128)(2,1)S(1)} %collective-permute-done.26.refs_2_, bf16[2,16,1024]{2,1,0:T(8,128)(2,1)S(1)} %collective-permute-done.27.refs_3_), custom_call_target="tpu_custom_call" | custom-call | tf_op jit(solution)/shard_map/place/pallas_call | solution.py:619
  (43 shorter events, 3.7 us)
Async XLA Ops:
  0.0 28.5 %copy-start = (bf16[1,8,8192]{2,1,0:T(8,128)(2,1)S(1)}, bf16[1,8,8192]{2,1,0:T(8,128)(2,1)}, u32[]{:S(2)}) copy-start(bf16[1,8,8192]{2,1,0:T(8,128)(2,1)} %param.10) | copy-start | bytes 393220
  0.0 31.3 %copy-start.1 = (f32[1,8192]{1,0:T(1,128)S(1)}, f32[1,8192]{1,0:T(1,128)}, u32[]{:S(2)}) copy-start(f32[1,8192]{1,0:T(1,128)} %refs_8_.1) | copy-start | bytes 98308
  0.0 10.6 %collective-permute-start = (bf16[8,8192]{1,0:T(8,128)(2,1)}, bf16[8,8192]{1,0:T(8,128)(2,1)S(1)}, u32[]{:S(2)}, u32[]{:S(2)}) collective-permute-start(bf16[8,8192]{1,0:T(8,128)(2,1)} %bitcast.12), channel_id=1, source_target_pairs={{0,4},{1,5},{2,6},{3,7},{4,0},{5,1},{6,2},{7,3},{8,12},{9,13},{10,... | collective-permute-start | bytes 393224 | tf_op jit(solution)/shard_map/ppermute | solution.py:159
  4.0 1.6 %collective-permute-start.2 = (s32[1,1,6]{2,1,0:T(1,128)}, s32[1,1,6]{2,1,0:T(1,128)S(1)}, u32[]{:S(2)}, u32[]{:S(2)}) collective-permute-start(s32[1,1,6]{2,1,0:T(1,128)} %retrieved_in.1), channel_id=1, source_target_pairs={{0,1},{1,0},{2,3},{3,2},{4,5},{5,4},{6,7},{7,6},{8,9},{9,8},{10,11... | collective-permute-start | bytes 80 | tf_op jit(solution)/shard_map/ppermute | solution.py:163
  4.0 1.6 %collective-permute-start.1 = (s32[1,1]{1,0:T(1,128)}, s32[1,1]{1,0:T(1,128)}, u32[]{:S(2)}, u32[]{:S(2)}) collective-permute-start(s32[1,1]{1,0:T(1,128)} %param.19), channel_id=1, source_target_pairs={{0,1},{1,0},{2,3},{3,2},{4,5},{5,4},{6,7},{7,6},{8,9},{9,8},{10,11... | collective-permute-start | bytes 20 | tf_op jit(solution)/shard_map/ppermute | solution.py:163
  7.6 20.9 %collective-permute-start.7 = (bf16[656,128]{1,0:T(8,128)(2,1)S(1)}, bf16[656,128]{1,0:T(8,128)(2,1)S(1)}, u32[]{:S(2)}, u32[]{:S(2)}) collective-permute-start(bf16[656,128]{1,0:T(8,128)(2,1)S(1)} %get-tuple-element.45), channel_id=1, source_target_pairs={{0,4},{1,5},{2,6},{3,7},{4,0},{5,1},{6,2},{7,3},{8,12},{9,13},{10,... | collective-permute-start | bytes 503816 | tf_op jit(solution)/shard_map/ppermute | solution.py:159
  7.7 10.7 %collective-permute-start.3 = (bf16[8,8192]{1,0:T(8,128)(2,1)}, bf16[8,8192]{1,0:T(8,128)(2,1)S(1)}, u32[]{:S(2)}, u32[]{:S(2)}) collective-permute-start(bf16[8,8192]{1,0:T(8,128)(2,1)} %bitcast.13), channel_id=1, source_target_pairs={{0,2},{1,3},{2,0},{3,1},{4,6},{5,7},{6,4},{7,5},{8,10},{9,11},{10,... | collective-permute-start | bytes 393224 | tf_op jit(solution)/shard_map/ppermute | solution.py:159
  10.6 17.9 %collective-permute-start.6 = (bf16[8,8192]{1,0:T(8,128)(2,1)S(1)}, bf16[8,8192]{1,0:T(8,128)(2,1)S(1)}, u32[]{:S(2)}, u32[]{:S(2)}) collective-permute-start(bf16[8,8192]{1,0:T(8,128)(2,1)S(1)} %collective-permute-done.refs_4_), channel_id=1, source_target_pairs={{0,2},{1,3},{2,0},{3,1},{4,6},{5,7},{6,4},{7,5},{8,10},{9,11},{10,... | collective-permute-start | bytes 393224 | tf_op jit(solution)/shard_map/ppermute | solution.py:159
  15.1 13.4 %collective-permute-start.8 = (bf16[384,128]{1,0:T(8,128)(2,1)S(1)}, bf16[384,128]{1,0:T(8,128)(2,1)S(1)}, u32[]{:S(2)}, u32[]{:S(2)}) collective-permute-start(bf16[384,128]{1,0:T(8,128)(2,1)S(1)} %get-tuple-element.52), channel_id=1, source_target_pairs={{0,4},{1,5},{2,6},{3,7},{4,0},{5,1},{6,2},{7,3},{8,12},{9,13},{10,... | collective-permute-start | bytes 294920 | tf_op jit(solution)/shard_map/ppermute | solution.py:159
  18.5 16.0 %collective-permute-start.4 = (bf16[1040,128]{1,0:T(8,128)(2,1)S(1)}, bf16[1040,128]{1,0:T(8,128)(2,1)S(1)}, u32[]{:S(2)}, u32[]{:S(2)}) collective-permute-start(bf16[1040,128]{1,0:T(8,128)(2,1)S(1)} %get-tuple-element.48), channel_id=1, source_target_pairs={{0,2},{1,3},{2,0},{3,1},{4,6},{5,7},{6,4},{7,5},{8,10},{9,11},{10,... | collective-permute-start | bytes 798728 | tf_op jit(solution)/shard_map/ppermute | solution.py:159
  18.5 16.8 %collective-permute-start.5 = (bf16[1040,128]{1,0:T(8,128)(2,1)S(1)}, bf16[1040,128]{1,0:T(8,128)(2,1)S(1)}, u32[]{:S(2)}, u32[]{:S(2)}) collective-permute-start(bf16[1040,128]{1,0:T(8,128)(2,1)S(1)} %get-tuple-element.49), channel_id=1, source_target_pairs={{0,6},{1,7},{2,4},{3,5},{4,2},{5,3},{6,0},{7,1},{8,14},{9,15},{10,... | collective-permute-start | bytes 798728 | tf_op jit(solution)/shard_map/ppermute | solution.py:159
  24.3 28.4 %slice-start = ((s8[8388608]{0:T(1024)(128)(4,1)}), s8[4194304]{0:T(1024)(128)(4,1)S(1)}, s32[]{:S(2)}) async-start(s8[8388608]{0:T(1024)(128)(4,1)} %bitcast.8), calls=%async_computation | async-start | bytes 8388608
  28.6 24.1 %slice-start.1 = ((s8[8388608]{0:T(1024)(128)(4,1)}), s8[4194304]{0:T(1024)(128)(4,1)S(1)}, s32[]{:S(2)}) async-start(s8[8388608]{0:T(1024)(128)(4,1)} %bitcast.8), calls=%async_computation.1 | async-start | bytes 8388608
  28.6 1.4 %collective-permute-start.9 = (bf16[8,8192]{1,0:T(8,128)(2,1)S(1)}, bf16[8,8192]{1,0:T(8,128)(2,1)S(1)}, u32[]{:S(2)}, u32[]{:S(2)}) collective-permute-start(bf16[8,8192]{1,0:T(8,128)(2,1)S(1)} %bitcast.14), channel_id=1, source_target_pairs={{0,1},{1,0},{2,3},{3,2},{4,5},{5,4},{6,7},{7,6},{8,9},{9,8},{10,11... | collective-permute-start | bytes 393224 | tf_op jit(solution)/shard_map/ppermute | solution.py:163
  28.6 1.5 %collective-permute-start.10 = (bf16[8,8192]{1,0:T(8,128)(2,1)S(1)}, bf16[8,8192]{1,0:T(8,128)(2,1)S(1)}, u32[]{:S(2)}, u32[]{:S(2)}) collective-permute-start(bf16[8,8192]{1,0:T(8,128)(2,1)S(1)} %collective-permute-done.3.refs_2_), channel_id=1, source_target_pairs={{0,1},{1,0},{2,3},{3,2},{4,5},{5,4},{6,7},{7,6},{8,9},{9,8},{10,11... | collective-permute-start | bytes 393224 | tf_op jit(solution)/shard_map/ppermute | solution.py:163
  29.1 1.3 %collective-permute-start.11 = (bf16[8,8192]{1,0:T(8,128)(2,1)S(1)}, bf16[8,8192]{1,0:T(8,128)(2,1)S(1)}, u32[]{:S(2)}, u32[]{:S(2)}) collective-permute-start(bf16[8,8192]{1,0:T(8,128)(2,1)S(1)} %collective-permute-done.refs_4_), channel_id=1, source_target_pairs={{0,1},{1,0},{2,3},{3,2},{4,5},{5,4},{6,7},{7,6},{8,9},{9,8},{10,11... | collective-permute-start | bytes 393224 | tf_op jit(solution)/shard_map/ppermute | solution.py:163
  30.0 1.3 %collective-permute-start.12 = (bf16[8,8192]{1,0:T(8,128)(2,1)S(1)}, bf16[8,8192]{1,0:T(8,128)(2,1)S(1)}, u32[]{:S(2)}, u32[]{:S(2)}) collective-permute-start(bf16[8,8192]{1,0:T(8,128)(2,1)S(1)} %collective-permute-done.6.refs_6_), channel_id=1, source_target_pairs={{0,1},{1,0},{2,3},{3,2},{4,5},{5,4},{6,7},{7,6},{8,9},{9,8},{10,11... | collective-permute-start | bytes 393224 | tf_op jit(solution)/shard_map/ppermute | solution.py:163
  35.3 1.4 %collective-permute-start.13 = (bf16[64,512]{1,0:T(8,128)(2,1)S(1)}, bf16[64,512]{1,0:T(8,128)(2,1)S(1)}, u32[]{:S(2)}, u32[]{:S(2)}) collective-permute-start(bf16[64,512]{1,0:T(8,128)(2,1)S(1)} %query.1.q_mine), channel_id=1, source_target_pairs={{0,1},{1,0},{2,3},{3,2},{4,5},{5,4},{6,7},{7,6},{8,9},{9,8},{10,11... | collective-permute-start | bytes 196616 | tf_op jit(solution)/shard_map/ppermute | solution.py:163
  35.3 1.3 %collective-permute-start.14 = (bf16[64,128]{1,0:T(8,128)(2,1)S(1)}, bf16[64,128]{1,0:T(8,128)(2,1)S(1)}, u32[]{:S(2)}, u32[]{:S(2)}) collective-permute-start(bf16[64,128]{1,0:T(8,128)(2,1)S(1)} %get-tuple-element.66.kv_mine), channel_id=1, source_target_pairs={{0,1},{1,0},{2,3},{3,2},{4,5},{5,4},{6,7},{7,6},{8,9},{9,8},{10,11... | collective-permute-start | bytes 49160 | tf_op jit(solution)/shard_map/ppermute | solution.py:163
  39.7 1.6 %collective-permute-start.15 = (f32[512,128]{1,0:T(8,128)S(1)}, f32[512,128]{1,0:T(8,128)S(1)}, u32[]{:S(2)}, u32[]{:S(2)}) collective-permute-start(f32[512,128]{1,0:T(8,128)S(1)} %get-tuple-element.73), channel_id=1, source_target_pairs={{0,1},{1,0},{2,3},{3,2},{4,5},{5,4},{6,7},{7,6},{8,9},{9,8},{10,11... | collective-permute-start | bytes 786440 | tf_op jit(solution)/shard_map/ppermute | solution.py:163
  41.6 6.8 %collective-permute-start.16 = (bf16[64,512]{1,0:T(8,128)(2,1)S(1)}, bf16[64,512]{1,0:T(8,128)(2,1)S(1)}, u32[]{:S(2)}, u32[]{:S(2)}) collective-permute-start(bf16[64,512]{1,0:T(8,128)(2,1)S(1)} %merge.1.refs_0_), channel_id=1, source_target_pairs={{0,4},{1,5},{2,6},{3,7},{4,0},{5,1},{6,2},{7,3},{8,12},{9,13},{10,... | collective-permute-start | bytes 196616 | tf_op jit(solution)/shard_map/ppermute | solution.py:159
  43.0 5.4 %collective-permute-start.21 = (bf16[64,512]{1,0:T(8,128)(2,1)S(1)}, bf16[64,512]{1,0:T(8,128)(2,1)S(1)}, u32[]{:S(2)}, u32[]{:S(2)}) collective-permute-start(bf16[64,512]{1,0:T(8,128)(2,1)S(1)} %merge.1.refs_0_), channel_id=1, source_target_pairs={{0,2},{1,3},{2,0},{3,1},{4,6},{5,7},{6,4},{7,5},{8,10},{9,11},{10,... | collective-permute-start | bytes 196616 | tf_op jit(solution)/shard_map/ppermute | solution.py:159
  48.4 4.3 %collective-permute-start.18 = (bf16[64,512]{1,0:T(8,128)(2,1)S(1)}, bf16[64,512]{1,0:T(8,128)(2,1)S(1)}, u32[]{:S(2)}, u32[]{:S(2)}) collective-permute-start(bf16[64,512]{1,0:T(8,128)(2,1)S(1)} %collective-permute-done.16.refs_0_), channel_id=1, source_target_pairs={{0,2},{1,3},{2,0},{3,1},{4,6},{5,7},{6,4},{7,5},{8,10},{9,11},{10,... | collective-permute-start | bytes 196616 | tf_op jit(solution)/shard_map/ppermute | solution.py:159
  48.4 4.2 %collective-permute-start.20 = (bf16[64,512]{1,0:T(8,128)(2,1)S(1)}, bf16[64,512]{1,0:T(8,128)(2,1)S(1)}, u32[]{:S(2)}, u32[]{:S(2)}) collective-permute-start(bf16[64,512]{1,0:T(8,128)(2,1)S(1)} %merge.1.refs_0_), channel_id=1, source_target_pairs={{0,1},{1,0},{2,3},{3,2},{4,5},{5,4},{6,7},{7,6},{8,9},{9,8},{10,11... | collective-permute-start | bytes 196616 | tf_op jit(solution)/shard_map/ppermute | solution.py:163
  48.5 4.2 %collective-permute-start.22 = (bf16[64,512]{1,0:T(8,128)(2,1)S(1)}, bf16[64,512]{1,0:T(8,128)(2,1)S(1)}, u32[]{:S(2)}, u32[]{:S(2)}) collective-permute-start(bf16[64,512]{1,0:T(8,128)(2,1)S(1)} %collective-permute-done.21.refs_2_), channel_id=1, source_target_pairs={{0,1},{1,0},{2,3},{3,2},{4,5},{5,4},{6,7},{7,6},{8,9},{9,8},{10,11... | collective-permute-start | bytes 196616 | tf_op jit(solution)/shard_map/ppermute | solution.py:163
  48.9 4.6 %collective-permute-start.17 = (bf16[64,512]{1,0:T(8,128)(2,1)S(1)}, bf16[64,512]{1,0:T(8,128)(2,1)S(1)}, u32[]{:S(2)}, u32[]{:S(2)}) collective-permute-start(bf16[64,512]{1,0:T(8,128)(2,1)S(1)} %collective-permute-done.16.refs_0_), channel_id=1, source_target_pairs={{0,1},{1,0},{2,3},{3,2},{4,5},{5,4},{6,7},{7,6},{8,9},{9,8},{10,11... | collective-permute-start | bytes 196616 | tf_op jit(solution)/shard_map/ppermute | solution.py:163
  52.7 1.3 %collective-permute-start.19 = (bf16[64,512]{1,0:T(8,128)(2,1)S(1)}, bf16[64,512]{1,0:T(8,128)(2,1)S(1)}, u32[]{:S(2)}, u32[]{:S(2)}) collective-permute-start(bf16[64,512]{1,0:T(8,128)(2,1)S(1)} %collective-permute-done.18.refs_2_), channel_id=1, source_target_pairs={{0,1},{1,0},{2,3},{3,2},{4,5},{5,4},{6,7},{7,6},{8,9},{9,8},{10,11... | collective-permute-start | bytes 196616 | tf_op jit(solution)/shard_map/ppermute | solution.py:163
  54.8 1.3 %collective-permute-start.23 = (bf16[32,1024]{1,0:T(8,128)(2,1)S(1)}, bf16[32,1024]{1,0:T(8,128)(2,1)S(1)}, u32[]{:S(2)}, u32[]{:S(2)}) collective-permute-start(bf16[32,1024]{1,0:T(8,128)(2,1)S(1)} %get-tuple-element.76), channel_id=1, source_target_pairs={{0,1},{1,0},{2,3},{3,2},{4,5},{5,4},{6,7},{7,6},{8,9},{9,8},{10,11... | collective-permute-start | bytes 196616 | tf_op jit(solution)/shard_map/ppermute | solution.py:163
  56.1 8.3 %collective-permute-start.24 = (bf16[2,16,1024]{2,1,0:T(8,128)(2,1)S(1)}, bf16[2,16,1024]{2,1,0:T(8,128)(2,1)S(1)}, u32[]{:S(2)}, u32[]{:S(2)}) collective-permute-start(bf16[2,16,1024]{2,1,0:T(8,128)(2,1)S(1)} %get-tuple-element.77), channel_id=1, source_target_pairs={{0,14},{1,13},{2,12},{3,15},{4,10},{5,9},{6,8},{7,11},{8,22},{9,21... | collective-permute-start | bytes 196616 | tf_op jit(solution)/shard_map/ppermute | solution.py:666
  59.3 5.6 %collective-permute-start.26 = (bf16[2,16,1024]{2,1,0:T(8,128)(2,1)S(1)}, bf16[2,16,1024]{2,1,0:T(8,128)(2,1)S(1)}, u32[]{:S(2)}, u32[]{:S(2)}) collective-permute-start(bf16[2,16,1024]{2,1,0:T(8,128)(2,1)S(1)} %get-tuple-element.78), channel_id=1, source_target_pairs={{0,8},{1,11},{2,10},{3,9},{4,12},{5,15},{6,14},{7,13},{8,16},{9,19... | collective-permute-start | bytes 196616 | tf_op jit(solution)/shard_map/ppermute | solution.py:666
  64.4 1.3 %collective-permute-start.25 = (bf16[2,16,1024]{2,1,0:T(8,128)(2,1)S(1)}, bf16[2,16,1024]{2,1,0:T(8,128)(2,1)S(1)}, u32[]{:S(2)}, u32[]{:S(2)}) collective-permute-start(bf16[2,16,1024]{2,1,0:T(8,128)(2,1)S(1)} %collective-permute-done.24.refs_0_), channel_id=1, source_target_pairs={{0,1},{1,0},{2,3},{3,2},{4,5},{5,4},{6,7},{7,6},{8,9},{9,8},{10,11... | collective-permute-start | bytes 196616 | tf_op jit(solution)/shard_map/ppermute | solution.py:163
  64.9 1.3 %collective-permute-start.27 = (bf16[2,16,1024]{2,1,0:T(8,128)(2,1)S(1)}, bf16[2,16,1024]{2,1,0:T(8,128)(2,1)S(1)}, u32[]{:S(2)}, u32[]{:S(2)}) collective-permute-start(bf16[2,16,1024]{2,1,0:T(8,128)(2,1)S(1)} %collective-permute-done.26.refs_2_), channel_id=1, source_target_pairs={{0,1},{1,0},{2,3},{3,2},{4,5},{5,4},{6,7},{7,6},{8,9},{9,8},{10,11... | collective-permute-start | bytes 196616 | tf_op jit(solution)/shard_map/ppermute | solution.py:163

commit v6 on v5

--- a/solution.py
+++ b/solution.py
@@ -261,7 +261,7 @@
 def pack(table, retrieved, counts, other_retrieved, other_counts, cache):
     rows, tokens = cache.shape[1], cache.shape[2]
     full = rows * 2 * tokens
-    early = full // tokens * 5 // 8 * tokens
+    early = full // tokens * 4 // 8 * tokens
     return pl.pallas_call(
         pack_kernel,
         out_shape=[
@@ -652,7 +652,7 @@
     )
     context = merge(mine, to_partner(give), size, q)
     contexts = {0: context, 2: to_pair(context, 2), 1: to_pair(context, 1)}
-    contexts[3] = to_pair(contexts[2], 1)
+    contexts[3] = to_pair(context, 3)
     contexts = [p for k in range(KV_HEADS) for p in (contexts[k], to_partner(contexts[k]))]
     before = partial_branch(contexts[:4], w_out[0])
     keep, give = finish(contexts[4:], before, cols, w_out[0])

time: 67 us -> 66.6 us (level)
  starting transfers between devices: 31.3 us -> 27.3 us
  waiting for transfers between devices: 19.7 us -> 23.3 us
    ppermute x10, starting transfers between devices: 23.6 us -> 19.8 us  [to_pair(): return lax.ppermute(x, 'dev', [(d, d ^ CORES * k) for d in range(size)])]
    ppermute x10, waiting for transfers between devices: 8.52 us -> 12.2 us  [to_pair(): return lax.ppermute(x, 'dev', [(d, d ^ CORES * k) for d in range(size)])]
  transfers between devices with their start and end apart: 28 -> 28, of which waited for: 16 -> 17; matrix products, arithmetic and copies ran while one was open for 0% -> 0% of each run, Pallas kernels for 15% -> 15%
where the time goes in v6:
time: 66.6 us; the launch traced here: 66.4 us
  starting transfers between devices  27.3 us (41%)
  waiting for transfers between devices  23.3 us (35%)
  Pallas kernels  15 us (23%)
  between operations  0.84 us (1%)
    ppermute x10, starting transfers between devices, to_pair(): return lax.ppermute(x, 'dev', [(d, d ^ CORES * k) for d in range(size)])  19.8 us
    ppermute x10, waiting for transfers between devices, to_pair(): return lax.ppermute(x, 'dev', [(d, d ^ CORES * k) for d in range(size)])  12.2 us
    ppermute x16, waiting for transfers between devices, to_partner(): lax.ppermute(x, 'dev', [(d, d ^ 1) for d in range(lax.axis_size('dev'))])  7.12 us
    ppermute x2, starting transfers between devices, by_head(): piece = lax.ppermute(piece, ('segment', 'dev'), route)  5.05 us
    pallas_call x1, Pallas kernels, load(): pl.pallas_call(functools.partial(load_kernel, len(arrays)), out_shape=[pl...  4.19 us
    ppermute x2, waiting for transfers between devices, by_head(): piece = lax.ppermute(piece, ('segment', 'dev'), route)  3.96 us
    pallas_call x1, Pallas kernels, attend(): pl.pallas_call(functools.partial(attend_kernel, listed, requests), out_sh...  3.06 us
    ppermute x16, starting transfers between devices, to_partner(): lax.ppermute(x, 'dev', [(d, d ^ 1) for d in range(lax.axis_size('dev'))])  2.48 us
  transfers between devices with their start and end apart: 28, of which 17 were waited for; matrix products, arithmetic and copies ran while one was open for 0% of the time, Pallas kernels for 15%

profile of v6, /device:TPU:0, one launch (start us, length us, event | category | flops | bytes accessed | tf_op | source)
XLA Modules:
  0.0 66.4 jit_solution(17448169872310739975)
XLA Ops:
  0.0 4.0 %collective-permute-start = (bf16[8,8192]{1,0:T(8,128)(2,1)}, bf16[8,8192]{1,0:T(8,128)(2,1)S(1)}, u32[]{:S(2)}, u32[]{:S(2)}) collective-permute-start(bf16[8,8192]{1,0:T(8,128)(2,1)} %bitcast.12), channel_id=1, source_target_pairs={{0,4},{1,5},{2,6},{3,7},{4,0},{5,1},{6,2},{7,3},{8,12},{9,13},{10,... | collective-permute-start | bytes 393224 | tf_op jit(solution)/shard_map/ppermute | solution.py:159
  4.0 0.5 collective-permute-start.1
  5.6 1.9 %pack.1 = (bf16[1040,128]{1,0:T(8,128)(2,1)S(1)}, bf16[1040,128]{1,0:T(8,128)(2,1)S(1)}, bf16[1040,128]{1,0:T(8,128)(2,1)S(1)}, bf16[528,128]{1,0:T(8,128)(2,1)S(1)}, bf16[512,128]{1,0:T(8,128)(2,1)S(1)}) custom-call(s32[1,1]{1,0:T(1,128)S(6)} %copy.11.counts, s32[1,1]{1,0:T(1,128)} %collective-permute-done.1.other_counts, s32[32]{0:T(128)} %table_in.1, ...), custom_call_target="tpu_custom_call" | custom-call | tf_op jit(solution)/shard_map/pack/pallas_call | solution.py:265
  7.7 1.8 %collective-permute-start.3 = (bf16[8,8192]{1,0:T(8,128)(2,1)}, bf16[8,8192]{1,0:T(8,128)(2,1)S(1)}, u32[]{:S(2)}, u32[]{:S(2)}) collective-permute-start(bf16[8,8192]{1,0:T(8,128)(2,1)} %bitcast.13), channel_id=1, source_target_pairs={{0,2},{1,3},{2,0},{3,1},{4,6},{5,7},{6,4},{7,5},{8,10},{9,11},{10,... | collective-permute-start | bytes 393224 | tf_op jit(solution)/shard_map/ppermute | solution.py:159
  9.6 1.1 %collective-permute-done.refs_4_ = bf16[8,8192]{1,0:T(8,128)(2,1)S(1)} collective-permute-done((bf16[8,8192]{1,0:T(8,128)(2,1)}, bf16[8,8192]{1,0:T(8,128)(2,1)S(1)}, u32[]{:S(2)}, u32[]{:S(2)}) %collective-permute-start) | collective-permute-done | bytes 131104 | tf_op jit(solution)/shard_map/ppermute | solution.py:159
  10.6 1.5 %collective-permute-start.8 = (bf16[512,128]{1,0:T(8,128)(2,1)S(1)}, bf16[512,128]{1,0:T(8,128)(2,1)S(1)}, u32[]{:S(2)}, u32[]{:S(2)}) collective-permute-start(bf16[512,128]{1,0:T(8,128)(2,1)S(1)} %get-tuple-element.52), channel_id=1, source_target_pairs={{0,4},{1,5},{2,6},{3,7},{4,0},{5,1},{6,2},{7,3},{8,12},{9,13},{10,... | collective-permute-start | bytes 393224 | tf_op jit(solution)/shard_map/ppermute | solution.py:159
  12.2 5.6 %collective-permute-start.6 = (bf16[8,8192]{1,0:T(8,128)(2,1)S(1)}, bf16[8,8192]{1,0:T(8,128)(2,1)S(1)}, u32[]{:S(2)}, u32[]{:S(2)}) collective-permute-start(bf16[8,8192]{1,0:T(8,128)(2,1)S(1)} %collective-permute-done.refs_4_), channel_id=1, source_target_pairs={{0,2},{1,3},{2,0},{3,1},{4,6},{5,7},{6,4},{7,5},{8,10},{9,11},{10,... | collective-permute-start | bytes 393224 | tf_op jit(solution)/shard_map/ppermute | solution.py:159
  17.8 2.7 %collective-permute-start.5 = (bf16[1040,128]{1,0:T(8,128)(2,1)S(1)}, bf16[1040,128]{1,0:T(8,128)(2,1)S(1)}, u32[]{:S(2)}, u32[]{:S(2)}) collective-permute-start(bf16[1040,128]{1,0:T(8,128)(2,1)S(1)} %get-tuple-element.49), channel_id=1, source_target_pairs={{0,6},{1,7},{2,4},{3,5},{4,2},{5,3},{6,0},{7,1},{8,14},{9,15},{10,... | collective-permute-start | bytes 798728 | tf_op jit(solution)/shard_map/ppermute | solution.py:159
  20.5 4.2 %load.1 = (bf16[8192,512]{1,0:T(8,128)(2,1)S(1)}, bf16[64,8192]{1,0:T(8,128)(2,1)S(1)}, bf16[64,8192]{1,0:T(8,128)(2,1)S(1)}) custom-call(bf16[1,8192,512]{2,1,0:T(8,128)(2,1)} %refs_0_.1, bf16[64,8192]{1,0:T(8,128)(2,1)} %bitcast.16, bf16[64,8192]{1,0:T(8,128)(2,1)} %bitcast.17), custom_call_target="tpu_custom_call" | custom-call | tf_op jit(solution)/shard_map/load/pallas_call | solution.py:205
  25.4 0.8 %collective-permute-done.9.refs_1_ = bf16[8,8192]{1,0:T(8,128)(2,1)S(1)} collective-permute-done((bf16[8,8192]{1,0:T(8,128)(2,1)S(1)}, bf16[8,8192]{1,0:T(8,128)(2,1)S(1)}, u32[]{:S(2)}, u32[]{:S(2)}) %collective-permute-start.9) | collective-permute-done | bytes 131104 | tf_op jit(solution)/shard_map/ppermute | solution.py:163
  26.7 0.8 %collective-permute-done.12.refs_7_ = bf16[8,8192]{1,0:T(8,128)(2,1)S(1)} collective-permute-done((bf16[8,8192]{1,0:T(8,128)(2,1)S(1)}, bf16[8,8192]{1,0:T(8,128)(2,1)S(1)}, u32[]{:S(2)}, u32[]{:S(2)}) %collective-permute-start.12) | collective-permute-done | bytes 131104 | tf_op jit(solution)/shard_map/ppermute | solution.py:163
  27.5 1.6 %project.1 = (bf16[64,8192]{1,0:T(8,128)(2,1)S(1)}, bf16[64,128]{1,0:T(8,128)(2,1)S(1)}, bf16[64,1024]{1,0:T(8,128)(2,1)S(1)}) custom-call(bf16[8,8192]{1,0:T(8,128)(2,1)S(1)} %bitcast.15, bf16[8,8192]{1,0:T(8,128)(2,1)S(1)} %collective-permute-done.9.refs_1_, bf16[8,8192]{1,0:T(8,128)(2,1)S(1)} %collective-permute-done.3.refs_2_, ...), custom_call_target="tpu_custom_call" | custom-call | tf_op jit(solution)/shard_map/project/pallas_call | solution.py:321
  29.1 1.5 %query.1.q_mine = bf16[64,512]{1,0:T(8,128)(2,1)S(1)} custom-call(bf16[64,8192]{1,0:T(8,128)(2,1)S(1)} %get-tuple-element.63.normed, bf16[8192,512]{1,0:T(8,128)(2,1)S(1)} %get-tuple-element.64.wq), custom_call_target="tpu_custom_call" | custom-call | tf_op jit(solution)/shard_map/query/pallas_call | solution.py:343
  30.7 4.6 %collective-permute-done.5.refs_3_ = bf16[1040,128]{1,0:T(8,128)(2,1)S(1)} collective-permute-done((bf16[1040,128]{1,0:T(8,128)(2,1)S(1)}, bf16[1040,128]{1,0:T(8,128)(2,1)S(1)}, u32[]{:S(2)}, u32[]{:S(2)}) %collective-permute-start.5) | collective-permute-done | bytes 266272 | tf_op jit(solution)/shard_map/ppermute | solution.py:159
  35.3 0.5 collective-permute-start.14
  35.8 0.8 %collective-permute-done.14.kv_other = bf16[64,128]{1,0:T(8,128)(2,1)S(1)} collective-permute-done((bf16[64,128]{1,0:T(8,128)(2,1)S(1)}, bf16[64,128]{1,0:T(8,128)(2,1)S(1)}, u32[]{:S(2)}, u32[]{:S(2)}) %collective-permute-start.14) | collective-permute-done | bytes 16416 | tf_op jit(solution)/shard_map/ppermute | solution.py:163
  36.6 3.1 %attend.1 = (f32[512,128]{1,0:T(8,128)S(1)}, f32[512,128]{1,0:T(8,128)S(1)}) custom-call(bf16[64,512]{1,0:T(8,128)(2,1)S(1)} %query.1.q_mine, bf16[64,512]{1,0:T(8,128)(2,1)S(1)} %collective-permute-done.13.q_other, bf16[64,128]{1,0:T(8,128)(2,1)S(1)} %get-tuple-element.66.kv_mine, bf16[64,128]{1,0:T(8,128)(2,1)S(1)} %collective-permute-done.14.kv_other, ...), custom_call_target="tpu_custom_call" | custom-call | flops 268435456 | bytes 2097152 | tf_op jit(solution)/shard_map/attend/pallas_call | solution.py:463
  40.1 1.2 %collective-permute-done.15.got = f32[512,128]{1,0:T(8,128)S(1)} collective-permute-done((f32[512,128]{1,0:T(8,128)S(1)}, f32[512,128]{1,0:T(8,128)S(1)}, u32[]{:S(2)}, u32[]{:S(2)}) %collective-permute-start.15) | collective-permute-done | bytes 262176 | tf_op jit(solution)/shard_map/ppermute | solution.py:163
  41.6 3.3 %collective-permute-start.18 = (bf16[64,512]{1,0:T(8,128)(2,1)S(1)}, bf16[64,512]{1,0:T(8,128)(2,1)S(1)}, u32[]{:S(2)}, u32[]{:S(2)}) collective-permute-start(bf16[64,512]{1,0:T(8,128)(2,1)S(1)} %merge.1.refs_0_), channel_id=1, source_target_pairs={{0,6},{1,7},{2,4},{3,5},{4,2},{5,3},{6,0},{7,1},{8,14},{9,15},{10,... | collective-permute-start | bytes 196616 | tf_op jit(solution)/shard_map/ppermute | solution.py:159
  45.4 0.5 collective-permute-done.21.refs_2_
  46.0 3.1 %collective-permute-done.18.refs_2_ = bf16[64,512]{1,0:T(8,128)(2,1)S(1)} collective-permute-done((bf16[64,512]{1,0:T(8,128)(2,1)S(1)}, bf16[64,512]{1,0:T(8,128)(2,1)S(1)}, u32[]{:S(2)}, u32[]{:S(2)}) %collective-permute-start.18) | collective-permute-done | bytes 65568 | tf_op jit(solution)/shard_map/ppermute | solution.py:159
  49.1 2.9 %collective-permute-done.16.refs_0_ = bf16[64,512]{1,0:T(8,128)(2,1)S(1)} collective-permute-done((bf16[64,512]{1,0:T(8,128)(2,1)S(1)}, bf16[64,512]{1,0:T(8,128)(2,1)S(1)}, u32[]{:S(2)}, u32[]{:S(2)}) %collective-permute-start.16) | collective-permute-done | bytes 65568 | tf_op jit(solution)/shard_map/ppermute | solution.py:159
  52.0 0.9 %partial.1.refs_4_ = f32[64,1024]{1,0:T(8,128)S(1)} custom-call(bf16[64,512]{1,0:T(8,128)(2,1)S(1)} %merge.1.refs_0_, bf16[64,512]{1,0:T(8,128)(2,1)S(1)} %collective-permute-done.20.refs_1_, bf16[64,512]{1,0:T(8,128)(2,1)S(1)} %collective-permute-done.21.refs_2_, bf16[64,512]{1,0:T(8,128)(2,1)S(1)} %collective-permute-done.22.refs_3_, ...), custom_call_target="tpu_custom_call" | custom-call | flops 268435456 | bytes 4194304 | tf_op jit(solution)/shard_map/partial/pallas_call | solution.py:531
  53.2 0.9 %finish.1 = (bf16[32,1024]{1,0:T(8,128)(2,1)S(1)}, bf16[32,1024]{1,0:T(8,128)(2,1)S(1)}) custom-call(bf16[64,512]{1,0:T(8,128)(2,1)S(1)} %collective-permute-done.16.refs_0_, bf16[64,512]{1,0:T(8,128)(2,1)S(1)} %collective-permute-done.17.refs_1_, bf16[64,512]{1,0:T(8,128)(2,1)S(1)} %collective-permute-done.18.refs_2_, ...), custom_call_target="tpu_custom_call" | custom-call | flops 268435456 | bytes 4194304 | tf_op jit(solution)/shard_map/finish/pallas_call | solution.py:570
  54.3 1.1 %collective-permute-done.23.got = bf16[32,1024]{1,0:T(8,128)(2,1)S(1)} collective-permute-done((bf16[32,1024]{1,0:T(8,128)(2,1)S(1)}, bf16[32,1024]{1,0:T(8,128)(2,1)S(1)}, u32[]{:S(2)}, u32[]{:S(2)}) %collective-permute-start.23) | collective-permute-done | bytes 65568 | tf_op jit(solution)/shard_map/ppermute | solution.py:163
  55.4 3.6 %collective-permute-start.24 = (bf16[2,16,1024]{2,1,0:T(8,128)(2,1)S(1)}, bf16[2,16,1024]{2,1,0:T(8,128)(2,1)S(1)}, u32[]{:S(2)}, u32[]{:S(2)}) collective-permute-start(bf16[2,16,1024]{2,1,0:T(8,128)(2,1)S(1)} %get-tuple-element.77), channel_id=1, source_target_pairs={{0,14},{1,13},{2,12},{3,15},{4,10},{5,9},{6,8},{7,11},{8,22},{9,21... | collective-permute-start | bytes 196616 | tf_op jit(solution)/shard_map/ppermute | solution.py:666
  59.0 1.5 %collective-permute-start.26 = (bf16[2,16,1024]{2,1,0:T(8,128)(2,1)S(1)}, bf16[2,16,1024]{2,1,0:T(8,128)(2,1)S(1)}, u32[]{:S(2)}, u32[]{:S(2)}) collective-permute-start(bf16[2,16,1024]{2,1,0:T(8,128)(2,1)S(1)} %get-tuple-element.78), channel_id=1, source_target_pairs={{0,8},{1,11},{2,10},{3,9},{4,12},{5,15},{6,14},{7,13},{8,16},{9,19... | collective-permute-start | bytes 196616 | tf_op jit(solution)/shard_map/ppermute | solution.py:666
  60.5 3.3 %collective-permute-done.24.refs_0_ = bf16[2,16,1024]{2,1,0:T(8,128)(2,1)S(1)} collective-permute-done((bf16[2,16,1024]{2,1,0:T(8,128)(2,1)S(1)}, bf16[2,16,1024]{2,1,0:T(8,128)(2,1)S(1)}, u32[]{:S(2)}, u32[]{:S(2)}) %collective-permute-start.24) | collective-permute-done | bytes 65568 | tf_op jit(solution)/shard_map/ppermute | solution.py:666
  63.8 0.7 collective-permute-done.26.refs_2_
  64.5 0.6 collective-permute-done.25.refs_1_
  65.0 0.7 collective-permute-done.27.refs_3_
  65.7 0.7 %place.1 = bf16[1,8,8192]{2,1,0:T(8,128)(2,1)} custom-call(bf16[2,16,1024]{2,1,0:T(8,128)(2,1)S(1)} %collective-permute-done.24.refs_0_, bf16[2,16,1024]{2,1,0:T(8,128)(2,1)S(1)} %collective-permute-done.25.refs_1_, bf16[2,16,1024]{2,1,0:T(8,128)(2,1)S(1)} %collective-permute-done.26.refs_2_, bf16[2,16,1024]{2,1,0:T(8,128)(2,1)S(1)} %collective-permute-done.27.refs_3_), custom_call_target="tpu_custom_call" | custom-call | tf_op jit(solution)/shard_map/place/pallas_call | solution.py:619
  (43 shorter events, 3.6 us)
Async XLA Ops:
  0.0 24.7 %copy-start = (bf16[1,8,8192]{2,1,0:T(8,128)(2,1)S(1)}, bf16[1,8,8192]{2,1,0:T(8,128)(2,1)}, u32[]{:S(2)}) copy-start(bf16[1,8,8192]{2,1,0:T(8,128)(2,1)} %param.10) | copy-start | bytes 393220
  0.0 27.5 %copy-start.1 = (f32[1,8192]{1,0:T(1,128)S(1)}, f32[1,8192]{1,0:T(1,128)}, u32[]{:S(2)}) copy-start(f32[1,8192]{1,0:T(1,128)} %refs_8_.1) | copy-start | bytes 98308
  0.0 10.6 %collective-permute-start = (bf16[8,8192]{1,0:T(8,128)(2,1)}, bf16[8,8192]{1,0:T(8,128)(2,1)S(1)}, u32[]{:S(2)}, u32[]{:S(2)}) collective-permute-start(bf16[8,8192]{1,0:T(8,128)(2,1)} %bitcast.12), channel_id=1, source_target_pairs={{0,4},{1,5},{2,6},{3,7},{4,0},{5,1},{6,2},{7,3},{8,12},{9,13},{10,... | collective-permute-start | bytes 393224 | tf_op jit(solution)/shard_map/ppermute | solution.py:159
  4.0 1.6 %collective-permute-start.2 = (s32[1,1,6]{2,1,0:T(1,128)}, s32[1,1,6]{2,1,0:T(1,128)S(1)}, u32[]{:S(2)}, u32[]{:S(2)}) collective-permute-start(s32[1,1,6]{2,1,0:T(1,128)} %retrieved_in.1), channel_id=1, source_target_pairs={{0,1},{1,0},{2,3},{3,2},{4,5},{5,4},{6,7},{7,6},{8,9},{9,8},{10,11... | collective-permute-start | bytes 80 | tf_op jit(solution)/shard_map/ppermute | solution.py:163
  4.0 1.6 %collective-permute-start.1 = (s32[1,1]{1,0:T(1,128)}, s32[1,1]{1,0:T(1,128)}, u32[]{:S(2)}, u32[]{:S(2)}) collective-permute-start(s32[1,1]{1,0:T(1,128)} %param.19), channel_id=1, source_target_pairs={{0,1},{1,0},{2,3},{3,2},{4,5},{5,4},{6,7},{7,6},{8,9},{9,8},{10,11... | collective-permute-start | bytes 20 | tf_op jit(solution)/shard_map/ppermute | solution.py:163
  7.6 17.1 %collective-permute-start.7 = (bf16[528,128]{1,0:T(8,128)(2,1)S(1)}, bf16[528,128]{1,0:T(8,128)(2,1)S(1)}, u32[]{:S(2)}, u32[]{:S(2)}) collective-permute-start(bf16[528,128]{1,0:T(8,128)(2,1)S(1)} %get-tuple-element.45), channel_id=1, source_target_pairs={{0,4},{1,5},{2,6},{3,7},{4,0},{5,1},{6,2},{7,3},{8,12},{9,13},{10,... | collective-permute-start | bytes 405512 | tf_op jit(solution)/shard_map/ppermute | solution.py:159
  7.7 10.0 %collective-permute-start.3 = (bf16[8,8192]{1,0:T(8,128)(2,1)}, bf16[8,8192]{1,0:T(8,128)(2,1)S(1)}, u32[]{:S(2)}, u32[]{:S(2)}) collective-permute-start(bf16[8,8192]{1,0:T(8,128)(2,1)} %bitcast.13), channel_id=1, source_target_pairs={{0,2},{1,3},{2,0},{3,1},{4,6},{5,7},{6,4},{7,5},{8,10},{9,11},{10,... | collective-permute-start | bytes 393224 | tf_op jit(solution)/shard_map/ppermute | solution.py:159
  10.6 14.1 %collective-permute-start.8 = (bf16[512,128]{1,0:T(8,128)(2,1)S(1)}, bf16[512,128]{1,0:T(8,128)(2,1)S(1)}, u32[]{:S(2)}, u32[]{:S(2)}) collective-permute-start(bf16[512,128]{1,0:T(8,128)(2,1)S(1)} %get-tuple-element.52), channel_id=1, source_target_pairs={{0,4},{1,5},{2,6},{3,7},{4,0},{5,1},{6,2},{7,3},{8,12},{9,13},{10,... | collective-permute-start | bytes 393224 | tf_op jit(solution)/shard_map/ppermute | solution.py:159
  12.2 12.6 %collective-permute-start.6 = (bf16[8,8192]{1,0:T(8,128)(2,1)S(1)}, bf16[8,8192]{1,0:T(8,128)(2,1)S(1)}, u32[]{:S(2)}, u32[]{:S(2)}) collective-permute-start(bf16[8,8192]{1,0:T(8,128)(2,1)S(1)} %collective-permute-done.refs_4_), channel_id=1, source_target_pairs={{0,2},{1,3},{2,0},{3,1},{4,6},{5,7},{6,4},{7,5},{8,10},{9,11},{10,... | collective-permute-start | bytes 393224 | tf_op jit(solution)/shard_map/ppermute | solution.py:159
  17.8 12.9 %collective-permute-start.4 = (bf16[1040,128]{1,0:T(8,128)(2,1)S(1)}, bf16[1040,128]{1,0:T(8,128)(2,1)S(1)}, u32[]{:S(2)}, u32[]{:S(2)}) collective-permute-start(bf16[1040,128]{1,0:T(8,128)(2,1)S(1)} %get-tuple-element.48), channel_id=1, source_target_pairs={{0,2},{1,3},{2,0},{3,1},{4,6},{5,7},{6,4},{7,5},{8,10},{9,11},{10,... | collective-permute-start | bytes 798728 | tf_op jit(solution)/shard_map/ppermute | solution.py:159
  17.8 17.5 %collective-permute-start.5 = (bf16[1040,128]{1,0:T(8,128)(2,1)S(1)}, bf16[1040,128]{1,0:T(8,128)(2,1)S(1)}, u32[]{:S(2)}, u32[]{:S(2)}) collective-permute-start(bf16[1040,128]{1,0:T(8,128)(2,1)S(1)} %get-tuple-element.49), channel_id=1, source_target_pairs={{0,6},{1,7},{2,4},{3,5},{4,2},{5,3},{6,0},{7,1},{8,14},{9,15},{10,... | collective-permute-start | bytes 798728 | tf_op jit(solution)/shard_map/ppermute | solution.py:159
  20.5 31.5 %slice-start = ((s8[8388608]{0:T(1024)(128)(4,1)}), s8[4194304]{0:T(1024)(128)(4,1)S(1)}, s32[]{:S(2)}) async-start(s8[8388608]{0:T(1024)(128)(4,1)} %bitcast.8), calls=%async_computation | async-start | bytes 8388608
  24.8 27.2 %slice-start.1 = ((s8[8388608]{0:T(1024)(128)(4,1)}), s8[4194304]{0:T(1024)(128)(4,1)S(1)}, s32[]{:S(2)}) async-start(s8[8388608]{0:T(1024)(128)(4,1)} %bitcast.8), calls=%async_computation.1 | async-start | bytes 8388608
  24.8 1.4 %collective-permute-start.9 = (bf16[8,8192]{1,0:T(8,128)(2,1)S(1)}, bf16[8,8192]{1,0:T(8,128)(2,1)S(1)}, u32[]{:S(2)}, u32[]{:S(2)}) collective-permute-start(bf16[8,8192]{1,0:T(8,128)(2,1)S(1)} %bitcast.14), channel_id=1, source_target_pairs={{0,1},{1,0},{2,3},{3,2},{4,5},{5,4},{6,7},{7,6},{8,9},{9,8},{10,11... | collective-permute-start | bytes 393224 | tf_op jit(solution)/shard_map/ppermute | solution.py:163
  24.8 1.5 %collective-permute-start.10 = (bf16[8,8192]{1,0:T(8,128)(2,1)S(1)}, bf16[8,8192]{1,0:T(8,128)(2,1)S(1)}, u32[]{:S(2)}, u32[]{:S(2)}) collective-permute-start(bf16[8,8192]{1,0:T(8,128)(2,1)S(1)} %collective-permute-done.3.refs_2_), channel_id=1, source_target_pairs={{0,1},{1,0},{2,3},{3,2},{4,5},{5,4},{6,7},{7,6},{8,9},{9,8},{10,11... | collective-permute-start | bytes 393224 | tf_op jit(solution)/shard_map/ppermute | solution.py:163
  25.3 1.3 %collective-permute-start.11 = (bf16[8,8192]{1,0:T(8,128)(2,1)S(1)}, bf16[8,8192]{1,0:T(8,128)(2,1)S(1)}, u32[]{:S(2)}, u32[]{:S(2)}) collective-permute-start(bf16[8,8192]{1,0:T(8,128)(2,1)S(1)} %collective-permute-done.refs_4_), channel_id=1, source_target_pairs={{0,1},{1,0},{2,3},{3,2},{4,5},{5,4},{6,7},{7,6},{8,9},{9,8},{10,11... | collective-permute-start | bytes 393224 | tf_op jit(solution)/shard_map/ppermute | solution.py:163
  26.2 1.3 %collective-permute-start.12 = (bf16[8,8192]{1,0:T(8,128)(2,1)S(1)}, bf16[8,8192]{1,0:T(8,128)(2,1)S(1)}, u32[]{:S(2)}, u32[]{:S(2)}) collective-permute-start(bf16[8,8192]{1,0:T(8,128)(2,1)S(1)} %collective-permute-done.6.refs_6_), channel_id=1, source_target_pairs={{0,1},{1,0},{2,3},{3,2},{4,5},{5,4},{6,7},{7,6},{8,9},{9,8},{10,11... | collective-permute-start | bytes 393224 | tf_op jit(solution)/shard_map/ppermute | solution.py:163
  35.3 1.4 %collective-permute-start.13 = (bf16[64,512]{1,0:T(8,128)(2,1)S(1)}, bf16[64,512]{1,0:T(8,128)(2,1)S(1)}, u32[]{:S(2)}, u32[]{:S(2)}) collective-permute-start(bf16[64,512]{1,0:T(8,128)(2,1)S(1)} %query.1.q_mine), channel_id=1, source_target_pairs={{0,1},{1,0},{2,3},{3,2},{4,5},{5,4},{6,7},{7,6},{8,9},{9,8},{10,11... | collective-permute-start | bytes 196616 | tf_op jit(solution)/shard_map/ppermute | solution.py:163
  35.3 1.3 %collective-permute-start.14 = (bf16[64,128]{1,0:T(8,128)(2,1)S(1)}, bf16[64,128]{1,0:T(8,128)(2,1)S(1)}, u32[]{:S(2)}, u32[]{:S(2)}) collective-permute-start(bf16[64,128]{1,0:T(8,128)(2,1)S(1)} %get-tuple-element.66.kv_mine), channel_id=1, source_target_pairs={{0,1},{1,0},{2,3},{3,2},{4,5},{5,4},{6,7},{7,6},{8,9},{9,8},{10,11... | collective-permute-start | bytes 49160 | tf_op jit(solution)/shard_map/ppermute | solution.py:163
  39.7 1.6 %collective-permute-start.15 = (f32[512,128]{1,0:T(8,128)S(1)}, f32[512,128]{1,0:T(8,128)S(1)}, u32[]{:S(2)}, u32[]{:S(2)}) collective-permute-start(f32[512,128]{1,0:T(8,128)S(1)} %get-tuple-element.73), channel_id=1, source_target_pairs={{0,1},{1,0},{2,3},{3,2},{4,5},{5,4},{6,7},{7,6},{8,9},{9,8},{10,11... | collective-permute-start | bytes 786440 | tf_op jit(solution)/shard_map/ppermute | solution.py:163
  41.6 4.4 %collective-permute-start.21 = (bf16[64,512]{1,0:T(8,128)(2,1)S(1)}, bf16[64,512]{1,0:T(8,128)(2,1)S(1)}, u32[]{:S(2)}, u32[]{:S(2)}) collective-permute-start(bf16[64,512]{1,0:T(8,128)(2,1)S(1)} %merge.1.refs_0_), channel_id=1, source_target_pairs={{0,2},{1,3},{2,0},{3,1},{4,6},{5,7},{6,4},{7,5},{8,10},{9,11},{10,... | collective-permute-start | bytes 196616 | tf_op jit(solution)/shard_map/ppermute | solution.py:159
  41.6 7.4 %collective-permute-start.18 = (bf16[64,512]{1,0:T(8,128)(2,1)S(1)}, bf16[64,512]{1,0:T(8,128)(2,1)S(1)}, u32[]{:S(2)}, u32[]{:S(2)}) collective-permute-start(bf16[64,512]{1,0:T(8,128)(2,1)S(1)} %merge.1.refs_0_), channel_id=1, source_target_pairs={{0,6},{1,7},{2,4},{3,5},{4,2},{5,3},{6,0},{7,1},{8,14},{9,15},{10,... | collective-permute-start | bytes 196616 | tf_op jit(solution)/shard_map/ppermute | solution.py:159
  44.9 7.0 %collective-permute-start.16 = (bf16[64,512]{1,0:T(8,128)(2,1)S(1)}, bf16[64,512]{1,0:T(8,128)(2,1)S(1)}, u32[]{:S(2)}, u32[]{:S(2)}) collective-permute-start(bf16[64,512]{1,0:T(8,128)(2,1)S(1)} %merge.1.refs_0_), channel_id=1, source_target_pairs={{0,4},{1,5},{2,6},{3,7},{4,0},{5,1},{6,2},{7,3},{8,12},{9,13},{10,... | collective-permute-start | bytes 196616 | tf_op jit(solution)/shard_map/ppermute | solution.py:159
  45.4 6.5 %collective-permute-start.20 = (bf16[64,512]{1,0:T(8,128)(2,1)S(1)}, bf16[64,512]{1,0:T(8,128)(2,1)S(1)}, u32[]{:S(2)}, u32[]{:S(2)}) collective-permute-start(bf16[64,512]{1,0:T(8,128)(2,1)S(1)} %merge.1.refs_0_), channel_id=1, source_target_pairs={{0,1},{1,0},{2,3},{3,2},{4,5},{5,4},{6,7},{7,6},{8,9},{9,8},{10,11... | collective-permute-start | bytes 196616 | tf_op jit(solution)/shard_map/ppermute | solution.py:163
  46.0 6.0 %collective-permute-start.22 = (bf16[64,512]{1,0:T(8,128)(2,1)S(1)}, bf16[64,512]{1,0:T(8,128)(2,1)S(1)}, u32[]{:S(2)}, u32[]{:S(2)}) collective-permute-start(bf16[64,512]{1,0:T(8,128)(2,1)S(1)} %collective-permute-done.21.refs_2_), channel_id=1, source_target_pairs={{0,1},{1,0},{2,3},{3,2},{4,5},{5,4},{6,7},{7,6},{8,9},{9,8},{10,11... | collective-permute-start | bytes 196616 | tf_op jit(solution)/shard_map/ppermute | solution.py:163
  49.1 3.8 %collective-permute-start.19 = (bf16[64,512]{1,0:T(8,128)(2,1)S(1)}, bf16[64,512]{1,0:T(8,128)(2,1)S(1)}, u32[]{:S(2)}, u32[]{:S(2)}) collective-permute-start(bf16[64,512]{1,0:T(8,128)(2,1)S(1)} %collective-permute-done.18.refs_2_), channel_id=1, source_target_pairs={{0,1},{1,0},{2,3},{3,2},{4,5},{5,4},{6,7},{7,6},{8,9},{9,8},{10,11... | collective-permute-start | bytes 196616 | tf_op jit(solution)/shard_map/ppermute | solution.py:163
  52.0 1.3 %collective-permute-start.17 = (bf16[64,512]{1,0:T(8,128)(2,1)S(1)}, bf16[64,512]{1,0:T(8,128)(2,1)S(1)}, u32[]{:S(2)}, u32[]{:S(2)}) collective-permute-start(bf16[64,512]{1,0:T(8,128)(2,1)S(1)} %collective-permute-done.16.refs_0_), channel_id=1, source_target_pairs={{0,1},{1,0},{2,3},{3,2},{4,5},{5,4},{6,7},{7,6},{8,9},{9,8},{10,11... | collective-permute-start | bytes 196616 | tf_op jit(solution)/shard_map/ppermute | solution.py:163
  54.1 1.3 %collective-permute-start.23 = (bf16[32,1024]{1,0:T(8,128)(2,1)S(1)}, bf16[32,1024]{1,0:T(8,128)(2,1)S(1)}, u32[]{:S(2)}, u32[]{:S(2)}) collective-permute-start(bf16[32,1024]{1,0:T(8,128)(2,1)S(1)} %get-tuple-element.76), channel_id=1, source_target_pairs={{0,1},{1,0},{2,3},{3,2},{4,5},{5,4},{6,7},{7,6},{8,9},{9,8},{10,11... | collective-permute-start | bytes 196616 | tf_op jit(solution)/shard_map/ppermute | solution.py:163
  55.4 8.4 %collective-permute-start.24 = (bf16[2,16,1024]{2,1,0:T(8,128)(2,1)S(1)}, bf16[2,16,1024]{2,1,0:T(8,128)(2,1)S(1)}, u32[]{:S(2)}, u32[]{:S(2)}) collective-permute-start(bf16[2,16,1024]{2,1,0:T(8,128)(2,1)S(1)} %get-tuple-element.77), channel_id=1, source_target_pairs={{0,14},{1,13},{2,12},{3,15},{4,10},{5,9},{6,8},{7,11},{8,22},{9,21... | collective-permute-start | bytes 196616 | tf_op jit(solution)/shard_map/ppermute | solution.py:666
  59.0 5.5 %collective-permute-start.26 = (bf16[2,16,1024]{2,1,0:T(8,128)(2,1)S(1)}, bf16[2,16,1024]{2,1,0:T(8,128)(2,1)S(1)}, u32[]{:S(2)}, u32[]{:S(2)}) collective-permute-start(bf16[2,16,1024]{2,1,0:T(8,128)(2,1)S(1)} %get-tuple-element.78), channel_id=1, source_target_pairs={{0,8},{1,11},{2,10},{3,9},{4,12},{5,15},{6,14},{7,13},{8,16},{9,19... | collective-permute-start | bytes 196616 | tf_op jit(solution)/shard_map/ppermute | solution.py:666
  63.8 1.3 %collective-permute-start.25 = (bf16[2,16,1024]{2,1,0:T(8,128)(2,1)S(1)}, bf16[2,16,1024]{2,1,0:T(8,128)(2,1)S(1)}, u32[]{:S(2)}, u32[]{:S(2)}) collective-permute-start(bf16[2,16,1024]{2,1,0:T(8,128)(2,1)S(1)} %collective-permute-done.24.refs_0_), channel_id=1, source_target_pairs={{0,1},{1,0},{2,3},{3,2},{4,5},{5,4},{6,7},{7,6},{8,9},{9,8},{10,11... | collective-permute-start | bytes 196616 | tf_op jit(solution)/shard_map/ppermute | solution.py:163
  64.5 1.3 %collective-permute-start.27 = (bf16[2,16,1024]{2,1,0:T(8,128)(2,1)S(1)}, bf16[2,16,1024]{2,1,0:T(8,128)(2,1)S(1)}, u32[]{:S(2)}, u32[]{:S(2)}) collective-permute-start(bf16[2,16,1024]{2,1,0:T(8,128)(2,1)S(1)} %collective-permute-done.26.refs_2_), channel_id=1, source_target_pairs={{0,1},{1,0},{2,3},{3,2},{4,5},{5,4},{6,7},{7,6},{8,9},{9,8},{10,11... | collective-permute-start | bytes 196616 | tf_op jit(solution)/shard_map/ppermute | solution.py:163
